TPU v7x, 32 devices: a whole 2x2x4 slice. The times are simulated.
32 devices in a mesh: grp: 4 (over x, core), qb: 8 (over z, y).
Axes of the slice: x: 2, y: 2, z: 4, core: 2. Of those that a mesh axis runs over, the one named last changes fastest.
Arguments:
- amplitudes: float32 [2, 4194304], P(None, ('grp', 'qb')), may hold values from -6 to 6
- layer_gates: float32 [4, 2, 128, 128], replicated, may hold values from -0.375 to 0.375
- cross_gates: float32 [2, 2, 4, 4], replicated, may hold values from -2 to 2
Outputs:
- final_state: float32 [2, 4194304], P(None, ('grp', 'qb'))
All inputs are finite; a program needn't handle non-finite values.
Results may differ from a plain program's by a relative error of at most 0.000084.
Values sent between devices are 32-bit elements; how exact they have to be, the bound alone decides.
No kernel may reach another device: no remote copies, remote signals or barrier semaphores. Data moves between devices by JAX's collectives and lax.ppermute only.
A program may use at most 64 MiB of HBM per device.

v0:
```python
import jax
import jax.numpy as jnp
from jax import lax
from jax.sharding import PartitionSpec as P


def dot_parts(first, second, numbers):

    def product(left, right):
        return lax.dot_general(
            left,
            right,
            numbers,
            precision=lax.Precision.HIGHEST,
            preferred_element_type=jnp.float32,
        )

    real_part = product(first[0], second[0]) - product(first[1], second[1])
    imag_part = product(first[0], second[1]) + product(first[1], second[0])
    return jnp.stack([real_part, imag_part])


def apply_high(amplitudes, matrix):
    width = matrix.shape[-1]
    blocks = amplitudes.reshape(2, width, -1)
    return dot_parts(matrix, blocks, (((1,), (0,)), ((), ()))).reshape(2, -1)


def apply_low(amplitudes, matrix):
    width = matrix.shape[-1]
    blocks = amplitudes.reshape(2, -1, width)
    return dot_parts(blocks, matrix, (((1,), (1,)), ((), ()))).reshape(2, -1)


def complex_mix(form, matrix, vector):
    precise = lax.Precision.HIGHEST
    real_part = jnp.einsum(form, matrix[0], vector[0], precision=precise) - jnp.einsum(
        form, matrix[1], vector[1], precision=precise
    )
    imag_part = jnp.einsum(form, matrix[0], vector[1], precision=precise) + jnp.einsum(
        form, matrix[1], vector[0], precision=precise
    )
    return jnp.stack([real_part, imag_part])


def on_device(amplitudes, layer_gates, cross_gates):
    section_one = apply_high(amplitudes, layer_gates[0])
    section_two = apply_low(section_one, layer_gates[1])
    inner = lax.axis_size("qb")
    blocks = section_two.reshape(2, inner, -1)
    swapped = lax.all_to_all(blocks, "qb", split_axis=1, concat_axis=1, tiled=True).reshape(2, -1)
    section_three = apply_high(swapped, layer_gates[2])
    section_four = apply_low(section_three, layer_gates[3])
    groups = lax.axis_size("grp")
    grouped = section_four.reshape(2, groups, -1)
    lower_view = lax.all_to_all(grouped, "grp", split_axis=1, concat_axis=1, tiled=True).reshape(
        2, groups // 4, 4, -1
    )
    mixed = complex_mix("kj,ajb->akb", cross_gates[0], lower_view)
    upper_view = mixed.reshape(2, 4, -1)
    mixed = complex_mix("kj,jb->kb", cross_gates[1], upper_view)
    return lax.all_to_all(
        mixed.reshape(2, groups, -1), "grp", split_axis=1, concat_axis=1, tiled=True
    ).reshape(2, -1)


def solution(mesh):
    return jax.shard_map(
        on_device,
        mesh=mesh,
        in_specs=(P(None, ("grp", "qb")), P(), P()),
        out_specs=P(None, ("grp", "qb")),
        check_vma=False,
    )
```

profile of v0, /device:TPU:0, one launch (start us, length us, event | category | flops | bytes accessed | tf_op | source)
XLA Modules:
  0.0 101.3 jit_solution(12346644580400482705)
XLA Ops:
  0.0 4.4 %slice_reduce_fusion.2 = (f32[131072]{0:T(1024)S(1)}, f32[131072]{0:T(1024)S(1)}) fusion(f32[2,131072]{1,0:T(2,128)} %param.3), kind=kLoop, calls=%fused_computation.29 | loop fusion | bytes 2097152 | tf_op jit(solution)/shard_map/slice | solution.py:18
  4.4 0.1 squeeze.47
  4.5 0.0 copy-start
  4.5 0.1 squeeze.45
  4.6 0.9 copy-done
  5.6 0.6 fusion.38
  6.2 0.6 fusion.36
  6.7 0.6 convolution_subtract_fusion.5
  7.3 0.1 squeeze.48
  7.4 0.6 fusion.28
  8.0 0.6 fusion.32
  8.6 0.6 convolution_add_fusion.5
  9.2 0.1 squeeze.50
  9.3 0.6 convolution_subtract_fusion.4
  9.9 0.6 convolution_add_fusion.4
  10.5 0.9 pad_maximum_fusion
  11.4 32.8 %all_to_all.15 = f32[2,8,16384]{2,0,1:T(2,128)S(1)} all-to-all(f32[2,8,16384]{2,0,1:T(2,128)S(1)} %pad_maximum_fusion), channel_id=1, replica_groups=mesh['grp'=4,'qb'=8] {'qb'}, dimensions={1} | all-to-all | bytes 2097152 | tf_op jit(solution)/shard_map/all_to_all | solution.py:51
  44.2 2.7 %slice_reduce_fusion = (f32[8,16384]{1,0:T(8,128)S(1)}, f32[8,16384]{1,0:T(8,128)S(1)}) fusion(f32[2,8,16384]{2,0,1:T(2,128)S(1)} %all_to_all.15), kind=kLoop, calls=%fused_computation.21 | loop fusion | bytes 2097152 | tf_op jit(solution)/shard_map/slice | solution.py:18
  47.0 0.1 squeeze.108
  47.1 0.1 squeeze.52
  47.2 1.0 fusion.26
  48.2 1.0 fusion.24
  49.2 1.0 fusion.5
  50.2 0.2 copy.8
  50.4 0.1 squeeze.110
  50.5 0.6 fusion.16
  51.1 0.6 fusion.20
  51.7 1.0 fusion.4
  52.7 0.2 copy.9
  52.9 0.1 squeeze.112
  53.0 0.6 convolution_subtract_fusion.2
  53.6 0.6 convolution_add_fusion.2
  54.2 0.9 pad_maximum_fusion.1
  55.1 17.0 %all_to_all.16 = f32[2,4,32768]{2,0,1:T(2,128)S(1)} all-to-all(f32[2,4,32768]{2,0,1:T(2,128)S(1)} %pad_maximum_fusion.1), channel_id=1, replica_groups=mesh['grp'=4,'qb'=8] {'grp'}, dimensions={1} | all-to-all | bytes 2097152 | tf_op jit(solution)/shard_map/all_to_all | solution.py:56
  72.1 0.8 fusion.74
  73.0 0.0 copy-done.1
  73.0 1.3 %fusion.10 = f32[32768,4]{0,1:T(4,128)S(1)} fusion(f32[1,4,32768]{2,0,1:T(1,128)S(1)} %get-tuple-element.9, f32[2,2,4,4]{3,2,1,0:T(4,128)S(1)} %copy-done.1), kind=kOutput, calls=%fused_computation.27 | convolution fusion | flops 6291456 | bytes 1050624 | tf_op jit(solution)/shard_map/kj,ajb->akb/dot_general | solution.py:37
  74.3 1.3 %fusion.6 = f32[32768,4]{0,1:T(4,128)S(1)} fusion(f32[1,4,32768]{2,0,1:T(1,128)S(1)} %get-tuple-element.10, f32[2,2,4,4]{3,2,1,0:T(4,128)S(1)} %copy-done.1), kind=kOutput, calls=%fused_computation.23 | convolution fusion | flops 6291456 | bytes 1050624 | tf_op jit(solution)/shard_map/kj,ajb->akb/dot_general | solution.py:40
  75.6 1.3 %fusion.3 = f32[4,32768]{1,0:T(4,128)S(1)} fusion(f32[32768,4]{0,1:T(4,128)S(1)} %fusion.10, f32[1,4,32768]{2,0,1:T(1,128)S(1)} %get-tuple-element.10, f32[2,2,4,4]{3,2,1,0:T(4,128)S(1)} %copy-done.1), kind=kOutput, calls=%fused_computation.7 | convolution fusion | flops 6422528 | bytes 1574912 | tf_op jit(solution)/shard_map/kj,ajb->akb/dot_general | solution.py:37
  76.9 1.3 %fusion.2 = f32[4,32768]{1,0:T(4,128)S(1)} fusion(f32[32768,4]{0,1:T(4,128)S(1)} %fusion.6, f32[1,4,32768]{2,0,1:T(1,128)S(1)} %get-tuple-element.9, f32[2,2,4,4]{3,2,1,0:T(4,128)S(1)} %copy-done.1), kind=kOutput, calls=%fused_computation.5 | convolution fusion | flops 6422528 | bytes 1574912 | tf_op jit(solution)/shard_map/kj,ajb->akb/dot_general | solution.py:40
  78.3 1.0 fusion.58
  79.3 1.0 fusion.60
  80.3 1.0 %fusion = f32[1,4,32768]{2,1,0:T(4,128)S(1)} fusion(f32[32768,4]{0,1:T(4,128)S(1)} %fusion.58, f32[4,32768]{1,0:T(4,128)S(1)} %fusion.3, f32[2,2,4,4]{3,2,1,0:T(4,128)S(1)} %copy-done.1), kind=kOutput, calls=%fused_computation.1 | convolution fusion | flops 6422528 | bytes 1574912 | tf_op jit(solution)/shard_map/kj,jb->kb/dot_general | solution.py:40
  81.3 1.0 %fusion.1 = f32[1,4,32768]{2,1,0:T(4,128)S(1)} fusion(f32[32768,4]{0,1:T(4,128)S(1)} %fusion.60, f32[4,32768]{1,0:T(4,128)S(1)} %fusion.2, f32[2,2,4,4]{3,2,1,0:T(4,128)S(1)} %copy-done.1), kind=kOutput, calls=%fused_computation.3 | convolution fusion | flops 6422528 | bytes 1574912 | tf_op jit(solution)/shard_map/kj,jb->kb/dot_general | solution.py:37
  82.3 0.2 pad_maximum_fusion.2
  82.6 0.8 copy.12
  83.4 16.9 %all_to_all.17 = f32[2,4,32768]{2,0,1:T(2,128)S(1)} all-to-all(f32[2,4,32768]{2,0,1:T(2,128)S(1)} %copy.12), channel_id=1, replica_groups=mesh['grp'=4,'qb'=8] {'grp'}, dimensions={1} | all-to-all | bytes 2097152 | tf_op jit(solution)/shard_map/all_to_all | solution.py:62
  100.3 1.0 copy.32
  (1 shorter events, 0.0 us)
Async XLA Ops:
  4.5 1.0 %copy-start = (f32[4,2,128,128]{3,2,1,0:T(8,128)S(1)}, f32[4,2,128,128]{3,2,1,0:T(8,128)}, u32[]{:S(2)}) copy-start(f32[4,2,128,128]{3,2,1,0:T(8,128)} %param.4) | copy-start | bytes 1572868
  72.1 0.8 copy-start.1
where the time goes:
time: 102 us; the launch traced here: 101 us
  blocking collectives  66.8 us (65%)
  matrix products  20.3 us (20%)
  local copies, waits for them, and re-layouts  11.8 us (12%)
  other arithmetic  2.1 us (2%)
    all_to_all x1, blocking collectives, on_device(): lax.all_to_all(blocks, 'qb', split_axis=1, concat_axis=1, tiled=True)  32.8 us
    all_to_all x1, blocking collectives, on_device(): lax.all_to_all(grouped, 'grp', split_axis=1, concat_axis=1, tiled=True)  17 us
    all_to_all x1, blocking collectives, on_device(): lax.all_to_all(mixed.reshape(2, groups, -1), 'grp', split_axis=1, concat_...  16.9 us
    dot_general x16, matrix products, product(): lax.dot_general(left, right, numbers, precision=lax.Precision.HIGHEST, pr...  11 us
    slice x2, local copies, waits for them, and re-layouts, dot_parts(): real_part = product(first[0], second[0]) - product(first[1], second[1])  7.17 us
    dot_general x2, matrix products, complex_mix(): jnp.einsum(form, matrix[1], vector[1], precision=precise)  2.34 us
    dot_general x2, matrix products, complex_mix(): jnp.einsum(form, matrix[1], vector[0], precision=precise)  2.34 us
    dot_general x2, matrix products, complex_mix(): jnp.einsum(form, matrix[0], vector[0], precision=precise)  2.32 us

commit v1 on v0

v1 whole, which is shorter than its diff:
```python
import functools

import jax
import jax.numpy as jnp
from jax import lax
from jax.experimental import pallas as pl
from jax.experimental.pallas import tpu as pltpu
from jax.sharding import PartitionSpec as P

F32, BF16 = jnp.float32, jnp.bfloat16


def split(value):
    high = value.astype(BF16)
    return high, (value - high.astype(F32)).astype(BF16)


def dot_split(first, second, dims=((1,), (0,))):
    product = functools.partial(
        lax.dot_general, dimension_numbers=(dims, ((), ())), preferred_element_type=F32
    )
    return product(first[0], second[0]) + (product(first[0], second[1]) + product(first[1], second[0]))


def joined(gates, at):
    real, imag = gates[at, 0], gates[at, 1]
    return jnp.concatenate(
        [jnp.concatenate([real, -imag], 1), jnp.concatenate([imag, real], 1)], 0
    )


def slot_source(place, me, width, block):
    row, part, slot = place % block, (place // block) % 2, place // (2 * block)
    return part * width + (slot ^ me) * block + row


def select(me, width, block, by_rows):
    size = (2 * width, 2 * width)
    here = lax.broadcasted_iota(jnp.int32, size, 0 if by_rows else 1)
    other = lax.broadcasted_iota(jnp.int32, size, 1 if by_rows else 0)
    return (slot_source(here, me, width, block) == other).astype(F32).astype(BF16)


def pick(first, second):
    return jnp.dot(first, second, preferred_element_type=F32).astype(BF16)


def columns(parts):
    return jnp.concatenate(parts, 1)


def rows(parts):
    return jnp.concatenate(parts, 0)


def first_chunk(sizes, x, out):
    width, mid, chunk = sizes["width"], sizes["mid"], sizes["a"]
    for i, m in enumerate(chunk):
        for part in range(2):
            out[pl.ds((2 * i + part) * width, width), :] = x[pl.ds(2 * m + part, width, 2 * mid), :]


def store_slots(sizes, value, count, outs):
    width, size = sizes["width"], 2 * sizes["block"]
    for s, out in enumerate(outs):
        for i in range(count):
            out[pl.ds(i * size, size), :] = value[s * size : (s + 1) * size, i * width : (i + 1) * width]


def load_slots(sizes, slots, count):
    size = 2 * sizes["block"]
    return columns([rows([s[pl.ds(i * size, size), :] for s in slots]) for i in range(count)])


def second_chunk(sizes, x, gates, high, low, *outs):
    width, mid, chunk = sizes["width"], sizes["mid"], sizes["b"]
    chosen = select(lax.axis_index("qb"), width, sizes["block"], True)
    gate = split(joined(gates, 0))
    gate = pick(chosen, gate[0]), pick(chosen, gate[1])
    high[...], low[...] = gate
    state = columns(
        [
            rows([x[pl.ds(2 * m + part, width, 2 * mid), :] for part in range(2)])
            for m in chunk
        ]
    )
    store_slots(sizes, dot_split(gate, split(state)), len(chunk), outs)


def prepare(sizes, gates, lane_high, lane_low, high, low):
    width = sizes["width"]
    lane = lax.dot_general(
        joined(gates, 1),
        joined(gates, 3),
        (((0,), (1,)), ((), ())),
        precision=lax.Precision.HIGHEST,
        preferred_element_type=F32,
    )
    lane_high[...], lane_low[...] = split(lane)
    chosen = select(lax.axis_index("qb"), width, sizes["block"], False)
    gate = split(joined(gates, 2))
    high[...], low[...] = pick(gate[0], chosen), pick(gate[1], chosen)


def entry(cross, which, i, j):
    if which is not None:
        return cross[which, 0, i, j], cross[which, 1, i, j]
    real = imag = None
    for k in range(cross.shape[-1]):
        ar, ai, br, bi = cross[1, 0, i, k], cross[1, 1, i, k], cross[0, 0, k, j], cross[0, 1, k, j]
        r, m = ar * br - ai * bi, ar * bi + ai * br
        real, imag = (r, m) if real is None else (real + r, imag + m)
    return real, imag


def mix(sizes, which, stride, count, own, far, cross, mine, other):
    width = sizes["width"]
    me = (lax.axis_index("grp") // stride) % 4
    for target, out in ((me, mine), (me ^ 1, other)):
        (ar, ai), (br, bi) = entry(cross, which, target, me), entry(cross, which, target, me ^ 2)
        for i in range(count):
            at, after = pl.ds(2 * i * width, width), pl.ds((2 * i + 1) * width, width)
            xr, xi, yr, yi = own[at, :], own[after, :], far[at, :], far[after, :]
            out[at, :] = ar * xr - ai * xi + (br * yr - bi * yi)
            out[after, :] = ar * xi + ai * xr + (br * yi + bi * yr)


def low_gates(sizes, parts, lane):
    width = sizes["width"]
    wide = rows([columns(parts[i : i + 2]) for i in range(0, len(parts), 2)])
    done = dot_split(split(wide), lane)
    done = [done[i * width : (i + 1) * width] for i in range(len(parts) // 2)]
    return columns([rows([d[:, :width], d[:, width:]]) for d in done])


def after_mix(sizes, count, mine, got, lane_high, lane_low, high, low, *outs):
    width = sizes["width"]
    parts = []
    for i in range(2 * count):
        at = pl.ds(i * width, width)
        parts.append(mine[at, :] + got[at, :])
    state = low_gates(sizes, parts, (lane_high[...], lane_low[...]))
    store_slots(sizes, dot_split((high[...], low[...]), split(state)), count, outs)


def after_swap(sizes, count, lane_high, lane_low, high, low, *refs):
    *slots, out = refs
    width = sizes["width"]
    state = dot_split((high[...], low[...]), split(load_slots(sizes, slots, count)))
    parts = [state[p * width : (p + 1) * width, i * width : (i + 1) * width] for i in range(count) for p in range(2)]
    state = low_gates(sizes, parts, (lane_high[...], lane_low[...]))
    for i in range(count):
        out[pl.ds(2 * i * width, 2 * width), :] = state[:, i * width : (i + 1) * width]


def last(sizes, mine, got, high, low, *refs):
    *slots, out = refs
    width, mid = sizes["width"], sizes["mid"]
    state = dot_split((high[...], low[...]), split(load_slots(sizes, slots, len(sizes["a"]))))
    for i, m in enumerate(sizes["b"]):
        for part in range(2):
            at = pl.ds((2 * i + part) * width, width)
            out[pl.ds(2 * m + part, width, 2 * mid), :] = mine[at, :] + got[at, :]
    for i, m in enumerate(sizes["a"]):
        for part in range(2):
            out[pl.ds(2 * m + part, width, 2 * mid), :] = state[
                part * width : (part + 1) * width, i * width : (i + 1) * width
            ]


def call(body, outs, *args, scalars=(), flops=0):
    vmem = pl.BlockSpec(memory_space=pltpu.VMEM)
    smem = pl.BlockSpec(memory_space=pltpu.SMEM)
    moved = sum(a.size * a.dtype.itemsize for a in args) + sum(o.size * o.dtype.itemsize for o in outs)
    return pl.pallas_call(
        body,
        out_shape=outs,
        in_specs=[smem if i in scalars else vmem for i in range(len(args))],
        out_specs=[vmem] * len(outs),
        compiler_params=pltpu.CompilerParams(vmem_limit_bytes=24 * 2**20),
        cost_estimate=pl.CostEstimate(flops=flops, bytes_accessed=moved, transcendentals=0),
    )(*args)


def on_device(amplitudes, layer_gates, cross_gates):
    inner, groups = lax.axis_size("qb"), lax.axis_size("grp")
    width = layer_gates.shape[-1]
    local = amplitudes.shape[-1]
    mid = local // (width * width)
    block = width // inner
    sizes = dict(width=width, mid=mid, block=block, a=range(mid // 2), b=range(mid // 2, mid))
    partial = lambda f, *more: functools.partial(f, sizes, *more)

    x = amplitudes.reshape(2, local // width, width).transpose(1, 0, 2).reshape(2 * local // width, width)
    table = jax.ShapeDtypeStruct((2 * width, 2 * width), BF16)
    chunk = lambda c: jax.ShapeDtypeStruct((len(c) * 2 * width, width), F32)
    pieces = lambda c: [jax.ShapeDtypeStruct((len(c) * 2 * block, width), F32)] * inner

    def swap(slots):
        return [slots[0]] + [
            lax.ppermute(slots[k], "qb", [(i, i ^ k) for i in range(inner)]) for k in range(1, inner)
        ]

    def across(value, step):
        return lax.ppermute(value, "grp", [(i, i ^ step) for i in range(groups)])

    order = cross_gates.shape[-1]
    stages = [(None, 1)] if groups == order else [(0, 1), (1, groups // order)]

    def cross(value, c):
        for which, stride in stages:
            far = across(value, 2 * stride)
            mine, other = call(partial(mix, which, stride, len(c)), [chunk(c)] * 2, value, far, cross_gates, scalars=(2,))
            got = across(other, stride)
            value = mine + got if stride != stages[-1][1] else None
        return mine, got

    a, b = sizes["a"], sizes["b"]
    (raw,) = call(partial(first_chunk), [chunk(a)], x)
    first_high, first_low, *slots = call(partial(second_chunk), [table, table] + pieces(b), x, layer_gates)
    lane_high, lane_low, third_high, third_low = call(partial(prepare), [table] * 4, layer_gates)
    mine_a, got_a = cross(raw, a)
    slots = swap(slots)
    (state_b,) = call(partial(after_swap, len(b)), [chunk(b)], lane_high, lane_low, third_high, third_low, *slots)
    slots = call(partial(after_mix, len(a)), pieces(a), mine_a, got_a, lane_high, lane_low, first_high, first_low)
    slots = swap(slots)
    mine_b, got_b = cross(state_b, b)
    (out,) = call(partial(last), [jax.ShapeDtypeStruct(x.shape, F32)], mine_b, got_b, third_high, third_low, *slots)
    return out.reshape(local // width, 2, width).transpose(1, 0, 2).reshape(2, local)


def solution(mesh):
    return jax.shard_map(
        on_device,
        mesh=mesh,
        in_specs=(P(None, ("grp", "qb")), P(), P()),
        out_specs=P(None, ("grp", "qb")),
        check_vma=False,
    )
```

time: 102 us -> 60.8 us (0.60)
  blocking collectives: 66.8 us -> 0 us
  starting transfers between devices: 0 us -> 27.1 us
  waiting for transfers between devices: 0 us -> 24.5 us
  matrix products: 20.3 us -> 0 us
  local copies, waits for them, and re-layouts: 11.8 us -> 2.27 us
  Pallas kernels: 0 us -> 6.65 us
  other arithmetic: 2.1 us -> 0 us
    all_to_all x3 -> x0, blocking collectives: 66.8 us -> none  [the longest x1 32.8 us: on_device(): lax.all_to_all(blocks, 'qb', split_axis=1, concat_axis=1, tiled=True)]
    ppermute x0 -> x18, starting transfers between devices: none -> 27.1 us  [the longest x14 23.7 us: swap(): lax.ppermute(slots[k], 'qb', [(i, i ^ k) for i in range(inner)])]
    ppermute x0 -> x18, waiting for transfers between devices: none -> 24.5 us  [the longest x4 13.1 us: across(): return lax.ppermute(value, 'grp', [(i, i ^ step) for i in range(groups)])]
    dot_general x24 -> x0, matrix products: 20.3 us -> none  [the longest x16 11 us: product(): lax.dot_general(left, right, numbers, precision=lax.Precision.HIGHEST, pr...]
    slice x3 -> x0, local copies, waits for them, and re-layouts: 7.98 us -> none  [the longest x2 7.17 us: dot_parts(): real_part = product(first[0], second[0]) - product(first[1], second[1])]
    pallas_call x0 -> x8, Pallas kernels: none -> 6.65 us  [call(): pl.pallas_call(body, out_shape=outs, in_specs=[smem if i in scalars else...]
    another operation x3 -> x0, other arithmetic: 2.1 us -> none  [the longest x2 1.87 us: dot_parts(): return jnp.stack([real_part, imag_part])]
    unnamed x5 -> x8, local copies, waits for them, and re-layouts: 1.92 us -> 2.27 us
  transfers between devices with their start and end apart: 0 -> 18, of which waited for: 0 -> 6; matrix products, arithmetic and copies ran while one was open for 0% -> 0% of each run, Pallas kernels for 0% -> 7%
where the time goes in v1:
time: 60.8 us; the launch traced here: 60.6 us
  starting transfers between devices  27.1 us (45%)
  waiting for transfers between devices  24.5 us (40%)
  Pallas kernels  6.65 us (11%)
  local copies, waits for them, and re-layouts  2.27 us (4%)
    ppermute x14, starting transfers between devices, swap(): lax.ppermute(slots[k], 'qb', [(i, i ^ k) for i in range(inner)])  23.7 us
    ppermute x4, waiting for transfers between devices, across(): return lax.ppermute(value, 'grp', [(i, i ^ step) for i in range(groups)])  13.1 us
    ppermute x14, waiting for transfers between devices, swap(): lax.ppermute(slots[k], 'qb', [(i, i ^ k) for i in range(inner)])  11.4 us
    pallas_call x8, Pallas kernels, call(): pl.pallas_call(body, out_shape=outs, in_specs=[smem if i in scalars else...  6.65 us
    ppermute x4, starting transfers between devices, across(): return lax.ppermute(value, 'grp', [(i, i ^ step) for i in range(groups)])  3.42 us
    unnamed x8, local copies, waits for them, and re-layouts  2.27 us
  transfers between devices with their start and end apart: 18, of which 6 were waited for; matrix products, arithmetic and copies ran while one was open for 0% of the time, Pallas kernels for 7%

profile of v1, /device:TPU:0, one launch (start us, length us, event | category | flops | bytes accessed | tf_op | source)
XLA Modules:
  0.0 60.6 jit_solution(1458627486879163429)
XLA Ops:
  0.0 1.2 %copy-done = f32[2,131072]{1,0:T(2,128)S(1)} copy-done((f32[2,131072]{1,0:T(2,128)S(1)}, f32[2,131072]{1,0:T(2,128)}, u32[]{:S(2)}) %copy-start) | copy-done | bytes 1048600
  1.2 1.0 %copy-done.2 = f32[4,2,128,128]{3,2,1,0:T(8,128)S(1)} copy-done((f32[4,2,128,128]{3,2,1,0:T(8,128)S(1)}, f32[4,2,128,128]{3,2,1,0:T(8,128)}, u32[]{:S(2)}) %copy-start.2) | copy-done | bytes 524312
  2.3 0.6 %shard_map.38 = (bf16[256,256]{1,0:T(8,128)(2,1)S(1)}, bf16[256,256]{1,0:T(8,128)(2,1)S(1)}, f32[128,128]{1,0:T(8,128)S(1)}, f32[128,128]{1,0:T(8,128)S(1)}, f32...) custom-call(f32[2048,128]{1,0:T(8,128)S(1)} %bitcast.10, ...), custom_call_target="tpu_custom_call" | custom-call | bytes 2359296 | tf_op jit(solution)/shard_map/pallas_call | solution.py:175
  2.9 3.0 %collective-permute-start = (f32[128,128]{1,0:T(8,128)S(1)}, f32[128,128]{1,0:T(8,128)S(1)}, u32[]{:S(2)}, u32[]{:S(2)}) collective-permute-start(f32[128,128]{1,0:T(8,128)S(1)} %get-tuple-element.36), channel_id=1, source_target_pairs={{0,1},{1,0},{2,3},{3,2},{4,5},{5,4},{6,7},{7,6},{8,9},{9,8},{10,11... | collective-permute-start | bytes 196616 | tf_op jit(solution)/shard_map/ppermute | solution.py:201
  5.9 1.6 %collective-permute-start.1 = (f32[128,128]{1,0:T(8,128)S(1)}, f32[128,128]{1,0:T(8,128)S(1)}, u32[]{:S(2)}, u32[]{:S(2)}) collective-permute-start(f32[128,128]{1,0:T(8,128)S(1)} %get-tuple-element.37), channel_id=1, source_target_pairs={{0,2},{1,3},{2,0},{3,1},{4,6},{5,7},{6,4},{7,5},{8,10},{9,11},{10,... | collective-permute-start | bytes 196616 | tf_op jit(solution)/shard_map/ppermute | solution.py:201
  7.5 0.0 collective-permute-start.2
  7.5 3.0 %collective-permute-start.3 = (f32[128,128]{1,0:T(8,128)S(1)}, f32[128,128]{1,0:T(8,128)S(1)}, u32[]{:S(2)}, u32[]{:S(2)}) collective-permute-start(f32[128,128]{1,0:T(8,128)S(1)} %get-tuple-element.39), channel_id=1, source_target_pairs={{0,4},{1,5},{2,6},{3,7},{4,0},{5,1},{6,2},{7,3},{8,12},{9,13},{10,... | collective-permute-start | bytes 196616 | tf_op jit(solution)/shard_map/ppermute | solution.py:201
  10.5 1.3 %collective-permute-start.4 = (f32[128,128]{1,0:T(8,128)S(1)}, f32[128,128]{1,0:T(8,128)S(1)}, u32[]{:S(2)}, u32[]{:S(2)}) collective-permute-start(f32[128,128]{1,0:T(8,128)S(1)} %get-tuple-element.40), channel_id=1, source_target_pairs={{0,5},{1,4},{2,7},{3,6},{4,1},{5,0},{6,3},{7,2},{8,13},{9,12},{10,... | collective-permute-start | bytes 196616 | tf_op jit(solution)/shard_map/ppermute | solution.py:201
  11.8 0.0 collective-permute-done.refs_1_
  11.8 3.6 %collective-permute-start.5 = (f32[128,128]{1,0:T(8,128)S(1)}, f32[128,128]{1,0:T(8,128)S(1)}, u32[]{:S(2)}, u32[]{:S(2)}) collective-permute-start(f32[128,128]{1,0:T(8,128)S(1)} %get-tuple-element.41), channel_id=1, source_target_pairs={{0,6},{1,7},{2,4},{3,5},{4,2},{5,3},{6,0},{7,1},{8,14},{9,15},{10,... | collective-permute-start | bytes 196616 | tf_op jit(solution)/shard_map/ppermute | solution.py:201
  15.4 0.0 collective-permute-done.1.refs_2_
  15.4 0.0 collective-permute-start.6
  15.4 0.0 copy-done.1
  15.4 0.2 shard_map.41.own
  15.6 0.0 collective-permute-done.2.refs_3_
  15.6 1.7 %collective-permute-start.9 = (f32[1024,128]{1,0:T(8,128)S(1)}, f32[1024,128]{1,0:T(8,128)S(1)}, u32[]{:S(2)}, u32[]{:S(2)}) collective-permute-start(f32[1024,128]{1,0:T(8,128)S(1)} %shard_map.41.own), channel_id=1, source_target_pairs={{0,16},{8,24},{16,0},{24,8},{1,17},{9,25},{17,1},{25,9},{2,18},{10... | collective-permute-start | bytes 1572872 | tf_op jit(solution)/shard_map/ppermute | solution.py:205
  17.3 0.5 shard_map.37
  17.8 0.0 collective-permute-done.3.refs_4_
  17.8 2.9 %collective-permute-done.4.refs_5_ = f32[128,128]{1,0:T(8,128)S(1)} collective-permute-done((f32[128,128]{1,0:T(8,128)S(1)}, f32[128,128]{1,0:T(8,128)S(1)}, u32[]{:S(2)}, u32[]{:S(2)}) %collective-permute-start.4) | collective-permute-done | bytes 65568 | tf_op jit(solution)/shard_map/ppermute | solution.py:201
  20.7 0.0 collective-permute-done.5.refs_6_
  20.7 1.7 %collective-permute-done.6.refs_7_ = f32[128,128]{1,0:T(8,128)S(1)} collective-permute-done((f32[128,128]{1,0:T(8,128)S(1)}, f32[128,128]{1,0:T(8,128)S(1)}, u32[]{:S(2)}, u32[]{:S(2)}) %collective-permute-start.6) | collective-permute-done | bytes 65568 | tf_op jit(solution)/shard_map/ppermute | solution.py:201
  22.5 0.8 %shard_map.39.own = f32[1024,128]{1,0:T(8,128)S(1)} custom-call(bf16[256,256]{1,0:T(8,128)(2,1)S(1)} %get-tuple-element.31.lane_high, bf16[256,256]{1,0:T(8,128)(2,1)S(1)} %get-tuple-element.32.lane_low, bf16[256,256]{1,0:T(8,128)(2,1)S(1)} %get-tuple-element.33.high, bf16[256,256]{1,0:T(8,128)(2,1)S(1)} %get-tuple-element.34.low, ...), custom_call_target="tpu_custom_call" | custom-call | bytes 1572864 | tf_op jit(solution)/shard_map/pallas_call | solution.py:175
  23.2 1.6 %collective-permute-start.7 = (f32[1024,128]{1,0:T(8,128)S(1)}, f32[1024,128]{1,0:T(8,128)S(1)}, u32[]{:S(2)}, u32[]{:S(2)}) collective-permute-start(f32[1024,128]{1,0:T(8,128)S(1)} %shard_map.39.own), channel_id=1, source_target_pairs={{0,16},{8,24},{16,0},{24,8},{1,17},{9,25},{17,1},{25,9},{2,18},{10... | collective-permute-start | bytes 1572872 | tf_op jit(solution)/shard_map/ppermute | solution.py:205
  24.8 5.7 %collective-permute-done.9.far = f32[1024,128]{1,0:T(8,128)S(1)} collective-permute-done((f32[1024,128]{1,0:T(8,128)S(1)}, f32[1024,128]{1,0:T(8,128)S(1)}, u32[]{:S(2)}, u32[]{:S(2)}) %collective-permute-start.9) | collective-permute-done | bytes 524320 | tf_op jit(solution)/shard_map/ppermute | solution.py:205
  30.5 0.0 copy-done.3
  30.5 1.0 %shard_map.42 = (f32[1024,128]{1,0:T(8,128)S(1)}, f32[1024,128]{1,0:T(8,128)S(1)}) custom-call(f32[1024,128]{1,0:T(8,128)S(1)} %shard_map.41.own, f32[1024,128]{1,0:T(8,128)S(1)} %collective-permute-done.9.far, f32[2,2,4,4]{3,2,1,0:T(4,128)S(1)} %copy-done.3), custom_call_target="tpu_custom_call" | custom-call | bytes 2097408 | tf_op jit(solution)/shard_map/pallas_call | solution.py:175
  31.5 0.1 collective-permute-start.10
  31.6 7.3 %collective-permute-done.7.far = f32[1024,128]{1,0:T(8,128)S(1)} collective-permute-done((f32[1024,128]{1,0:T(8,128)S(1)}, f32[1024,128]{1,0:T(8,128)S(1)}, u32[]{:S(2)}, u32[]{:S(2)}) %collective-permute-start.7) | collective-permute-done | bytes 524320 | tf_op jit(solution)/shard_map/ppermute | solution.py:205
  38.9 1.0 %shard_map.40 = (f32[1024,128]{1,0:T(8,128)S(1)}, f32[1024,128]{1,0:T(8,128)S(1)}) custom-call(f32[1024,128]{1,0:T(8,128)S(1)} %shard_map.39.own, f32[1024,128]{1,0:T(8,128)S(1)} %collective-permute-done.7.far, f32[2,2,4,4]{3,2,1,0:T(4,128)S(1)} %copy-done.3), custom_call_target="tpu_custom_call" | custom-call | bytes 2097408 | tf_op jit(solution)/shard_map/pallas_call | solution.py:175
  39.9 0.1 collective-permute-start.8
  39.9 0.0 collective-permute-done.10.got
  39.9 1.0 %shard_map.43 = (f32[128,128]{1,0:T(8,128)S(1)}, f32[128,128]{1,0:T(8,128)S(1)}, f32[128,128]{1,0:T(8,128)S(1)}, f32[128,128]{1,0:T(8,128)S(1)}, f32[128,128]{1,...) custom-call(f32[1024,128]{1,0:T(8,128)S(1)} %get-tuple-element.45.mine, ...), custom_call_target="tpu_custom_call" | custom-call | bytes 2097152 | tf_op jit(solution)/shard_map/pallas_call | solution.py:175
  41.0 1.6 %collective-permute-start.11 = (f32[128,128]{1,0:T(8,128)S(1)}, f32[128,128]{1,0:T(8,128)S(1)}, u32[]{:S(2)}, u32[]{:S(2)}) collective-permute-start(f32[128,128]{1,0:T(8,128)S(1)} %get-tuple-element.50), channel_id=1, source_target_pairs={{0,1},{1,0},{2,3},{3,2},{4,5},{5,4},{6,7},{7,6},{8,9},{9,8},{10,11... | collective-permute-start | bytes 196616 | tf_op jit(solution)/shard_map/ppermute | solution.py:201
  42.6 0.0 collective-permute-start.12
  42.6 2.0 %collective-permute-start.13 = (f32[128,128]{1,0:T(8,128)S(1)}, f32[128,128]{1,0:T(8,128)S(1)}, u32[]{:S(2)}, u32[]{:S(2)}) collective-permute-start(f32[128,128]{1,0:T(8,128)S(1)} %get-tuple-element.52), channel_id=1, source_target_pairs={{0,3},{1,2},{2,1},{3,0},{4,7},{5,6},{6,5},{7,4},{8,11},{9,10},{10,... | collective-permute-start | bytes 196616 | tf_op jit(solution)/shard_map/ppermute | solution.py:201
  44.5 2.1 %collective-permute-start.14 = (f32[128,128]{1,0:T(8,128)S(1)}, f32[128,128]{1,0:T(8,128)S(1)}, u32[]{:S(2)}, u32[]{:S(2)}) collective-permute-start(f32[128,128]{1,0:T(8,128)S(1)} %get-tuple-element.53), channel_id=1, source_target_pairs={{0,4},{1,5},{2,6},{3,7},{4,0},{5,1},{6,2},{7,3},{8,12},{9,13},{10,... | collective-permute-start | bytes 196616 | tf_op jit(solution)/shard_map/ppermute | solution.py:201
  46.6 0.0 collective-permute-done.8.got
  46.6 1.8 %collective-permute-start.15 = (f32[128,128]{1,0:T(8,128)S(1)}, f32[128,128]{1,0:T(8,128)S(1)}, u32[]{:S(2)}, u32[]{:S(2)}) collective-permute-start(f32[128,128]{1,0:T(8,128)S(1)} %get-tuple-element.54), channel_id=1, source_target_pairs={{0,5},{1,4},{2,7},{3,6},{4,1},{5,0},{6,3},{7,2},{8,13},{9,12},{10,... | collective-permute-start | bytes 196616 | tf_op jit(solution)/shard_map/ppermute | solution.py:201
  48.4 0.0 collective-permute-done.11.refs_1_
  48.4 3.5 %collective-permute-start.16 = (f32[128,128]{1,0:T(8,128)S(1)}, f32[128,128]{1,0:T(8,128)S(1)}, u32[]{:S(2)}, u32[]{:S(2)}) collective-permute-start(f32[128,128]{1,0:T(8,128)S(1)} %get-tuple-element.55), channel_id=1, source_target_pairs={{0,6},{1,7},{2,4},{3,5},{4,2},{5,3},{6,0},{7,1},{8,14},{9,15},{10,... | collective-permute-start | bytes 196616 | tf_op jit(solution)/shard_map/ppermute | solution.py:201
  51.9 0.0 collective-permute-done.12.refs_2_
  51.9 0.3 collective-permute-start.17
  52.2 0.0 collective-permute-done.13.refs_3_
  52.2 0.0 collective-permute-done.14.refs_4_
  52.2 5.2 %collective-permute-done.15.refs_5_ = f32[128,128]{1,0:T(8,128)S(1)} collective-permute-done((f32[128,128]{1,0:T(8,128)S(1)}, f32[128,128]{1,0:T(8,128)S(1)}, u32[]{:S(2)}, u32[]{:S(2)}) %collective-permute-start.15) | collective-permute-done | bytes 65568 | tf_op jit(solution)/shard_map/ppermute | solution.py:201
  57.4 0.0 collective-permute-done.16.refs_6_
  57.4 1.6 %collective-permute-done.17.refs_7_ = f32[128,128]{1,0:T(8,128)S(1)} collective-permute-done((f32[128,128]{1,0:T(8,128)S(1)}, f32[128,128]{1,0:T(8,128)S(1)}, u32[]{:S(2)}, u32[]{:S(2)}) %collective-permute-start.17) | collective-permute-done | bytes 65568 | tf_op jit(solution)/shard_map/ppermute | solution.py:201
  59.0 1.6 %shard_map.44 = f32[2048,128]{1,0:T(8,128)} custom-call(f32[1024,128]{1,0:T(8,128)S(1)} %get-tuple-element.43.mine, f32[1024,128]{1,0:T(8,128)S(1)} %collective-permute-done.8.got, bf16[256,256]{1,0:T(8,128)(2,1)S(1)} %get-tuple-element.33.high, bf16[256,256]{1,0:T(8,128)(2,1)S(1)} %get-tuple-element.34.low, f32[128,128]{1,0:T(8,128)S(1)} %get-tuple-element.49.refs_0_, ...), custom_call_target="tpu_custom_call" | custom-call | bytes 2883584 | tf_op jit(solution)/shard_map/pallas_call | solution.py:175
  (4 shorter events, 0.0 us)
Async XLA Ops:
  0.0 1.2 %copy-start = (f32[2,131072]{1,0:T(2,128)S(1)}, f32[2,131072]{1,0:T(2,128)}, u32[]{:S(2)}) copy-start(f32[2,131072]{1,0:T(2,128)} %param.3) | copy-start | bytes 3145732
  1.2 1.0 %copy-start.2 = (f32[4,2,128,128]{3,2,1,0:T(8,128)S(1)}, f32[4,2,128,128]{3,2,1,0:T(8,128)}, u32[]{:S(2)}) copy-start(f32[4,2,128,128]{3,2,1,0:T(8,128)} %gates.3) | copy-start | bytes 1572868
  2.3 13.1 %copy-start.1 = (f32[2,131072]{1,0:T(2,128)S(1)}, f32[2,131072]{1,0:T(2,128)}, u32[]{:S(2)}) copy-start(f32[2,131072]{1,0:T(2,128)} %param.3) | copy-start | bytes 3145732
  2.9 8.9 %collective-permute-start = (f32[128,128]{1,0:T(8,128)S(1)}, f32[128,128]{1,0:T(8,128)S(1)}, u32[]{:S(2)}, u32[]{:S(2)}) collective-permute-start(f32[128,128]{1,0:T(8,128)S(1)} %get-tuple-element.36), channel_id=1, source_target_pairs={{0,1},{1,0},{2,3},{3,2},{4,5},{5,4},{6,7},{7,6},{8,9},{9,8},{10,11... | collective-permute-start | bytes 196616 | tf_op jit(solution)/shard_map/ppermute | solution.py:201
  5.9 9.5 %collective-permute-start.1 = (f32[128,128]{1,0:T(8,128)S(1)}, f32[128,128]{1,0:T(8,128)S(1)}, u32[]{:S(2)}, u32[]{:S(2)}) collective-permute-start(f32[128,128]{1,0:T(8,128)S(1)} %get-tuple-element.37), channel_id=1, source_target_pairs={{0,2},{1,3},{2,0},{3,1},{4,6},{5,7},{6,4},{7,5},{8,10},{9,11},{10,... | collective-permute-start | bytes 196616 | tf_op jit(solution)/shard_map/ppermute | solution.py:201
  7.5 8.1 %collective-permute-start.2 = (f32[128,128]{1,0:T(8,128)S(1)}, f32[128,128]{1,0:T(8,128)S(1)}, u32[]{:S(2)}, u32[]{:S(2)}) collective-permute-start(f32[128,128]{1,0:T(8,128)S(1)} %get-tuple-element.38), channel_id=1, source_target_pairs={{0,3},{1,2},{2,1},{3,0},{4,7},{5,6},{6,5},{7,4},{8,11},{9,10},{10,... | collective-permute-start | bytes 196616 | tf_op jit(solution)/shard_map/ppermute | solution.py:201
  7.5 10.3 %collective-permute-start.3 = (f32[128,128]{1,0:T(8,128)S(1)}, f32[128,128]{1,0:T(8,128)S(1)}, u32[]{:S(2)}, u32[]{:S(2)}) collective-permute-start(f32[128,128]{1,0:T(8,128)S(1)} %get-tuple-element.39), channel_id=1, source_target_pairs={{0,4},{1,5},{2,6},{3,7},{4,0},{5,1},{6,2},{7,3},{8,12},{9,13},{10,... | collective-permute-start | bytes 196616 | tf_op jit(solution)/shard_map/ppermute | solution.py:201
  10.5 10.2 %collective-permute-start.4 = (f32[128,128]{1,0:T(8,128)S(1)}, f32[128,128]{1,0:T(8,128)S(1)}, u32[]{:S(2)}, u32[]{:S(2)}) collective-permute-start(f32[128,128]{1,0:T(8,128)S(1)} %get-tuple-element.40), channel_id=1, source_target_pairs={{0,5},{1,4},{2,7},{3,6},{4,1},{5,0},{6,3},{7,2},{8,13},{9,12},{10,... | collective-permute-start | bytes 196616 | tf_op jit(solution)/shard_map/ppermute | solution.py:201
  11.8 8.9 %collective-permute-start.5 = (f32[128,128]{1,0:T(8,128)S(1)}, f32[128,128]{1,0:T(8,128)S(1)}, u32[]{:S(2)}, u32[]{:S(2)}) collective-permute-start(f32[128,128]{1,0:T(8,128)S(1)} %get-tuple-element.41), channel_id=1, source_target_pairs={{0,6},{1,7},{2,4},{3,5},{4,2},{5,3},{6,0},{7,1},{8,14},{9,15},{10,... | collective-permute-start | bytes 196616 | tf_op jit(solution)/shard_map/ppermute | solution.py:201
  15.4 7.1 %collective-permute-start.6 = (f32[128,128]{1,0:T(8,128)S(1)}, f32[128,128]{1,0:T(8,128)S(1)}, u32[]{:S(2)}, u32[]{:S(2)}) collective-permute-start(f32[128,128]{1,0:T(8,128)S(1)} %get-tuple-element.42), channel_id=1, source_target_pairs={{0,7},{1,6},{2,5},{3,4},{4,3},{5,2},{6,1},{7,0},{8,15},{9,14},{10,... | collective-permute-start | bytes 196616 | tf_op jit(solution)/shard_map/ppermute | solution.py:201
  15.6 14.9 %collective-permute-start.9 = (f32[1024,128]{1,0:T(8,128)S(1)}, f32[1024,128]{1,0:T(8,128)S(1)}, u32[]{:S(2)}, u32[]{:S(2)}) collective-permute-start(f32[1024,128]{1,0:T(8,128)S(1)} %shard_map.41.own), channel_id=1, source_target_pairs={{0,16},{8,24},{16,0},{24,8},{1,17},{9,25},{17,1},{25,9},{2,18},{10... | collective-permute-start | bytes 1572872 | tf_op jit(solution)/shard_map/ppermute | solution.py:205
  22.5 8.1 %copy-start.3 = (f32[2,2,4,4]{3,2,1,0:T(4,128)S(1)}, f32[2,2,4,4]{3,2,1,0:T(4,128)}, u32[]{:S(2)}) copy-start(f32[2,2,4,4]{3,2,1,0:T(4,128)} %cross.3) | copy-start | bytes 772
  23.2 15.7 %collective-permute-start.7 = (f32[1024,128]{1,0:T(8,128)S(1)}, f32[1024,128]{1,0:T(8,128)S(1)}, u32[]{:S(2)}, u32[]{:S(2)}) collective-permute-start(f32[1024,128]{1,0:T(8,128)S(1)} %shard_map.39.own), channel_id=1, source_target_pairs={{0,16},{8,24},{16,0},{24,8},{1,17},{9,25},{17,1},{25,9},{2,18},{10... | collective-permute-start | bytes 1572872 | tf_op jit(solution)/shard_map/ppermute | solution.py:205
  31.5 8.4 %collective-permute-start.10 = (f32[1024,128]{1,0:T(8,128)S(1)}, f32[1024,128]{1,0:T(8,128)S(1)}, u32[]{:S(2)}, u32[]{:S(2)}) collective-permute-start(f32[1024,128]{1,0:T(8,128)S(1)} %get-tuple-element.46), channel_id=1, source_target_pairs={{0,8},{8,0},{16,24},{24,16},{1,9},{9,1},{17,25},{25,17},{2,10},{10... | collective-permute-start | bytes 1572872 | tf_op jit(solution)/shard_map/ppermute | solution.py:205
  39.9 6.8 %collective-permute-start.8 = (f32[1024,128]{1,0:T(8,128)S(1)}, f32[1024,128]{1,0:T(8,128)S(1)}, u32[]{:S(2)}, u32[]{:S(2)}) collective-permute-start(f32[1024,128]{1,0:T(8,128)S(1)} %get-tuple-element.44), channel_id=1, source_target_pairs={{0,8},{8,0},{16,24},{24,16},{1,9},{9,1},{17,25},{25,17},{2,10},{10... | collective-permute-start | bytes 1572872 | tf_op jit(solution)/shard_map/ppermute | solution.py:205
  41.0 7.4 %collective-permute-start.11 = (f32[128,128]{1,0:T(8,128)S(1)}, f32[128,128]{1,0:T(8,128)S(1)}, u32[]{:S(2)}, u32[]{:S(2)}) collective-permute-start(f32[128,128]{1,0:T(8,128)S(1)} %get-tuple-element.50), channel_id=1, source_target_pairs={{0,1},{1,0},{2,3},{3,2},{4,5},{5,4},{6,7},{7,6},{8,9},{9,8},{10,11... | collective-permute-start | bytes 196616 | tf_op jit(solution)/shard_map/ppermute | solution.py:201
  42.6 9.3 %collective-permute-start.12 = (f32[128,128]{1,0:T(8,128)S(1)}, f32[128,128]{1,0:T(8,128)S(1)}, u32[]{:S(2)}, u32[]{:S(2)}) collective-permute-start(f32[128,128]{1,0:T(8,128)S(1)} %get-tuple-element.51), channel_id=1, source_target_pairs={{0,2},{1,3},{2,0},{3,1},{4,6},{5,7},{6,4},{7,5},{8,10},{9,11},{10,... | collective-permute-start | bytes 196616 | tf_op jit(solution)/shard_map/ppermute | solution.py:201
  42.6 9.6 %collective-permute-start.13 = (f32[128,128]{1,0:T(8,128)S(1)}, f32[128,128]{1,0:T(8,128)S(1)}, u32[]{:S(2)}, u32[]{:S(2)}) collective-permute-start(f32[128,128]{1,0:T(8,128)S(1)} %get-tuple-element.52), channel_id=1, source_target_pairs={{0,3},{1,2},{2,1},{3,0},{4,7},{5,6},{6,5},{7,4},{8,11},{9,10},{10,... | collective-permute-start | bytes 196616 | tf_op jit(solution)/shard_map/ppermute | solution.py:201
  44.5 7.7 %collective-permute-start.14 = (f32[128,128]{1,0:T(8,128)S(1)}, f32[128,128]{1,0:T(8,128)S(1)}, u32[]{:S(2)}, u32[]{:S(2)}) collective-permute-start(f32[128,128]{1,0:T(8,128)S(1)} %get-tuple-element.53), channel_id=1, source_target_pairs={{0,4},{1,5},{2,6},{3,7},{4,0},{5,1},{6,2},{7,3},{8,12},{9,13},{10,... | collective-permute-start | bytes 196616 | tf_op jit(solution)/shard_map/ppermute | solution.py:201
  46.6 10.8 %collective-permute-start.15 = (f32[128,128]{1,0:T(8,128)S(1)}, f32[128,128]{1,0:T(8,128)S(1)}, u32[]{:S(2)}, u32[]{:S(2)}) collective-permute-start(f32[128,128]{1,0:T(8,128)S(1)} %get-tuple-element.54), channel_id=1, source_target_pairs={{0,5},{1,4},{2,7},{3,6},{4,1},{5,0},{6,3},{7,2},{8,13},{9,12},{10,... | collective-permute-start | bytes 196616 | tf_op jit(solution)/shard_map/ppermute | solution.py:201
  48.4 8.9 %collective-permute-start.16 = (f32[128,128]{1,0:T(8,128)S(1)}, f32[128,128]{1,0:T(8,128)S(1)}, u32[]{:S(2)}, u32[]{:S(2)}) collective-permute-start(f32[128,128]{1,0:T(8,128)S(1)} %get-tuple-element.55), channel_id=1, source_target_pairs={{0,6},{1,7},{2,4},{3,5},{4,2},{5,3},{6,0},{7,1},{8,14},{9,15},{10,... | collective-permute-start | bytes 196616 | tf_op jit(solution)/shard_map/ppermute | solution.py:201
  51.9 7.1 %collective-permute-start.17 = (f32[128,128]{1,0:T(8,128)S(1)}, f32[128,128]{1,0:T(8,128)S(1)}, u32[]{:S(2)}, u32[]{:S(2)}) collective-permute-start(f32[128,128]{1,0:T(8,128)S(1)} %get-tuple-element.56), channel_id=1, source_target_pairs={{0,7},{1,6},{2,5},{3,4},{4,3},{5,2},{6,1},{7,0},{8,15},{9,14},{10,... | collective-permute-start | bytes 196616 | tf_op jit(solution)/shard_map/ppermute | solution.py:201

commit v2 on v0

v2 whole, which is shorter than its diff:
```python
import functools

import jax
import jax.numpy as jnp
from jax import lax
from jax.experimental import pallas as pl
from jax.experimental.pallas import tpu as pltpu
from jax.sharding import PartitionSpec as P

F32, BF16 = jnp.float32, jnp.bfloat16
COST = dict(enter=2, prepare=1, mix=1, after_mix=1, between=20, finish=20, last=2)


def split(value):
    high = value.astype(BF16)
    return high, (value - high.astype(F32)).astype(BF16)


def dot_split(first, second):
    product = functools.partial(jnp.dot, preferred_element_type=F32)
    return product(first[0], second[0]) + (product(first[0], second[1]) + product(first[1], second[0]))


def joined(real, imag):
    return rows([columns([real, -imag]), columns([imag, real])])


def columns(parts):
    return jnp.concatenate(parts, 1)


def rows(parts):
    return jnp.concatenate(parts, 0)


def select(width, block, by_rows):
    size = (2 * width, 2 * width)
    here = lax.broadcasted_iota(jnp.int32, size, 0 if by_rows else 1)
    other = lax.broadcasted_iota(jnp.int32, size, 1 if by_rows else 0)
    row, part, slot = here % block, (here // block) % 2, here // (2 * block)
    source = part * width + (slot ^ lax.axis_index("qb")) * block + row
    return (source == other).astype(F32).astype(BF16)


def pick(first, second):
    return jnp.dot(first, second, preferred_element_type=F32).astype(BF16)


class Sizes:
    def __init__(self, width, inner, mid, count):
        self.width, self.inner, self.mid, self.count = width, inner, mid, count
        self.block, self.upper = width // inner, inner // 2
        self.cell = count * self.block

    def in_pair(self, part, slot, i):
        return pl.ds((part * self.upper + slot // 2) * self.cell + i * self.block, self.block)

    def in_piece(self, part, slot, i):
        return pl.ds((part * 2 + slot % 2) * self.cell + i * self.block, self.block)

    def in_chunk(self, part, slot, i):
        return pl.ds(((part * 2 + slot % 2) * self.upper + slot // 2) * self.cell + i * self.block, self.block)

    def cut(self, value, slot, part, i):
        at = (slot * 2 + part) * self.block
        return value[at : at + self.block, i * self.width : (i + 1) * self.width]

    def collect(self, read):
        return columns(
            [
                rows([read(part, slot, i) for slot in range(self.inner) for part in range(2)])
                for i in range(self.count)
            ]
        )


def enter(a, b, x, gates, high, low, near, far, *refs):
    *pieces, held, table, sems = refs
    width, mid = a.width, a.mid
    copies = [
        pltpu.make_async_copy(gates.at[0], table, sems.at[0]),
        pltpu.make_async_copy(x, held, sems.at[1]),
    ]
    for copy in copies:
        copy.start()
    chosen = select(width, a.block, True)
    copies[0].wait()
    gate = split(joined(table[0], table[1]))
    gate = pick(chosen, gate[0]), pick(chosen, gate[1])
    high[...], low[...] = gate
    copies[1].wait()
    state = columns([rows([held[pl.ds(2 * m + part, width, 2 * mid), :] for part in range(2)]) for m in range(mid)])
    done_a = dot_split(gate, split(state[:, : a.count * width]))
    for slot in range(a.inner):
        for part in range(2):
            for i in range(a.count):
                (near, far)[slot % 2][a.in_pair(part, slot, i), :] = a.cut(done_a, slot, part, i)
    done_b = dot_split(gate, split(state[:, a.count * width :]))
    for slot in range(b.inner):
        for part in range(2):
            for i in range(b.count):
                pieces[slot // 2][b.in_piece(part, slot, i), :] = b.cut(done_b, slot, part, i)


def prepare(width, block, gates, lane_high, lane_low, high, low):
    lane = lax.dot_general(
        joined(gates[1, 0], gates[1, 1]),
        joined(gates[3, 0], gates[3, 1]),
        (((0,), (1,)), ((), ())),
        precision=lax.Precision.HIGHEST,
        preferred_element_type=F32,
    )
    lane_high[...], lane_low[...] = split(lane)
    chosen = select(width, block, False)
    gate = split(joined(gates[2, 0], gates[2, 1]))
    high[...], low[...] = pick(gate[0], chosen), pick(gate[1], chosen)


def entry(cross, which, i, j):
    if which is not None:
        return cross[which, 0, i, j], cross[which, 1, i, j]
    real = imag = None
    for k in range(cross.shape[-1]):
        ar, ai, br, bi = cross[1, 0, i, k], cross[1, 1, i, k], cross[0, 0, k, j], cross[0, 1, k, j]
        r, m = ar * br - ai * bi, ar * bi + ai * br
        real, imag = (r, m) if real is None else (real + r, imag + m)
    return real, imag


def mix(which, stride, cross, *refs):
    *pairs, mine, other = refs
    count = len(pairs) // 2
    me = (lax.axis_index("grp") // stride) % 4
    for target, out in ((me, mine), (me ^ 1, other)):
        (ar, ai), (br, bi) = entry(cross, which, target, me), entry(cross, which, target, me ^ 2)
        for i in range(count):
            own, far = pairs[2 * i], pairs[2 * i + 1]
            half = own.shape[0] // 2
            real, imag = pl.ds(0, half), pl.ds(half, half)
            xr, xi, yr, yi = own[real, :], own[imag, :], far[real, :], far[imag, :]
            out[pl.ds(i * half, half), :] = ar * xr - ai * xi + (br * yr - bi * yi)
            out[pl.ds((count + i) * half, half), :] = ar * xi + ai * xr + (br * yi + bi * yr)


def after_mix(s, mine, got, lane_high, lane_low, *pieces):
    half, width = mine.shape[0] // 2, s.width
    real, imag = pl.ds(0, half), pl.ds(half, half)
    wide = columns([mine[real, :] + got[real, :], mine[imag, :] + got[imag, :]])
    wide = dot_split(split(wide), (lane_high[...], lane_low[...]))
    for part in range(2):
        for low in range(2):
            for up, piece in enumerate(pieces):
                at = (low * s.upper + up) * s.cell
                piece[pl.ds((part * 2 + low) * s.cell, s.cell), :] = wide[
                    at : at + s.cell, part * width : (part + 1) * width
                ]


def between(s, lane_high, lane_low, *refs):
    *pieces, near, far = refs
    half, width = 2 * s.cell, s.width
    wide = rows([columns([p[pl.ds(0, half), :], p[pl.ds(half, half), :]]) for p in pieces])
    wide = dot_split(split(wide), (lane_high[...], lane_low[...]))
    for part in range(2):
        for low, pair in enumerate((near, far)):
            for up in range(s.upper):
                at = (up * 2 + low) * s.cell
                pair[pl.ds((part * s.upper + up) * s.cell, s.cell), :] = wide[
                    at : at + s.cell, part * width : (part + 1) * width
                ]


def finish(s, high, low, *refs):
    *pieces, out = refs
    state = s.collect(lambda part, slot, i: pieces[slot // 2][s.in_piece(part, slot, i), :])
    state = dot_split((high[...], low[...]), split(state))
    for i in range(s.count):
        out[pl.ds(2 * i * s.width, 2 * s.width), :] = state[:, i * s.width : (i + 1) * s.width]


def last(a, b, high, low, mine, got, done, out):
    width, step = a.width, 2 * a.mid

    def read(part, slot, i):
        at = b.in_chunk(part, slot, i)
        return mine[at, :] + got[at, :]

    for i in range(a.count):
        for part in range(2):
            out[pl.ds(2 * i + part, width, step), :] = done[pl.ds((2 * i + part) * width, width), :]
    state = dot_split((high[...], low[...]), split(b.collect(read)))
    for i in range(b.count):
        for part in range(2):
            out[pl.ds(2 * (a.count + i) + part, width, step), :] = state[
                part * width : (part + 1) * width, i * width : (i + 1) * width
            ]


def call(body, outs, *args, places={}, scratch=()):
    vmem = pl.BlockSpec(memory_space=pltpu.VMEM)
    cost = COST[body.func.__name__]
    return pl.pallas_call(
        body,
        out_shape=outs,
        in_specs=[pl.BlockSpec(memory_space=places[i]) if i in places else vmem for i in range(len(args))],
        out_specs=[vmem] * len(outs),
        scratch_shapes=scratch,
        compiler_params=pltpu.CompilerParams(vmem_limit_bytes=24 * 2**20),
        cost_estimate=pl.CostEstimate(flops=int(cost * 1e9), bytes_accessed=0, transcendentals=0),
    )(*args)


def on_device(amplitudes, layer_gates, cross_gates):
    inner, groups = lax.axis_size("qb"), lax.axis_size("grp")
    width, local = layer_gates.shape[-1], amplitudes.shape[-1]
    mid = local // (width * width)
    a, b = (Sizes(width, inner, mid, count) for count in (mid // 2, mid - mid // 2))
    bind = functools.partial
    array = lambda count, dtype=F32: jax.ShapeDtypeStruct((count, width), dtype)
    table = jax.ShapeDtypeStruct((2 * width, 2 * width), BF16)
    pair = lambda s: [array(2 * s.upper * s.cell)] * 2
    piece = lambda s: [array(4 * s.cell)] * s.upper
    whole = lambda s: array(4 * s.upper * s.cell)

    def send(value, group_step, inner_step):
        devices = [(g, q) for g in range(groups) for q in range(inner)]
        number = lambda g, q: g * inner + q
        perm = [(number(g, q), number(g ^ group_step, q ^ inner_step)) for g, q in devices]
        return lax.ppermute(value, ("grp", "qb"), perm)

    order = cross_gates.shape[-1]
    stages = [(None, 1)] if groups == order else [(0, 1), (1, groups // order)]

    def swap_low_and_cross(near, far, s):
        (which, stride), *more = stages
        pairs = [near, send(near, 2 * stride, 0), send(far, 0, 1), send(far, 2 * stride, 1)]
        while True:
            mine, other = call(bind(mix, which, stride), [whole(s)] * 2, cross_gates, *pairs, places={0: pltpu.SMEM})
            got = send(other, stride, 0)
            if not more:
                return mine, got
            (which, stride), *more = more
            pairs = [mine + got, send(mine + got, 2 * stride, 0)]

    def swap_upper(pieces):
        moved = {k: send(pieces[k], 0, 2 * k) for k in reversed(range(1, len(pieces)))}
        return [pieces[0]] + [moved[k] for k in range(1, len(pieces))]

    x = amplitudes.reshape(2, local // width, width).transpose(1, 0, 2).reshape(2 * local // width, width)
    gate_high, gate_low, near, far, *pieces = call(
        bind(enter, a, b),
        [table, table] + pair(a) + piece(b),
        x,
        layer_gates,
        places={0: pltpu.HBM, 1: pltpu.HBM},
        scratch=[pltpu.VMEM(x.shape, F32), pltpu.VMEM(layer_gates.shape[1:], F32), pltpu.SemaphoreType.DMA((2,))],
    )
    lane_high, lane_low, third_high, third_low = call(bind(prepare, width, a.block), [table] * 4, layer_gates)
    mine, got = swap_low_and_cross(near, far, a)
    near, far = call(bind(between, b), pair(b), lane_high, lane_low, *swap_upper(pieces))
    pieces = call(bind(after_mix, a), piece(a), mine, got, lane_high, lane_low)
    (done,) = call(bind(finish, a), [whole(a)], third_high, third_low, *swap_upper(pieces))
    mine, got = swap_low_and_cross(near, far, b)
    (out,) = call(bind(last, a, b), [jax.ShapeDtypeStruct(x.shape, F32)], third_high, third_low, mine, got, done)
    return out.reshape(local // width, 2, width).transpose(1, 0, 2).reshape(2, local)


def solution(mesh):
    return jax.shard_map(
        on_device,
        mesh=mesh,
        in_specs=(P(None, ("grp", "qb")), P(), P()),
        out_specs=P(None, ("grp", "qb")),
        check_vma=False,
    )
```

time: 102 us -> 42.7 us (0.42)
  blocking collectives: 66.8 us -> 0 us
  starting transfers between devices: 0 us -> 23.9 us
  matrix products: 20.3 us -> 0 us
  local copies, waits for them, and re-layouts: 11.8 us -> 2.27 us
  waiting for transfers between devices: 0 us -> 9.34 us
  Pallas kernels: 0 us -> 6.92 us
  other arithmetic: 2.1 us -> 0 us
    all_to_all x3 -> x0, blocking collectives: 66.8 us -> none  [the longest x1 32.8 us: on_device(): lax.all_to_all(blocks, 'qb', split_axis=1, concat_axis=1, tiled=True)]
    ppermute x0 -> x14, starting transfers between devices: none -> 23.9 us  [send(): return lax.ppermute(value, ('grp', 'qb'), perm)]
    dot_general x24 -> x0, matrix products: 20.3 us -> none  [the longest x16 11 us: product(): lax.dot_general(left, right, numbers, precision=lax.Precision.HIGHEST, pr...]
    ppermute x0 -> x14, waiting for transfers between devices: none -> 9.34 us  [send(): return lax.ppermute(value, ('grp', 'qb'), perm)]
    slice x3 -> x0, local copies, waits for them, and re-layouts: 7.98 us -> none  [the longest x2 7.17 us: dot_parts(): real_part = product(first[0], second[0]) - product(first[1], second[1])]
    pallas_call x0 -> x8, Pallas kernels: none -> 6.92 us  [call(): pl.pallas_call(body, out_shape=outs, in_specs=[pl.BlockSpec(memory_space=...]
    another operation x3 -> x0, other arithmetic: 2.1 us -> none  [the longest x2 1.87 us: dot_parts(): return jnp.stack([real_part, imag_part])]
    unnamed x5 -> x6, local copies, waits for them, and re-layouts: 1.92 us -> 2.27 us
  transfers between devices with their start and end apart: 0 -> 14, of which waited for: 0 -> 7; matrix products, arithmetic and copies ran while one was open for 0% -> 0% of each run, Pallas kernels for 0% -> 8%
where the time goes in v2:
time: 42.7 us; the launch traced here: 42.5 us
  starting transfers between devices  23.9 us (56%)
  waiting for transfers between devices  9.34 us (22%)
  Pallas kernels  6.92 us (16%)
  local copies, waits for them, and re-layouts  2.27 us (5%)
    ppermute x14, starting transfers between devices, send(): return lax.ppermute(value, ('grp', 'qb'), perm)  23.9 us
    ppermute x14, waiting for transfers between devices, send(): return lax.ppermute(value, ('grp', 'qb'), perm)  9.34 us
    pallas_call x8, Pallas kernels, call(): pl.pallas_call(body, out_shape=outs, in_specs=[pl.BlockSpec(memory_space=...  6.92 us
    unnamed x6, local copies, waits for them, and re-layouts  2.27 us
  transfers between devices with their start and end apart: 14, of which 7 were waited for; matrix products, arithmetic and copies ran while one was open for 0% of the time, Pallas kernels for 8%

profile of v2, /device:TPU:0, one launch (start us, length us, event | category | flops | bytes accessed | tf_op | source)
XLA Modules:
  0.0 42.5 jit_solution(15530428327440033255)
XLA Ops:
  0.0 0.0 copy-start
  0.0 1.2 %copy-done = f32[2,131072]{1,0:T(2,128)S(1)} copy-done((f32[2,131072]{1,0:T(2,128)S(1)}, f32[2,131072]{1,0:T(2,128)}, u32[]{:S(2)}) %copy-start) | copy-done | bytes 1048600
  1.2 0.0 copy-start.1
  1.2 1.0 %copy-done.1 = f32[4,2,128,128]{3,2,1,0:T(8,128)S(1)} copy-done((f32[4,2,128,128]{3,2,1,0:T(8,128)S(1)}, f32[4,2,128,128]{3,2,1,0:T(8,128)}, u32[]{:S(2)}) %copy-start.1) | copy-done | bytes 524312
  2.3 1.8 %shard_map.38 = (bf16[256,256]{1,0:T(8,128)(2,1)}, bf16[256,256]{1,0:T(8,128)(2,1)}, f32[512,128]{1,0:T(8,128)S(1)}, f32[512,128]{1,0:T(8,128)S(1)}, f32[256,128...) custom-call(f32[2048,128]{1,0:T(8,128)S(1)} %bitcast.10, ...), custom_call_target="tpu_custom_call" | custom-call | flops 2000000000 | tf_op jit(solution)/shard_map/pallas_call | solution.py:202
  4.1 3.0 %collective-permute-start.7 = (f32[512,128]{1,0:T(8,128)S(1)}, f32[512,128]{1,0:T(8,128)S(1)}, u32[]{:S(2)}, u32[]{:S(2)}) collective-permute-start(f32[512,128]{1,0:T(8,128)S(1)} %get-tuple-element.37.refs_0_), channel_id=1, source_target_pairs={{0,16},{1,17},{2,18},{3,19},{4,20},{5,21},{6,22},{7,23},{8,24},{9,... | collective-permute-start | bytes 786440 | tf_op jit(solution)/shard_map/ppermute | solution.py:229
  7.1 1.5 %collective-permute-start.8 = (f32[512,128]{1,0:T(8,128)S(1)}, f32[512,128]{1,0:T(8,128)S(1)}, u32[]{:S(2)}, u32[]{:S(2)}) collective-permute-start(f32[512,128]{1,0:T(8,128)S(1)} %get-tuple-element.38), channel_id=1, source_target_pairs={{0,1},{1,0},{2,3},{3,2},{4,5},{5,4},{6,7},{7,6},{8,9},{9,8},{10,11... | collective-permute-start | bytes 786440 | tf_op jit(solution)/shard_map/ppermute | solution.py:229
  8.6 0.0 collective-permute-start.9
  8.6 2.0 %collective-permute-start = (f32[256,128]{1,0:T(8,128)S(1)}, f32[256,128]{1,0:T(8,128)S(1)}, u32[]{:S(2)}, u32[]{:S(2)}) collective-permute-start(f32[256,128]{1,0:T(8,128)S(1)} %get-tuple-element.30), channel_id=1, source_target_pairs={{0,2},{1,3},{2,0},{3,1},{4,6},{5,7},{6,4},{7,5},{8,10},{9,11},{10,... | collective-permute-start | bytes 393224 | tf_op jit(solution)/shard_map/ppermute | solution.py:229
  10.6 2.6 %collective-permute-start.1 = (f32[256,128]{1,0:T(8,128)S(1)}, f32[256,128]{1,0:T(8,128)S(1)}, u32[]{:S(2)}, u32[]{:S(2)}) collective-permute-start(f32[256,128]{1,0:T(8,128)S(1)} %get-tuple-element.31), channel_id=1, source_target_pairs={{0,4},{1,5},{2,6},{3,7},{4,0},{5,1},{6,2},{7,3},{8,12},{9,13},{10,... | collective-permute-start | bytes 393224 | tf_op jit(solution)/shard_map/ppermute | solution.py:229
  13.2 1.0 %collective-permute-done.7.refs_1_ = f32[512,128]{1,0:T(8,128)S(1)} collective-permute-done((f32[512,128]{1,0:T(8,128)S(1)}, f32[512,128]{1,0:T(8,128)S(1)}, u32[]{:S(2)}, u32[]{:S(2)}) %collective-permute-start.7) | collective-permute-done | bytes 262176 | tf_op jit(solution)/shard_map/ppermute | solution.py:229
  14.2 0.0 copy-start.2
  14.2 4.2 %collective-permute-start.2 = (f32[256,128]{1,0:T(8,128)S(1)}, f32[256,128]{1,0:T(8,128)S(1)}, u32[]{:S(2)}, u32[]{:S(2)}) collective-permute-start(f32[256,128]{1,0:T(8,128)S(1)} %get-tuple-element.32), channel_id=1, source_target_pairs={{0,6},{1,7},{2,4},{3,5},{4,2},{5,3},{6,0},{7,1},{8,14},{9,15},{10,... | collective-permute-start | bytes 393224 | tf_op jit(solution)/shard_map/ppermute | solution.py:229
  18.4 0.5 %shard_map.37 = (bf16[256,256]{1,0:T(8,128)(2,1)S(1)}, bf16[256,256]{1,0:T(8,128)(2,1)S(1)}, bf16[256,256]{1,0:T(8,128)(2,1)S(1)}, bf16[256,256]{1,0:T(8,128)(2,1)S(1)}) custom-call(f32[4,2,128,128]{3,2,1,0:T(8,128)S(1)} %copy-done.1), custom_call_target="tpu_custom_call" | custom-call | flops 1000000000 | tf_op jit(solution)/shard_map/pallas_call | solution.py:202
  18.9 1.6 %collective-permute-done.8.refs_2_ = f32[512,128]{1,0:T(8,128)S(1)} collective-permute-done((f32[512,128]{1,0:T(8,128)S(1)}, f32[512,128]{1,0:T(8,128)S(1)}, u32[]{:S(2)}, u32[]{:S(2)}) %collective-permute-start.8) | collective-permute-done | bytes 262176 | tf_op jit(solution)/shard_map/ppermute | solution.py:229
  20.5 0.0 collective-permute-done.9.refs_3_
  20.5 0.0 copy-done.2
  20.5 1.0 %shard_map.41 = (f32[1024,128]{1,0:T(8,128)S(1)}, f32[1024,128]{1,0:T(8,128)S(1)}) custom-call(f32[2,2,4,4]{3,2,1,0:T(4,128)S(1)} %copy-done.2, f32[512,128]{1,0:T(8,128)S(1)} %get-tuple-element.37.refs_0_, f32[512,128]{1,0:T(8,128)S(1)} %collective-permute-done.7.refs_1_, f32[512,128]{1,0:T(8,128)S(1)} %collective-permute-done.8.refs_2_, ...), custom_call_target="tpu_custom_call" | custom-call | flops 1000000000 | tf_op jit(solution)/shard_map/pallas_call | solution.py:202
  21.5 0.1 collective-permute-start.10
  21.5 0.0 collective-permute-done.refs_1_
  21.5 0.7 %collective-permute-done.1.refs_2_ = f32[256,128]{1,0:T(8,128)S(1)} collective-permute-done((f32[256,128]{1,0:T(8,128)S(1)}, f32[256,128]{1,0:T(8,128)S(1)}, u32[]{:S(2)}, u32[]{:S(2)}) %collective-permute-start.1) | collective-permute-done | bytes 131104 | tf_op jit(solution)/shard_map/ppermute | solution.py:229
  22.2 0.0 collective-permute-done.2.refs_3_
  22.2 0.4 shard_map.39
  22.6 1.6 %collective-permute-start.3 = (f32[512,128]{1,0:T(8,128)S(1)}, f32[512,128]{1,0:T(8,128)S(1)}, u32[]{:S(2)}, u32[]{:S(2)}) collective-permute-start(f32[512,128]{1,0:T(8,128)S(1)} %get-tuple-element.33.refs_0_), channel_id=1, source_target_pairs={{0,16},{1,17},{2,18},{3,19},{4,20},{5,21},{6,22},{7,23},{8,24},{9,... | collective-permute-start | bytes 786440 | tf_op jit(solution)/shard_map/ppermute | solution.py:229
  24.1 1.5 %collective-permute-start.4 = (f32[512,128]{1,0:T(8,128)S(1)}, f32[512,128]{1,0:T(8,128)S(1)}, u32[]{:S(2)}, u32[]{:S(2)}) collective-permute-start(f32[512,128]{1,0:T(8,128)S(1)} %get-tuple-element.34), channel_id=1, source_target_pairs={{0,1},{1,0},{2,3},{3,2},{4,5},{5,4},{6,7},{7,6},{8,9},{9,8},{10,11... | collective-permute-start | bytes 786440 | tf_op jit(solution)/shard_map/ppermute | solution.py:229
  25.7 0.5 %collective-permute-start.5 = (f32[512,128]{1,0:T(8,128)S(1)}, f32[512,128]{1,0:T(8,128)S(1)}, u32[]{:S(2)}, u32[]{:S(2)}) collective-permute-start(f32[512,128]{1,0:T(8,128)S(1)} %get-tuple-element.34), channel_id=1, source_target_pairs={{0,17},{1,16},{2,19},{3,18},{4,21},{5,20},{6,23},{7,22},{8,25},{9,... | collective-permute-start | bytes 786440 | tf_op jit(solution)/shard_map/ppermute | solution.py:229
  26.1 0.0 collective-permute-done.10.got
  26.1 0.4 shard_map.42
  26.5 2.6 %collective-permute-start.11 = (f32[256,128]{1,0:T(8,128)S(1)}, f32[256,128]{1,0:T(8,128)S(1)}, u32[]{:S(2)}, u32[]{:S(2)}) collective-permute-start(f32[256,128]{1,0:T(8,128)S(1)} %get-tuple-element.42), channel_id=1, source_target_pairs={{0,2},{1,3},{2,0},{3,1},{4,6},{5,7},{6,4},{7,5},{8,10},{9,11},{10,... | collective-permute-start | bytes 393224 | tf_op jit(solution)/shard_map/ppermute | solution.py:229
  29.1 1.3 %collective-permute-start.12 = (f32[256,128]{1,0:T(8,128)S(1)}, f32[256,128]{1,0:T(8,128)S(1)}, u32[]{:S(2)}, u32[]{:S(2)}) collective-permute-start(f32[256,128]{1,0:T(8,128)S(1)} %get-tuple-element.43), channel_id=1, source_target_pairs={{0,4},{1,5},{2,6},{3,7},{4,0},{5,1},{6,2},{7,3},{8,12},{9,13},{10,... | collective-permute-start | bytes 393224 | tf_op jit(solution)/shard_map/ppermute | solution.py:229
  30.4 1.5 %collective-permute-done.3.refs_1_ = f32[512,128]{1,0:T(8,128)S(1)} collective-permute-done((f32[512,128]{1,0:T(8,128)S(1)}, f32[512,128]{1,0:T(8,128)S(1)}, u32[]{:S(2)}, u32[]{:S(2)}) %collective-permute-start.3) | collective-permute-done | bytes 262176 | tf_op jit(solution)/shard_map/ppermute | solution.py:229
  31.8 3.0 %collective-permute-start.13 = (f32[256,128]{1,0:T(8,128)S(1)}, f32[256,128]{1,0:T(8,128)S(1)}, u32[]{:S(2)}, u32[]{:S(2)}) collective-permute-start(f32[256,128]{1,0:T(8,128)S(1)} %get-tuple-element.44), channel_id=1, source_target_pairs={{0,6},{1,7},{2,4},{3,5},{4,2},{5,3},{6,0},{7,1},{8,14},{9,15},{10,... | collective-permute-start | bytes 393224 | tf_op jit(solution)/shard_map/ppermute | solution.py:229
  34.8 0.8 %collective-permute-done.4.refs_2_ = f32[512,128]{1,0:T(8,128)S(1)} collective-permute-done((f32[512,128]{1,0:T(8,128)S(1)}, f32[512,128]{1,0:T(8,128)S(1)}, u32[]{:S(2)}, u32[]{:S(2)}) %collective-permute-start.4) | collective-permute-done | bytes 262176 | tf_op jit(solution)/shard_map/ppermute | solution.py:229
  35.6 1.6 %collective-permute-done.5.refs_3_ = f32[512,128]{1,0:T(8,128)S(1)} collective-permute-done((f32[512,128]{1,0:T(8,128)S(1)}, f32[512,128]{1,0:T(8,128)S(1)}, u32[]{:S(2)}, u32[]{:S(2)}) %collective-permute-start.5) | collective-permute-done | bytes 262176 | tf_op jit(solution)/shard_map/ppermute | solution.py:229
  37.3 1.0 %shard_map.40 = (f32[1024,128]{1,0:T(8,128)S(1)}, f32[1024,128]{1,0:T(8,128)S(1)}) custom-call(f32[2,2,4,4]{3,2,1,0:T(4,128)S(1)} %copy-done.2, f32[512,128]{1,0:T(8,128)S(1)} %get-tuple-element.33.refs_0_, f32[512,128]{1,0:T(8,128)S(1)} %collective-permute-done.3.refs_1_, f32[512,128]{1,0:T(8,128)S(1)} %collective-permute-done.4.refs_2_, ...), custom_call_target="tpu_custom_call" | custom-call | flops 1000000000 | tf_op jit(solution)/shard_map/pallas_call | solution.py:202
  38.3 0.1 collective-permute-start.6
  38.3 0.0 collective-permute-done.11.refs_1_
  38.4 2.2 %collective-permute-done.12.refs_2_ = f32[256,128]{1,0:T(8,128)S(1)} collective-permute-done((f32[256,128]{1,0:T(8,128)S(1)}, f32[256,128]{1,0:T(8,128)S(1)}, u32[]{:S(2)}, u32[]{:S(2)}) %collective-permute-start.12) | collective-permute-done | bytes 131104 | tf_op jit(solution)/shard_map/ppermute | solution.py:229
  40.6 0.0 collective-permute-done.13.refs_3_
  40.6 0.4 shard_map.43.done
  41.0 0.0 collective-permute-done.6.got
  41.0 1.5 %shard_map.44 = f32[2048,128]{1,0:T(8,128)} custom-call(bf16[256,256]{1,0:T(8,128)(2,1)S(1)} %get-tuple-element.25.high, bf16[256,256]{1,0:T(8,128)(2,1)S(1)} %get-tuple-element.26.low, f32[1024,128]{1,0:T(8,128)S(1)} %get-tuple-element.35.mine, f32[1024,128]{1,0:T(8,128)S(1)} %collective-permute-done.6.got, f32[1024,128]{1,0:T(8,128)S(1)} %shard_map.43.done), custom_call_target="tpu_custom_call" | custom-call | flops 2000000000 | tf_op jit(solution)/shard_map/pallas_call | solution.py:202
Async XLA Ops:
  0.0 1.2 %copy-start = (f32[2,131072]{1,0:T(2,128)S(1)}, f32[2,131072]{1,0:T(2,128)}, u32[]{:S(2)}) copy-start(f32[2,131072]{1,0:T(2,128)} %param.3) | copy-start | bytes 3145732
  1.2 1.0 %copy-start.1 = (f32[4,2,128,128]{3,2,1,0:T(8,128)S(1)}, f32[4,2,128,128]{3,2,1,0:T(8,128)}, u32[]{:S(2)}) copy-start(f32[4,2,128,128]{3,2,1,0:T(8,128)} %gates.3) | copy-start | bytes 1572868
  4.1 10.1 %collective-permute-start.7 = (f32[512,128]{1,0:T(8,128)S(1)}, f32[512,128]{1,0:T(8,128)S(1)}, u32[]{:S(2)}, u32[]{:S(2)}) collective-permute-start(f32[512,128]{1,0:T(8,128)S(1)} %get-tuple-element.37.refs_0_), channel_id=1, source_target_pairs={{0,16},{1,17},{2,18},{3,19},{4,20},{5,21},{6,22},{7,23},{8,24},{9,... | collective-permute-start | bytes 786440 | tf_op jit(solution)/shard_map/ppermute | solution.py:229
  7.1 13.4 %collective-permute-start.8 = (f32[512,128]{1,0:T(8,128)S(1)}, f32[512,128]{1,0:T(8,128)S(1)}, u32[]{:S(2)}, u32[]{:S(2)}) collective-permute-start(f32[512,128]{1,0:T(8,128)S(1)} %get-tuple-element.38), channel_id=1, source_target_pairs={{0,1},{1,0},{2,3},{3,2},{4,5},{5,4},{6,7},{7,6},{8,9},{9,8},{10,11... | collective-permute-start | bytes 786440 | tf_op jit(solution)/shard_map/ppermute | solution.py:229
  8.6 11.9 %collective-permute-start.9 = (f32[512,128]{1,0:T(8,128)S(1)}, f32[512,128]{1,0:T(8,128)S(1)}, u32[]{:S(2)}, u32[]{:S(2)}) collective-permute-start(f32[512,128]{1,0:T(8,128)S(1)} %get-tuple-element.38), channel_id=1, source_target_pairs={{0,17},{1,16},{2,19},{3,18},{4,21},{5,20},{6,23},{7,22},{8,25},{9,... | collective-permute-start | bytes 786440 | tf_op jit(solution)/shard_map/ppermute | solution.py:229
  8.6 12.9 %collective-permute-start = (f32[256,128]{1,0:T(8,128)S(1)}, f32[256,128]{1,0:T(8,128)S(1)}, u32[]{:S(2)}, u32[]{:S(2)}) collective-permute-start(f32[256,128]{1,0:T(8,128)S(1)} %get-tuple-element.30), channel_id=1, source_target_pairs={{0,2},{1,3},{2,0},{3,1},{4,6},{5,7},{6,4},{7,5},{8,10},{9,11},{10,... | collective-permute-start | bytes 393224 | tf_op jit(solution)/shard_map/ppermute | solution.py:229
  10.6 11.5 %collective-permute-start.1 = (f32[256,128]{1,0:T(8,128)S(1)}, f32[256,128]{1,0:T(8,128)S(1)}, u32[]{:S(2)}, u32[]{:S(2)}) collective-permute-start(f32[256,128]{1,0:T(8,128)S(1)} %get-tuple-element.31), channel_id=1, source_target_pairs={{0,4},{1,5},{2,6},{3,7},{4,0},{5,1},{6,2},{7,3},{8,12},{9,13},{10,... | collective-permute-start | bytes 393224 | tf_op jit(solution)/shard_map/ppermute | solution.py:229
  14.2 6.3 %copy-start.2 = (f32[2,2,4,4]{3,2,1,0:T(4,128)S(1)}, f32[2,2,4,4]{3,2,1,0:T(4,128)}, u32[]{:S(2)}) copy-start(f32[2,2,4,4]{3,2,1,0:T(4,128)} %cross.3) | copy-start | bytes 772
  14.2 8.0 %collective-permute-start.2 = (f32[256,128]{1,0:T(8,128)S(1)}, f32[256,128]{1,0:T(8,128)S(1)}, u32[]{:S(2)}, u32[]{:S(2)}) collective-permute-start(f32[256,128]{1,0:T(8,128)S(1)} %get-tuple-element.32), channel_id=1, source_target_pairs={{0,6},{1,7},{2,4},{3,5},{4,2},{5,3},{6,0},{7,1},{8,14},{9,15},{10,... | collective-permute-start | bytes 393224 | tf_op jit(solution)/shard_map/ppermute | solution.py:229
  21.5 4.7 %collective-permute-start.10 = (f32[1024,128]{1,0:T(8,128)S(1)}, f32[1024,128]{1,0:T(8,128)S(1)}, u32[]{:S(2)}, u32[]{:S(2)}) collective-permute-start(f32[1024,128]{1,0:T(8,128)S(1)} %get-tuple-element.40), channel_id=1, source_target_pairs={{0,8},{1,9},{2,10},{3,11},{4,12},{5,13},{6,14},{7,15},{8,0},{9,1},... | collective-permute-start | bytes 1572872 | tf_op jit(solution)/shard_map/ppermute | solution.py:229
  22.6 9.3 %collective-permute-start.3 = (f32[512,128]{1,0:T(8,128)S(1)}, f32[512,128]{1,0:T(8,128)S(1)}, u32[]{:S(2)}, u32[]{:S(2)}) collective-permute-start(f32[512,128]{1,0:T(8,128)S(1)} %get-tuple-element.33.refs_0_), channel_id=1, source_target_pairs={{0,16},{1,17},{2,18},{3,19},{4,20},{5,21},{6,22},{7,23},{8,24},{9,... | collective-permute-start | bytes 786440 | tf_op jit(solution)/shard_map/ppermute | solution.py:229
  24.1 11.5 %collective-permute-start.4 = (f32[512,128]{1,0:T(8,128)S(1)}, f32[512,128]{1,0:T(8,128)S(1)}, u32[]{:S(2)}, u32[]{:S(2)}) collective-permute-start(f32[512,128]{1,0:T(8,128)S(1)} %get-tuple-element.34), channel_id=1, source_target_pairs={{0,1},{1,0},{2,3},{3,2},{4,5},{5,4},{6,7},{7,6},{8,9},{9,8},{10,11... | collective-permute-start | bytes 786440 | tf_op jit(solution)/shard_map/ppermute | solution.py:229
  25.7 11.6 %collective-permute-start.5 = (f32[512,128]{1,0:T(8,128)S(1)}, f32[512,128]{1,0:T(8,128)S(1)}, u32[]{:S(2)}, u32[]{:S(2)}) collective-permute-start(f32[512,128]{1,0:T(8,128)S(1)} %get-tuple-element.34), channel_id=1, source_target_pairs={{0,17},{1,16},{2,19},{3,18},{4,21},{5,20},{6,23},{7,22},{8,25},{9,... | collective-permute-start | bytes 786440 | tf_op jit(solution)/shard_map/ppermute | solution.py:229
  26.5 11.8 %collective-permute-start.11 = (f32[256,128]{1,0:T(8,128)S(1)}, f32[256,128]{1,0:T(8,128)S(1)}, u32[]{:S(2)}, u32[]{:S(2)}) collective-permute-start(f32[256,128]{1,0:T(8,128)S(1)} %get-tuple-element.42), channel_id=1, source_target_pairs={{0,2},{1,3},{2,0},{3,1},{4,6},{5,7},{6,4},{7,5},{8,10},{9,11},{10,... | collective-permute-start | bytes 393224 | tf_op jit(solution)/shard_map/ppermute | solution.py:229
  29.1 11.5 %collective-permute-start.12 = (f32[256,128]{1,0:T(8,128)S(1)}, f32[256,128]{1,0:T(8,128)S(1)}, u32[]{:S(2)}, u32[]{:S(2)}) collective-permute-start(f32[256,128]{1,0:T(8,128)S(1)} %get-tuple-element.43), channel_id=1, source_target_pairs={{0,4},{1,5},{2,6},{3,7},{4,0},{5,1},{6,2},{7,3},{8,12},{9,13},{10,... | collective-permute-start | bytes 393224 | tf_op jit(solution)/shard_map/ppermute | solution.py:229
  31.8 8.7 %collective-permute-start.13 = (f32[256,128]{1,0:T(8,128)S(1)}, f32[256,128]{1,0:T(8,128)S(1)}, u32[]{:S(2)}, u32[]{:S(2)}) collective-permute-start(f32[256,128]{1,0:T(8,128)S(1)} %get-tuple-element.44), channel_id=1, source_target_pairs={{0,6},{1,7},{2,4},{3,5},{4,2},{5,3},{6,0},{7,1},{8,14},{9,15},{10,... | collective-permute-start | bytes 393224 | tf_op jit(solution)/shard_map/ppermute | solution.py:229
  38.3 2.7 %collective-permute-start.6 = (f32[1024,128]{1,0:T(8,128)S(1)}, f32[1024,128]{1,0:T(8,128)S(1)}, u32[]{:S(2)}, u32[]{:S(2)}) collective-permute-start(f32[1024,128]{1,0:T(8,128)S(1)} %get-tuple-element.36), channel_id=1, source_target_pairs={{0,8},{1,9},{2,10},{3,11},{4,12},{5,13},{6,14},{7,15},{8,0},{9,1},... | collective-permute-start | bytes 1572872 | tf_op jit(solution)/shard_map/ppermute | solution.py:229

commit v3 on v2

v3 whole, which is shorter than its diff:
```python
import functools

import jax
import jax.numpy as jnp
from jax import lax
from jax.experimental import pallas as pl
from jax.experimental.pallas import tpu as pltpu
from jax.sharding import PartitionSpec as P

F32, BF16 = jnp.float32, jnp.bfloat16
COST = dict(enter=2, prepare=1, mix=1, after_mix=1, between=20, finish=20, last=2)


def split(value):
    high = value.astype(BF16)
    return high, (value - high.astype(F32)).astype(BF16)


def dot_split(first, second):
    product = functools.partial(jnp.dot, preferred_element_type=F32)
    return product(first[0], second[0]) + (product(first[0], second[1]) + product(first[1], second[0]))


def joined(real, imag):
    return rows([columns([real, -imag]), columns([imag, real])])


def columns(parts):
    return jnp.concatenate(parts, 1)


def rows(parts):
    return jnp.concatenate(parts, 0)


def turned(pieces):
    return [pieces[0], *pieces[:0:-1]]


def select(width, block, by_rows):
    size = (2 * width, 2 * width)
    here = lax.broadcasted_iota(jnp.int32, size, 0 if by_rows else 1)
    other = lax.broadcasted_iota(jnp.int32, size, 1 if by_rows else 0)
    row, part, slot = here % block, (here // block) % 2, here // (2 * block)
    source = part * width + (slot ^ lax.axis_index("qb")) * block + row
    return (source == other).astype(F32).astype(BF16)


def pick(first, second):
    return jnp.dot(first, second, preferred_element_type=F32).astype(BF16)


class Sizes:
    def __init__(self, width, inner, mid, count):
        self.width, self.inner, self.mid, self.count = width, inner, mid, count
        self.block, self.upper = width // inner, inner // 2
        self.cell = count * self.block

    def in_pair(self, part, slot, i):
        return pl.ds((part * self.upper + slot // 2) * self.cell + i * self.block, self.block)

    def in_piece(self, part, slot, i):
        return pl.ds((part * 2 + slot % 2) * self.cell + i * self.block, self.block)

    def cut(self, value, slot, part, i):
        at = (slot * 2 + part) * self.block
        return value[at : at + self.block, i * self.width : (i + 1) * self.width]

    def collect(self, read):
        return columns(
            [
                rows([read(part, slot, i) for slot in range(self.inner) for part in range(2)])
                for i in range(self.count)
            ]
        )


def state_of(s, read):
    return columns([rows([read(part, i) for part in range(2)]) for i in range(s.count)])


def enter(a, b, which, stride, x, gates, cross, mixing, near, far, *refs):
    *pieces, held, table, elements, sems = refs
    width, mid = a.width, a.mid
    copies = [
        pltpu.make_async_copy(gates.at[0], table, sems.at[0]),
        pltpu.make_async_copy(x, held, sems.at[1]),
        pltpu.make_async_copy(cross, elements, sems.at[2]),
    ]
    for copy in copies:
        copy.start()
    chosen = select(width, a.block, True)
    me = (lax.axis_index("grp") // stride) % 4
    copies[2].wait()
    at = 0
    for target, source in [(0, 0), (0, 2), (1, 0), (1, 2)]:
        for number in entry(elements, which, me ^ target, me ^ source):
            mixing[pl.ds(at, 1), :] = jnp.full((1, width), number, F32)
            at += 1
    copies[0].wait()
    gate = split(joined(table[0], table[1]))
    gate = pick(chosen, gate[0]), pick(chosen, gate[1])
    copies[1].wait()

    def apply(first, s):
        state = columns(
            [rows([held[pl.ds(2 * m + part, width, 2 * mid), :] for part in range(2)]) for m in range(first, first + s.count)]
        )
        return dot_split(gate, split(state))

    state = apply(a.count, b)
    for slot in range(b.inner):
        for part in range(2):
            for i in range(b.count):
                pieces[slot // 2][b.in_piece(part, slot, i), :] = b.cut(state, slot, part, i)
    state = apply(0, a)
    for slot in range(a.inner):
        for part in range(2):
            for i in range(a.count):
                (near, far)[slot % 2][a.in_pair(part, slot, i), :] = a.cut(state, slot, part, i)


def prepare(width, block, gates, lane_high, lane_low, high, low):
    lane = lax.dot_general(
        joined(gates[1, 0], gates[1, 1]),
        joined(gates[3, 0], gates[3, 1]),
        (((0,), (1,)), ((), ())),
        precision=lax.Precision.HIGHEST,
        preferred_element_type=F32,
    )
    lane_high[...], lane_low[...] = split(lane)
    chosen = select(width, block, False)
    gate = split(joined(gates[2, 0], gates[2, 1]))
    high[...], low[...] = pick(gate[0], chosen), pick(gate[1], chosen)


def entry(cross, which, i, j):
    if which is not None:
        return cross[which, 0, i, j], cross[which, 1, i, j]
    real = imag = None
    for k in range(cross.shape[-1]):
        ar, ai, br, bi = cross[1, 0, i, k], cross[1, 1, i, k], cross[0, 0, k, j], cross[0, 1, k, j]
        r, m = ar * br - ai * bi, ar * bi + ai * br
        real, imag = (r, m) if real is None else (real + r, imag + m)
    return real, imag


def times(mixing, at, real, imag):
    r, i = mixing[pl.ds(at, 1), :], mixing[pl.ds(at + 1, 1), :]
    return r * real - i * imag, r * imag + i * real


def halves(ref, first=0, count=1):
    half = ref.shape[0] // (2 * count)
    return [pl.ds((2 * first + part) * half, half) for part in range(2)]


def mixed(mixing, first, pairs):
    done = []
    for own, got in zip(pairs[::2], pairs[1::2]):
        real, imag = halves(own)
        one, two = times(mixing, first, own[real, :], own[imag, :]), times(mixing, first + 2, got[real, :], got[imag, :])
        done.append([one[0] + two[0], one[1] + two[1]])
    return done


def mix(mixing, *refs):
    *pairs, out = refs
    for low, pair in enumerate(mixed(mixing, 4, pairs)):
        for at, value in zip(halves(out, low, 2), pair):
            out[at, :] = value


def sums(mixing, got, pairs):
    return [
        [value + got[at, :] for at, value in zip(halves(got, low, 2), pair)]
        for low, pair in enumerate(mixed(mixing, 0, pairs))
    ]


def after_mix(s, mixing, got, near, near_got, far, far_got, lane_high, lane_low, *pieces):
    wide = rows([columns(pair) for pair in sums(mixing, got, (near, near_got, far, far_got))])
    wide = dot_split(split(wide), (lane_high[...], lane_low[...]))
    for part in range(2):
        for low in range(2):
            for up, piece in enumerate(pieces):
                at = (low * s.upper + up) * s.cell
                piece[pl.ds((part * 2 + low) * s.cell, s.cell), :] = wide[
                    at : at + s.cell, part * s.width : (part + 1) * s.width
                ]


def between(s, lane_high, lane_low, *refs):
    *pieces, near, far = refs
    pieces = turned(pieces)
    half, width = 2 * s.cell, s.width
    wide = rows([columns([p[pl.ds(0, half), :], p[pl.ds(half, half), :]]) for p in pieces])
    wide = dot_split(split(wide), (lane_high[...], lane_low[...]))
    for part in range(2):
        for low, pair in enumerate((near, far)):
            for up in range(s.upper):
                at = (up * 2 + low) * s.cell
                pair[pl.ds((part * s.upper + up) * s.cell, s.cell), :] = wide[
                    at : at + s.cell, part * width : (part + 1) * width
                ]


def finish(s, high, low, *refs):
    *pieces, out = refs
    pieces = turned(pieces)
    state = s.collect(lambda part, slot, i: pieces[slot // 2][s.in_piece(part, slot, i), :])
    state = dot_split((high[...], low[...]), split(state))
    for i in range(s.count):
        out[pl.ds(2 * i * s.width, 2 * s.width), :] = state[:, i * s.width : (i + 1) * s.width]


def last(a, b, mixing, got, near, near_got, far, far_got, high, low, done, out):
    width, step = a.width, 2 * a.mid
    for i in range(a.count):
        for part in range(2):
            out[pl.ds(2 * i + part, width, step), :] = done[pl.ds((2 * i + part) * width, width), :]
    pairs = sums(mixing, got, (near, near_got, far, far_got))

    def read(part, slot, i):
        at = slot // 2 * b.cell + i * b.block
        return pairs[slot % 2][part][at : at + b.block]

    state = dot_split((high[...], low[...]), split(b.collect(read)))
    for i in range(b.count):
        for part in range(2):
            out[pl.ds(2 * (a.count + i) + part, width, step), :] = state[
                part * width : (part + 1) * width, i * width : (i + 1) * width
            ]


def call(body, outs, *args, places={}, scratch=(), after=()):
    vmem = pl.BlockSpec(memory_space=pltpu.VMEM)
    specs = [pl.BlockSpec(memory_space=places[i]) if i in places else vmem for i in range(len(args))]
    cost = COST[body.func.__name__]

    def kernel(*refs):
        body(*refs[: len(args)], *refs[len(args) + len(after) :])

    return pl.pallas_call(
        kernel,
        out_shape=outs,
        in_specs=specs + [pl.BlockSpec(memory_space=pl.ANY)] * len(after),
        out_specs=[vmem] * len(outs),
        scratch_shapes=scratch,
        compiler_params=pltpu.CompilerParams(vmem_limit_bytes=24 * 2**20),
        cost_estimate=pl.CostEstimate(flops=int(cost * 1e9), bytes_accessed=0, transcendentals=0),
    )(*args, *after)


def on_device(amplitudes, layer_gates, cross_gates):
    inner, groups = lax.axis_size("qb"), lax.axis_size("grp")
    width, local = layer_gates.shape[-1], amplitudes.shape[-1]
    mid = local // (width * width)
    a, b = (Sizes(width, inner, mid, count) for count in (mid // 2, mid - mid // 2))
    bind = functools.partial
    array = lambda count, dtype=F32: jax.ShapeDtypeStruct((count, width), dtype)
    table = jax.ShapeDtypeStruct((2 * width, 2 * width), BF16)
    pair = lambda s: array(2 * s.upper * s.cell)
    piece = lambda s: [array(4 * s.cell)] * s.upper
    whole = lambda s: array(4 * s.upper * s.cell)

    def send(value, group_step, inner_step):
        devices = [(g, q) for g in range(groups) for q in range(inner)]
        number = lambda g, q: g * inner + q
        perm = [(number(g, q), number(g ^ group_step, q ^ inner_step)) for g, q in devices]
        return lax.ppermute(value, ("grp", "qb"), perm)

    def cross_alone(value, which, stride):
        me = (lax.axis_index("grp") // stride) % 4
        beside = send(value, stride, 0)

        def towards(target):
            (ar, ai), (br, bi) = entry(cross_gates, which, target, me), entry(cross_gates, which, target, me ^ 1)
            return jnp.stack(
                [
                    ar * value[0] - ai * value[1] + br * beside[0] - bi * beside[1],
                    ar * value[1] + ai * value[0] + br * beside[1] + bi * beside[0],
                ]
            )

        return towards(me) + send(towards(me ^ 2), 2 * stride, 0)

    order = cross_gates.shape[-1]
    which, stride = None, 1
    if groups != order:
        amplitudes = cross_alone(amplitudes, 0, 1)
        which, stride = 1, groups // order

    def lines(value):
        return value.reshape(2, local // width, width).transpose(1, 0, 2).reshape(2 * local // width, width)

    x = lines(amplitudes)
    mixing, near_a, far_a, *pieces_b = call(
        bind(enter, a, b, which, stride),
        [array(8), pair(a), pair(a)] + piece(b),
        *(pltpu.with_memory_space_constraint(ref, pltpu.HBM) for ref in (x, layer_gates, cross_gates)),
        places={i: pltpu.HBM for i in range(3)},
        scratch=[
            pltpu.VMEM(x.shape, F32),
            pltpu.VMEM(layer_gates.shape[1:], F32),
            pltpu.SMEM(cross_gates.shape, F32),
            pltpu.SemaphoreType.DMA((3,)),
        ],
    )
    *lane, third_high, third_low = call(bind(prepare, width, a.block), [table] * 4, layer_gates)
    third = third_high, third_low

    def swap_upper(pieces):
        moved = {k: send(pieces[k], 0, 2 * k) for k in reversed(range(1, len(pieces)))}
        return [pieces[0]] + [moved[k] for k in range(1, len(pieces))]

    def cross(near, far, s):
        pairs = near, send(near, 2 * stride, 0), send(far, 0, 1), send(far, 2 * stride, 1)
        (other,) = call(bind(mix), [whole(s)], mixing, *pairs)
        return mixing, send(other, stride, 0), *pairs

    pieces_b = swap_upper(pieces_b)
    sums_a = cross(near_a, far_a, a)
    near_b, far_b = call(bind(between, b), [pair(b)] * 2, *lane, *turned(pieces_b))
    pieces_a = call(bind(after_mix, a), piece(a), *sums_a, *lane)
    pieces_a = swap_upper(pieces_a)
    sums_b = cross(near_b, far_b, b)
    (done,) = call(bind(finish, a), [whole(a)], *third, *turned(pieces_a))
    (out,) = call(bind(last, a, b), [jax.ShapeDtypeStruct(x.shape, F32)], *sums_b, *third, done)
    return out.reshape(local // width, 2, width).transpose(1, 0, 2).reshape(2, local)


def solution(mesh):
    return jax.shard_map(
        on_device,
        mesh=mesh,
        in_specs=(P(None, ("grp", "qb")), P(), P()),
        out_specs=P(None, ("grp", "qb")),
        check_vma=False,
    )
```

time: 42.7 us -> 40.2 us (0.941)
  waiting for transfers between devices: 9.34 us -> 17.2 us
  starting transfers between devices: 23.9 us -> 17 us
  local copies, waits for them, and re-layouts: 2.27 us -> 0.01 us
  Pallas kernels: 6.92 us -> 5.77 us
    ppermute x14, waiting for transfers between devices: 9.34 us -> 17.2 us  [send(): return lax.ppermute(value, ('grp', 'qb'), perm)]
    ppermute x14, starting transfers between devices: 23.9 us -> 17 us  [send(): return lax.ppermute(value, ('grp', 'qb'), perm)]
    unnamed x6 -> x2, local copies, waits for them, and re-layouts: 2.27 us -> 0.01 us
    pallas_call x8, Pallas kernels: 6.92 us -> 5.77 us  [call(): pl.pallas_call(kernel, out_shape=outs, in_specs=specs + [pl.BlockSpec(mem...]
  transfers between devices with their start and end apart: 14 -> 14, of which waited for: 7 -> 6; matrix products, arithmetic and copies ran while one was open for 0% -> 0% of each run, Pallas kernels for 8% -> 5%
where the time goes in v3:
time: 40.2 us; the launch traced here: 40.1 us
  waiting for transfers between devices  17.2 us (43%)
  starting transfers between devices  17 us (42%)
  Pallas kernels  5.77 us (14%)
    ppermute x14, waiting for transfers between devices, send(): return lax.ppermute(value, ('grp', 'qb'), perm)  17.2 us
    ppermute x14, starting transfers between devices, send(): return lax.ppermute(value, ('grp', 'qb'), perm)  17 us
    pallas_call x8, Pallas kernels, call(): pl.pallas_call(kernel, out_shape=outs, in_specs=specs + [pl.BlockSpec(mem...  5.77 us
  transfers between devices with their start and end apart: 14, of which 6 were waited for; matrix products, arithmetic and copies ran while one was open for 0% of the time, Pallas kernels for 5%

profile of v3, /device:TPU:0, one launch (start us, length us, event | category | flops | bytes accessed | tf_op | source)
XLA Modules:
  0.0 40.1 jit_solution(1874849500385708546)
XLA Ops:
  0.0 0.0 copy-start
  0.0 2.2 %shard_map.37 = (f32[8,128]{1,0:T(8,128)S(1)}, f32[512,128]{1,0:T(8,128)S(1)}, f32[512,128]{1,0:T(8,128)S(1)}, f32[256,128]{1,0:T(8,128)S(1)}, f32[256,128]{1,0:...) custom-call(f32[2048,128]{1,0:T(8,128)} %bitcast.10, f32[4,2,128,128]{3,2,1,0:T(8,128)} %refs_0_.1, ...), custom_call_target="tpu_custom_call" | custom-call | flops 2000000000 | tf_op jit(solution)/shard_map/pallas_call | solution.py:244
  2.2 3.0 %collective-permute-start.7 = (f32[512,128]{1,0:T(8,128)S(1)}, f32[512,128]{1,0:T(8,128)S(1)}, u32[]{:S(2)}, u32[]{:S(2)}) collective-permute-start(f32[512,128]{1,0:T(8,128)S(1)} %get-tuple-element.33.refs_1_.refs_2_), channel_id=1, source_target_pairs={{0,16},{1,17},{2,18},{3,19},{4,20},{5,21},{6,22},{7,23},{8,24},{9,... | collective-permute-start | bytes 786440 | tf_op jit(solution)/shard_map/ppermute | solution.py:271
  5.2 1.5 %collective-permute-start.8 = (f32[512,128]{1,0:T(8,128)S(1)}, f32[512,128]{1,0:T(8,128)S(1)}, u32[]{:S(2)}, u32[]{:S(2)}) collective-permute-start(f32[512,128]{1,0:T(8,128)S(1)} %get-tuple-element.34), channel_id=1, source_target_pairs={{0,1},{1,0},{2,3},{3,2},{4,5},{5,4},{6,7},{7,6},{8,9},{9,8},{10,11... | collective-permute-start | bytes 786440 | tf_op jit(solution)/shard_map/ppermute | solution.py:271
  6.7 0.0 collective-permute-start.9
  6.8 4.0 %collective-permute-start = (f32[256,128]{1,0:T(8,128)S(1)}, f32[256,128]{1,0:T(8,128)S(1)}, u32[]{:S(2)}, u32[]{:S(2)}) collective-permute-start(f32[256,128]{1,0:T(8,128)S(1)} %get-tuple-element.26), channel_id=1, source_target_pairs={{0,6},{1,7},{2,4},{3,5},{4,2},{5,3},{6,0},{7,1},{8,14},{9,15},{10,... | collective-permute-start | bytes 393224 | tf_op jit(solution)/shard_map/ppermute | solution.py:271
  10.8 0.0 collective-permute-start.1
  10.8 1.5 %collective-permute-done.7.refs_2_.refs_3_ = f32[512,128]{1,0:T(8,128)S(1)} collective-permute-done((f32[512,128]{1,0:T(8,128)S(1)}, f32[512,128]{1,0:T(8,128)S(1)}, u32[]{:S(2)}, u32[]{:S(2)}) %collective-permute-start.7) | collective-permute-done | bytes 262176 | tf_op jit(solution)/shard_map/ppermute | solution.py:271
  12.4 2.1 %collective-permute-start.2 = (f32[256,128]{1,0:T(8,128)S(1)}, f32[256,128]{1,0:T(8,128)S(1)}, u32[]{:S(2)}, u32[]{:S(2)}) collective-permute-start(f32[256,128]{1,0:T(8,128)S(1)} %get-tuple-element.28), channel_id=1, source_target_pairs={{0,2},{1,3},{2,0},{3,1},{4,6},{5,7},{6,4},{7,5},{8,10},{9,11},{10,... | collective-permute-start | bytes 393224 | tf_op jit(solution)/shard_map/ppermute | solution.py:271
  14.5 0.0 copy-done
  14.5 0.5 %shard_map.38 = (bf16[256,256]{1,0:T(8,128)(2,1)S(1)}, bf16[256,256]{1,0:T(8,128)(2,1)S(1)}, bf16[256,256]{1,0:T(8,128)(2,1)S(1)}, bf16[256,256]{1,0:T(8,128)(2,1)S(1)}) custom-call(f32[4,2,128,128]{3,2,1,0:T(8,128)S(1)} %copy-done), custom_call_target="tpu_custom_call" | custom-call | flops 1000000000 | tf_op jit(solution)/shard_map/pallas_call | solution.py:244
  15.0 3.6 %collective-permute-done.8.refs_3_.refs_4_ = f32[512,128]{1,0:T(8,128)S(1)} collective-permute-done((f32[512,128]{1,0:T(8,128)S(1)}, f32[512,128]{1,0:T(8,128)S(1)}, u32[]{:S(2)}, u32[]{:S(2)}) %collective-permute-start.8) | collective-permute-done | bytes 262176 | tf_op jit(solution)/shard_map/ppermute | solution.py:271
  18.6 0.0 collective-permute-done.9.refs_4_.refs_5_
  18.6 0.1 shard_map.41
  18.8 0.1 collective-permute-start.10
  18.8 0.0 collective-permute-done.refs_3_
  18.8 2.2 %collective-permute-done.1.refs_4_ = f32[256,128]{1,0:T(8,128)S(1)} collective-permute-done((f32[256,128]{1,0:T(8,128)S(1)}, f32[256,128]{1,0:T(8,128)S(1)}, u32[]{:S(2)}, u32[]{:S(2)}) %collective-permute-start.1) | collective-permute-done | bytes 131104 | tf_op jit(solution)/shard_map/ppermute | solution.py:271
  21.0 0.0 collective-permute-done.2.refs_5_
  21.0 0.4 shard_map.39
  21.4 1.6 %collective-permute-start.3 = (f32[512,128]{1,0:T(8,128)S(1)}, f32[512,128]{1,0:T(8,128)S(1)}, u32[]{:S(2)}, u32[]{:S(2)}) collective-permute-start(f32[512,128]{1,0:T(8,128)S(1)} %get-tuple-element.29.refs_1_.refs_2_), channel_id=1, source_target_pairs={{0,16},{1,17},{2,18},{3,19},{4,20},{5,21},{6,22},{7,23},{8,24},{9,... | collective-permute-start | bytes 786440 | tf_op jit(solution)/shard_map/ppermute | solution.py:271
  23.0 1.5 %collective-permute-start.4 = (f32[512,128]{1,0:T(8,128)S(1)}, f32[512,128]{1,0:T(8,128)S(1)}, u32[]{:S(2)}, u32[]{:S(2)}) collective-permute-start(f32[512,128]{1,0:T(8,128)S(1)} %get-tuple-element.30), channel_id=1, source_target_pairs={{0,1},{1,0},{2,3},{3,2},{4,5},{5,4},{6,7},{7,6},{8,9},{9,8},{10,11... | collective-permute-start | bytes 786440 | tf_op jit(solution)/shard_map/ppermute | solution.py:271
  24.5 0.5 %collective-permute-start.5 = (f32[512,128]{1,0:T(8,128)S(1)}, f32[512,128]{1,0:T(8,128)S(1)}, u32[]{:S(2)}, u32[]{:S(2)}) collective-permute-start(f32[512,128]{1,0:T(8,128)S(1)} %get-tuple-element.30), channel_id=1, source_target_pairs={{0,17},{1,16},{2,19},{3,18},{4,21},{5,20},{6,23},{7,22},{8,25},{9,... | collective-permute-start | bytes 786440 | tf_op jit(solution)/shard_map/ppermute | solution.py:271
  25.0 0.0 collective-permute-done.10.refs_1_
  25.0 0.4 %shard_map.42 = (f32[256,128]{1,0:T(8,128)S(1)}, f32[256,128]{1,0:T(8,128)S(1)}, f32[256,128]{1,0:T(8,128)S(1)}, f32[256,128]{1,0:T(8,128)S(1)}) custom-call(f32[8,128]{1,0:T(8,128)S(1)} %get-tuple-element.22.refs_0_, f32[1024,128]{1,0:T(8,128)S(1)} %collective-permute-done.10.refs_1_, f32[512,128]{1,0:T(8,128)S(1)} %get-tuple-element.33.refs_1_.refs_2_, ...), custom_call_target="tpu_custom_call" | custom-call | flops 1000000000 | tf_op jit(solution)/shard_map/pallas_call | solution.py:244
  25.4 2.5 %collective-permute-start.11 = (f32[256,128]{1,0:T(8,128)S(1)}, f32[256,128]{1,0:T(8,128)S(1)}, u32[]{:S(2)}, u32[]{:S(2)}) collective-permute-start(f32[256,128]{1,0:T(8,128)S(1)} %get-tuple-element.36), channel_id=1, source_target_pairs={{0,6},{1,7},{2,4},{3,5},{4,2},{5,3},{6,0},{7,1},{8,14},{9,15},{10,... | collective-permute-start | bytes 393224 | tf_op jit(solution)/shard_map/ppermute | solution.py:271
  28.0 0.0 collective-permute-start.12
  28.0 2.8 %collective-permute-done.3.refs_2_.refs_3_ = f32[512,128]{1,0:T(8,128)S(1)} collective-permute-done((f32[512,128]{1,0:T(8,128)S(1)}, f32[512,128]{1,0:T(8,128)S(1)}, u32[]{:S(2)}, u32[]{:S(2)}) %collective-permute-start.3) | collective-permute-done | bytes 262176 | tf_op jit(solution)/shard_map/ppermute | solution.py:271
  30.7 0.0 collective-permute-start.13
  30.7 4.9 %collective-permute-done.4.refs_3_.refs_4_ = f32[512,128]{1,0:T(8,128)S(1)} collective-permute-done((f32[512,128]{1,0:T(8,128)S(1)}, f32[512,128]{1,0:T(8,128)S(1)}, u32[]{:S(2)}, u32[]{:S(2)}) %collective-permute-start.4) | collective-permute-done | bytes 262176 | tf_op jit(solution)/shard_map/ppermute | solution.py:271
  35.7 0.0 collective-permute-done.5.refs_4_.refs_5_
  35.7 0.1 shard_map.40
  35.8 0.1 collective-permute-start.6
  35.9 0.0 collective-permute-done.11.refs_3_
  35.9 2.2 %collective-permute-done.12.refs_4_ = f32[256,128]{1,0:T(8,128)S(1)} collective-permute-done((f32[256,128]{1,0:T(8,128)S(1)}, f32[256,128]{1,0:T(8,128)S(1)}, u32[]{:S(2)}, u32[]{:S(2)}) %collective-permute-start.12) | collective-permute-done | bytes 131104 | tf_op jit(solution)/shard_map/ppermute | solution.py:271
  38.1 0.0 collective-permute-done.13.refs_5_
  38.1 0.4 shard_map.43.refs_8_
  38.5 0.0 collective-permute-done.6.refs_1_
  38.5 1.6 %shard_map.44 = f32[2048,128]{1,0:T(8,128)} custom-call(f32[8,128]{1,0:T(8,128)S(1)} %get-tuple-element.22.refs_0_, f32[1024,128]{1,0:T(8,128)S(1)} %collective-permute-done.6.refs_1_, f32[512,128]{1,0:T(8,128)S(1)} %get-tuple-element.29.refs_1_.refs_2_, f32[512,128]{1,0:T(8,128)S(1)} %collective-permute-done.3.refs_2_.refs_3_, ...), custom_call_target="tpu_custom_call" | custom-call | flops 2000000000 | tf_op jit(solution)/shard_map/pallas_call | solution.py:244
Async XLA Ops:
  0.0 14.5 %copy-start = (f32[4,2,128,128]{3,2,1,0:T(8,128)S(1)}, f32[4,2,128,128]{3,2,1,0:T(8,128)}, u32[]{:S(2)}) copy-start(f32[4,2,128,128]{3,2,1,0:T(8,128)} %refs_0_.1) | copy-start | bytes 1572868
  2.2 10.1 %collective-permute-start.7 = (f32[512,128]{1,0:T(8,128)S(1)}, f32[512,128]{1,0:T(8,128)S(1)}, u32[]{:S(2)}, u32[]{:S(2)}) collective-permute-start(f32[512,128]{1,0:T(8,128)S(1)} %get-tuple-element.33.refs_1_.refs_2_), channel_id=1, source_target_pairs={{0,16},{1,17},{2,18},{3,19},{4,20},{5,21},{6,22},{7,23},{8,24},{9,... | collective-permute-start | bytes 786440 | tf_op jit(solution)/shard_map/ppermute | solution.py:271
  5.2 13.4 %collective-permute-start.8 = (f32[512,128]{1,0:T(8,128)S(1)}, f32[512,128]{1,0:T(8,128)S(1)}, u32[]{:S(2)}, u32[]{:S(2)}) collective-permute-start(f32[512,128]{1,0:T(8,128)S(1)} %get-tuple-element.34), channel_id=1, source_target_pairs={{0,1},{1,0},{2,3},{3,2},{4,5},{5,4},{6,7},{7,6},{8,9},{9,8},{10,11... | collective-permute-start | bytes 786440 | tf_op jit(solution)/shard_map/ppermute | solution.py:271
  6.7 11.9 %collective-permute-start.9 = (f32[512,128]{1,0:T(8,128)S(1)}, f32[512,128]{1,0:T(8,128)S(1)}, u32[]{:S(2)}, u32[]{:S(2)}) collective-permute-start(f32[512,128]{1,0:T(8,128)S(1)} %get-tuple-element.34), channel_id=1, source_target_pairs={{0,17},{1,16},{2,19},{3,18},{4,21},{5,20},{6,23},{7,22},{8,25},{9,... | collective-permute-start | bytes 786440 | tf_op jit(solution)/shard_map/ppermute | solution.py:271
  6.8 12.1 %collective-permute-start = (f32[256,128]{1,0:T(8,128)S(1)}, f32[256,128]{1,0:T(8,128)S(1)}, u32[]{:S(2)}, u32[]{:S(2)}) collective-permute-start(f32[256,128]{1,0:T(8,128)S(1)} %get-tuple-element.26), channel_id=1, source_target_pairs={{0,6},{1,7},{2,4},{3,5},{4,2},{5,3},{6,0},{7,1},{8,14},{9,15},{10,... | collective-permute-start | bytes 393224 | tf_op jit(solution)/shard_map/ppermute | solution.py:271
  10.8 10.2 %collective-permute-start.1 = (f32[256,128]{1,0:T(8,128)S(1)}, f32[256,128]{1,0:T(8,128)S(1)}, u32[]{:S(2)}, u32[]{:S(2)}) collective-permute-start(f32[256,128]{1,0:T(8,128)S(1)} %get-tuple-element.27), channel_id=1, source_target_pairs={{0,4},{1,5},{2,6},{3,7},{4,0},{5,1},{6,2},{7,3},{8,12},{9,13},{10,... | collective-permute-start | bytes 393224 | tf_op jit(solution)/shard_map/ppermute | solution.py:271
  12.4 8.7 %collective-permute-start.2 = (f32[256,128]{1,0:T(8,128)S(1)}, f32[256,128]{1,0:T(8,128)S(1)}, u32[]{:S(2)}, u32[]{:S(2)}) collective-permute-start(f32[256,128]{1,0:T(8,128)S(1)} %get-tuple-element.28), channel_id=1, source_target_pairs={{0,2},{1,3},{2,0},{3,1},{4,6},{5,7},{6,4},{7,5},{8,10},{9,11},{10,... | collective-permute-start | bytes 393224 | tf_op jit(solution)/shard_map/ppermute | solution.py:271
  18.8 6.2 %collective-permute-start.10 = (f32[1024,128]{1,0:T(8,128)S(1)}, f32[1024,128]{1,0:T(8,128)S(1)}, u32[]{:S(2)}, u32[]{:S(2)}) collective-permute-start(f32[1024,128]{1,0:T(8,128)S(1)} %shard_map.41), channel_id=1, source_target_pairs={{0,8},{1,9},{2,10},{3,11},{4,12},{5,13},{6,14},{7,15},{8,0},{9,1},... | collective-permute-start | bytes 1572872 | tf_op jit(solution)/shard_map/ppermute | solution.py:271
  21.4 9.3 %collective-permute-start.3 = (f32[512,128]{1,0:T(8,128)S(1)}, f32[512,128]{1,0:T(8,128)S(1)}, u32[]{:S(2)}, u32[]{:S(2)}) collective-permute-start(f32[512,128]{1,0:T(8,128)S(1)} %get-tuple-element.29.refs_1_.refs_2_), channel_id=1, source_target_pairs={{0,16},{1,17},{2,18},{3,19},{4,20},{5,21},{6,22},{7,23},{8,24},{9,... | collective-permute-start | bytes 786440 | tf_op jit(solution)/shard_map/ppermute | solution.py:271
  23.0 12.7 %collective-permute-start.4 = (f32[512,128]{1,0:T(8,128)S(1)}, f32[512,128]{1,0:T(8,128)S(1)}, u32[]{:S(2)}, u32[]{:S(2)}) collective-permute-start(f32[512,128]{1,0:T(8,128)S(1)} %get-tuple-element.30), channel_id=1, source_target_pairs={{0,1},{1,0},{2,3},{3,2},{4,5},{5,4},{6,7},{7,6},{8,9},{9,8},{10,11... | collective-permute-start | bytes 786440 | tf_op jit(solution)/shard_map/ppermute | solution.py:271
  24.5 11.1 %collective-permute-start.5 = (f32[512,128]{1,0:T(8,128)S(1)}, f32[512,128]{1,0:T(8,128)S(1)}, u32[]{:S(2)}, u32[]{:S(2)}) collective-permute-start(f32[512,128]{1,0:T(8,128)S(1)} %get-tuple-element.30), channel_id=1, source_target_pairs={{0,17},{1,16},{2,19},{3,18},{4,21},{5,20},{6,23},{7,22},{8,25},{9,... | collective-permute-start | bytes 786440 | tf_op jit(solution)/shard_map/ppermute | solution.py:271
  25.4 10.5 %collective-permute-start.11 = (f32[256,128]{1,0:T(8,128)S(1)}, f32[256,128]{1,0:T(8,128)S(1)}, u32[]{:S(2)}, u32[]{:S(2)}) collective-permute-start(f32[256,128]{1,0:T(8,128)S(1)} %get-tuple-element.36), channel_id=1, source_target_pairs={{0,6},{1,7},{2,4},{3,5},{4,2},{5,3},{6,0},{7,1},{8,14},{9,15},{10,... | collective-permute-start | bytes 393224 | tf_op jit(solution)/shard_map/ppermute | solution.py:271
  28.0 10.1 %collective-permute-start.12 = (f32[256,128]{1,0:T(8,128)S(1)}, f32[256,128]{1,0:T(8,128)S(1)}, u32[]{:S(2)}, u32[]{:S(2)}) collective-permute-start(f32[256,128]{1,0:T(8,128)S(1)} %get-tuple-element.37), channel_id=1, source_target_pairs={{0,4},{1,5},{2,6},{3,7},{4,0},{5,1},{6,2},{7,3},{8,12},{9,13},{10,... | collective-permute-start | bytes 393224 | tf_op jit(solution)/shard_map/ppermute | solution.py:271
  30.7 7.3 %collective-permute-start.13 = (f32[256,128]{1,0:T(8,128)S(1)}, f32[256,128]{1,0:T(8,128)S(1)}, u32[]{:S(2)}, u32[]{:S(2)}) collective-permute-start(f32[256,128]{1,0:T(8,128)S(1)} %get-tuple-element.38), channel_id=1, source_target_pairs={{0,2},{1,3},{2,0},{3,1},{4,6},{5,7},{6,4},{7,5},{8,10},{9,11},{10,... | collective-permute-start | bytes 393224 | tf_op jit(solution)/shard_map/ppermute | solution.py:271
  35.8 2.7 %collective-permute-start.6 = (f32[1024,128]{1,0:T(8,128)S(1)}, f32[1024,128]{1,0:T(8,128)S(1)}, u32[]{:S(2)}, u32[]{:S(2)}) collective-permute-start(f32[1024,128]{1,0:T(8,128)S(1)} %shard_map.40), channel_id=1, source_target_pairs={{0,8},{1,9},{2,10},{3,11},{4,12},{5,13},{6,14},{7,15},{8,0},{9,1},... | collective-permute-start | bytes 1572872 | tf_op jit(solution)/shard_map/ppermute | solution.py:271

commit v4 on v3

--- a/solution.py
+++ b/solution.py
@@ -8,7 +8,7 @@
 from jax.sharding import PartitionSpec as P
 
 F32, BF16 = jnp.float32, jnp.bfloat16
-COST = dict(enter=2, prepare=1, mix=1, after_mix=1, between=20, finish=20, last=2)
+COST = dict(enter=2, mix_cores=1, prepare=1, mix=1, after_mix=10, between=1, finish=5, last=2)
 
 
 def split(value):
@@ -33,8 +33,10 @@
     return jnp.concatenate(parts, 0)
 
 
-def turned(pieces):
-    return [pieces[0], *pieces[:0:-1]]
+def turned(pieces, by=1):
+    own, *rest = pieces
+    by %= max(len(rest), 1)
+    return [own, *rest[by:], *rest[:by]]
 
 
 def select(width, block, by_rows):
@@ -59,6 +61,9 @@
     def in_pair(self, part, slot, i):
         return pl.ds((part * self.upper + slot // 2) * self.cell + i * self.block, self.block)
 
+    def in_chunk(self, part, slot, i):
+        return pl.ds(((slot % 2 * 2 + part) * self.upper + slot // 2) * self.cell + i * self.block, self.block)
+
     def in_piece(self, part, slot, i):
         return pl.ds((part * 2 + slot % 2) * self.cell + i * self.block, self.block)
 
@@ -79,7 +84,7 @@
     return columns([rows([read(part, i) for part in range(2)]) for i in range(s.count)])
 
 
-def enter(a, b, which, stride, x, gates, cross, mixing, near, far, *refs):
+def enter(a, b, which, stride, x, gates, cross, mixing, own, *refs):
     *pieces, held, table, elements, sems = refs
     width, mid = a.width, a.mid
     copies = [
@@ -93,7 +98,7 @@
     me = (lax.axis_index("grp") // stride) % 4
     copies[2].wait()
     at = 0
-    for target, source in [(0, 0), (0, 2), (1, 0), (1, 2)]:
+    for target, source in [(0, 0), (0, 2), (1, 0), (1, 2), (0, 0), (0, 1), (2, 0), (2, 1)]:
         for number in entry(elements, which, me ^ target, me ^ source):
             mixing[pl.ds(at, 1), :] = jnp.full((1, width), number, F32)
             at += 1
@@ -117,7 +122,7 @@
     for slot in range(a.inner):
         for part in range(2):
             for i in range(a.count):
-                (near, far)[slot % 2][a.in_pair(part, slot, i), :] = a.cut(state, slot, part, i)
+                own[a.in_chunk(part, slot, i), :] = a.cut(state, slot, part, i)
 
 
 def prepare(width, block, gates, lane_high, lane_low, high, low):
@@ -164,6 +169,16 @@
     return done
 
 
+def mix_cores(own, beside, mixing, near, near_out, far, far_out):
+    for low, outs in enumerate(((near, near_out), (far, far_out))):
+        real, imag = halves(own, low, 2)
+        values = own[real, :], own[imag, :], beside[real, :], beside[imag, :]
+        for first, out in zip((8, 12), outs):
+            real, imag = halves(out)
+            one, two = times(mixing, first, *values[:2]), times(mixing, first + 2, *values[2:])
+            out[real, :], out[imag, :] = one[0] + two[0], one[1] + two[1]
+
+
 def mix(mixing, *refs):
     *pairs, out = refs
     for low, pair in enumerate(mixed(mixing, 4, pairs)):
@@ -178,8 +193,10 @@
     ]
 
 
-def after_mix(s, mixing, got, near, near_got, far, far_got, lane_high, lane_low, *pieces):
-    wide = rows([columns(pair) for pair in sums(mixing, got, (near, near_got, far, far_got))])
+def after_mix(s, near, near_got, far, far_got, lane_high, lane_low, *pieces):
+    real, imag = halves(near)
+    pairs = (near, near_got), (far, far_got)
+    wide = rows([columns([one[at, :] + two[at, :] for at in (real, imag)]) for one, two in pairs])
     wide = dot_split(split(wide), (lane_high[...], lane_low[...]))
     for part in range(2):
         for low in range(2):
@@ -192,7 +209,7 @@
 
 def between(s, lane_high, lane_low, *refs):
     *pieces, near, far = refs
-    pieces = turned(pieces)
+    pieces = turned(pieces, -1)
     half, width = 2 * s.cell, s.width
     wide = rows([columns([p[pl.ds(0, half), :], p[pl.ds(half, half), :]]) for p in pieces])
     wide = dot_split(split(wide), (lane_high[...], lane_low[...]))
@@ -205,35 +222,41 @@
                 ]
 
 
+def third_gate(s, gate, state, out):
+    step = 2 * s.count
+    flat = out.reshape(s.width * step, s.width)
+    state = dot_split(gate, split(state))
+    for i in range(s.count):
+        for part in range(2):
+            flat[pl.ds(2 * i + part, s.width, step), :] = state[
+                part * s.width : (part + 1) * s.width, i * s.width : (i + 1) * s.width
+            ]
+
+
 def finish(s, high, low, *refs):
     *pieces, out = refs
-    pieces = turned(pieces)
+    pieces = turned(pieces, -1)
     state = s.collect(lambda part, slot, i: pieces[slot // 2][s.in_piece(part, slot, i), :])
-    state = dot_split((high[...], low[...]), split(state))
-    for i in range(s.count):
-        out[pl.ds(2 * i * s.width, 2 * s.width), :] = state[:, i * s.width : (i + 1) * s.width]
-
-
-def last(a, b, mixing, got, near, near_got, far, far_got, high, low, done, out):
-    width, step = a.width, 2 * a.mid
-    for i in range(a.count):
-        for part in range(2):
-            out[pl.ds(2 * i + part, width, step), :] = done[pl.ds((2 * i + part) * width, width), :]
+    third_gate(s, (high[...], low[...]), state, out)
+
+
+def last(a, b, mixing, got, near, near_got, far, far_got, high, low, done, out, held, sems):
+    first = pltpu.make_async_copy(done, out.at[:, pl.ds(0, 2 * a.count), :], sems.at[0])
+    first.start()
     pairs = sums(mixing, got, (near, near_got, far, far_got))
 
     def read(part, slot, i):
         at = slot // 2 * b.cell + i * b.block
         return pairs[slot % 2][part][at : at + b.block]
 
-    state = dot_split((high[...], low[...]), split(b.collect(read)))
-    for i in range(b.count):
-        for part in range(2):
-            out[pl.ds(2 * (a.count + i) + part, width, step), :] = state[
-                part * width : (part + 1) * width, i * width : (i + 1) * width
-            ]
-
-
-def call(body, outs, *args, places={}, scratch=(), after=()):
+    third_gate(b, (high[...], low[...]), b.collect(read), held)
+    second = pltpu.make_async_copy(held, out.at[:, pl.ds(2 * a.count, 2 * b.count), :], sems.at[1])
+    second.start()
+    first.wait()
+    second.wait()
+
+
+def call(body, outs, *args, places={}, scratch=(), after=(), out_place=pltpu.VMEM):
     vmem = pl.BlockSpec(memory_space=pltpu.VMEM)
     specs = [pl.BlockSpec(memory_space=places[i]) if i in places else vmem for i in range(len(args))]
     cost = COST[body.func.__name__]
@@ -245,7 +268,7 @@
         kernel,
         out_shape=outs,
         in_specs=specs + [pl.BlockSpec(memory_space=pl.ANY)] * len(after),
-        out_specs=[vmem] * len(outs),
+        out_specs=[pl.BlockSpec(memory_space=out_place)] * len(outs),
         scratch_shapes=scratch,
         compiler_params=pltpu.CompilerParams(vmem_limit_bytes=24 * 2**20),
         cost_estimate=pl.CostEstimate(flops=int(cost * 1e9), bytes_accessed=0, transcendentals=0),
@@ -295,9 +318,9 @@
         return value.reshape(2, local // width, width).transpose(1, 0, 2).reshape(2 * local // width, width)
 
     x = lines(amplitudes)
-    mixing, near_a, far_a, *pieces_b = call(
+    mixing, own_a, *pieces_b = call(
         bind(enter, a, b, which, stride),
-        [array(8), pair(a), pair(a)] + piece(b),
+        [array(16), whole(a)] + piece(b),
         *(pltpu.with_memory_space_constraint(ref, pltpu.HBM) for ref in (x, layer_gates, cross_gates)),
         places={i: pltpu.HBM for i in range(3)},
         scratch=[
@@ -307,12 +330,14 @@
             pltpu.SemaphoreType.DMA((3,)),
         ],
     )
-    *lane, third_high, third_low = call(bind(prepare, width, a.block), [table] * 4, layer_gates)
-    third = third_high, third_low
 
     def swap_upper(pieces):
         moved = {k: send(pieces[k], 0, 2 * k) for k in reversed(range(1, len(pieces)))}
         return [pieces[0]] + [moved[k] for k in range(1, len(pieces))]
+
+    def cross_first(own, s):
+        near, near_out, far, far_out = call(bind(mix_cores), [pair(s)] * 4, own, send(own, stride, 0), mixing)
+        return near, send(near_out, 2 * stride, 0), send(far, 0, 1), send(far_out, 2 * stride, 1)
 
     def cross(near, far, s):
         pairs = near, send(near, 2 * stride, 0), send(far, 0, 1), send(far, 2 * stride, 1)
@@ -320,13 +345,24 @@
         return mixing, send(other, stride, 0), *pairs
 
     pieces_b = swap_upper(pieces_b)
-    sums_a = cross(near_a, far_a, a)
+    sums_a = cross_first(own_a, a)
+    *lane, third_high, third_low = call(bind(prepare, width, a.block), [table] * 4, layer_gates, after=sums_a[:1])
+    third = third_high, third_low
     near_b, far_b = call(bind(between, b), [pair(b)] * 2, *lane, *turned(pieces_b))
     pieces_a = call(bind(after_mix, a), piece(a), *sums_a, *lane)
     pieces_a = swap_upper(pieces_a)
     sums_b = cross(near_b, far_b, b)
-    (done,) = call(bind(finish, a), [whole(a)], *third, *turned(pieces_a))
-    (out,) = call(bind(last, a, b), [jax.ShapeDtypeStruct(x.shape, F32)], *sums_b, *third, done)
+    tiles = lambda s: jax.ShapeDtypeStruct((width, 2 * s.count, width), F32)
+    (done,) = call(bind(finish, a), [tiles(a)], *third, *turned(pieces_a))
+    (out,) = call(
+        bind(last, a, b),
+        [jax.ShapeDtypeStruct((width, 2 * mid, width), F32)],
+        *sums_b,
+        *third,
+        done,
+        scratch=[pltpu.VMEM(tiles(b).shape, F32), pltpu.SemaphoreType.DMA((2,))],
+        out_place=pltpu.HBM,
+    )
     return out.reshape(local // width, 2, width).transpose(1, 0, 2).reshape(2, local)
 
 

time: 40.2 us -> 39.1 us (0.973)
  waiting for transfers between devices: 17.2 us -> 13.5 us
  starting transfers between devices: 17 us -> 19.7 us
    ppermute x14, waiting for transfers between devices: 17.2 us -> 13.5 us  [send(): return lax.ppermute(value, ('grp', 'qb'), perm)]
    ppermute x14, starting transfers between devices: 17 us -> 19.7 us  [send(): return lax.ppermute(value, ('grp', 'qb'), perm)]
  transfers between devices with their start and end apart: 14 -> 14, of which waited for: 6 -> 8; matrix products, arithmetic and copies ran while one was open for 0% -> 0% of each run, Pallas kernels for 5% -> 5%
where the time goes in v4:
time: 39.1 us; the launch traced here: 38.9 us
  starting transfers between devices  19.7 us (50%)
  waiting for transfers between devices  13.5 us (35%)
  Pallas kernels  5.62 us (14%)
    ppermute x14, starting transfers between devices, send(): return lax.ppermute(value, ('grp', 'qb'), perm)  19.7 us
    ppermute x14, waiting for transfers between devices, send(): return lax.ppermute(value, ('grp', 'qb'), perm)  13.5 us
    pallas_call x8, Pallas kernels, call(): pl.pallas_call(kernel, out_shape=outs, in_specs=specs + [pl.BlockSpec(mem...  5.62 us
  transfers between devices with their start and end apart: 14, of which 8 were waited for; matrix products, arithmetic and copies ran while one was open for 0% of the time, Pallas kernels for 5%

profile of v4, /device:TPU:0, one launch (start us, length us, event | category | flops | bytes accessed | tf_op | source)
XLA Modules:
  0.0 38.9 jit_solution(1867963515289295600)
XLA Ops:
  0.0 2.2 %shard_map.37 = (f32[16,128]{1,0:T(8,128)S(1)}, f32[1024,128]{1,0:T(8,128)S(1)}, f32[256,128]{1,0:T(8,128)S(1)}, f32[256,128]{1,0:T(8,128)S(1)}, f32[256,128]{1,0:T(8,128)S(1)}, /*index=5*/f32[256,128]{1,0:T(8,128)S(1)}) custom-call(f32[2048,128]{1,0:T(8,128)} %bitcast.10, f32[4,2,128,128]{3,2,1,0:T(8,128)} %refs_0_.1, f32[2,2,4,4]{3,2,1,0:T(4,128)} %refs_2_.1), custom_call_target="tpu_custom_call" | custom-call | flops 2000000000 | tf_op jit(solution)/shard_map/pallas_call | solution.py:267
  2.2 0.5 %collective-permute-start = (f32[1024,128]{1,0:T(8,128)S(1)}, f32[1024,128]{1,0:T(8,128)S(1)}, u32[]{:S(2)}, u32[]{:S(2)}) collective-permute-start(f32[1024,128]{1,0:T(8,128)S(1)} %get-tuple-element.26.refs_0_), channel_id=1, source_target_pairs={{0,8},{1,9},{2,10},{3,11},{4,12},{5,13},{6,14},{7,15},{8,0},{9,1},... | collective-permute-start | bytes 1572872 | tf_op jit(solution)/shard_map/ppermute | solution.py:294
  2.7 3.7 %collective-permute-start.1 = (f32[256,128]{1,0:T(8,128)S(1)}, f32[256,128]{1,0:T(8,128)S(1)}, u32[]{:S(2)}, u32[]{:S(2)}) collective-permute-start(f32[256,128]{1,0:T(8,128)S(1)} %get-tuple-element.31), channel_id=1, source_target_pairs={{0,4},{1,5},{2,6},{3,7},{4,0},{5,1},{6,2},{7,3},{8,12},{9,13},{10,... | collective-permute-start | bytes 393224 | tf_op jit(solution)/shard_map/ppermute | solution.py:294
  6.4 0.0 collective-permute-done.refs_1_
  6.4 0.0 copy-start
  6.4 0.3 shard_map.38
  6.7 1.6 %collective-permute-start.8 = (f32[512,128]{1,0:T(8,128)S(1)}, f32[512,128]{1,0:T(8,128)S(1)}, u32[]{:S(2)}, u32[]{:S(2)}) collective-permute-start(f32[512,128]{1,0:T(8,128)S(1)} %get-tuple-element.38), channel_id=1, source_target_pairs={{0,16},{1,17},{2,18},{3,19},{4,20},{5,21},{6,22},{7,23},{8,24},{9,... | collective-permute-start | bytes 786440 | tf_op jit(solution)/shard_map/ppermute | solution.py:294
  8.2 1.5 %collective-permute-start.9 = (f32[512,128]{1,0:T(8,128)S(1)}, f32[512,128]{1,0:T(8,128)S(1)}, u32[]{:S(2)}, u32[]{:S(2)}) collective-permute-start(f32[512,128]{1,0:T(8,128)S(1)} %get-tuple-element.39), channel_id=1, source_target_pairs={{0,1},{1,0},{2,3},{3,2},{4,5},{5,4},{6,7},{7,6},{8,9},{9,8},{10,11... | collective-permute-start | bytes 786440 | tf_op jit(solution)/shard_map/ppermute | solution.py:294
  9.8 0.5 %collective-permute-start.10 = (f32[512,128]{1,0:T(8,128)S(1)}, f32[512,128]{1,0:T(8,128)S(1)}, u32[]{:S(2)}, u32[]{:S(2)}) collective-permute-start(f32[512,128]{1,0:T(8,128)S(1)} %get-tuple-element.40), channel_id=1, source_target_pairs={{0,17},{1,16},{2,19},{3,18},{4,21},{5,20},{6,23},{7,22},{8,25},{9,... | collective-permute-start | bytes 786440 | tf_op jit(solution)/shard_map/ppermute | solution.py:294
  10.2 2.8 %collective-permute-start.2 = (f32[256,128]{1,0:T(8,128)S(1)}, f32[256,128]{1,0:T(8,128)S(1)}, u32[]{:S(2)}, u32[]{:S(2)}) collective-permute-start(f32[256,128]{1,0:T(8,128)S(1)} %get-tuple-element.32), channel_id=1, source_target_pairs={{0,6},{1,7},{2,4},{3,5},{4,2},{5,3},{6,0},{7,1},{8,14},{9,15},{10,... | collective-permute-start | bytes 393224 | tf_op jit(solution)/shard_map/ppermute | solution.py:294
  13.1 0.3 collective-permute-done.1.refs_3_
  13.3 0.8 %collective-permute-start.3 = (f32[256,128]{1,0:T(8,128)S(1)}, f32[256,128]{1,0:T(8,128)S(1)}, u32[]{:S(2)}, u32[]{:S(2)}) collective-permute-start(f32[256,128]{1,0:T(8,128)S(1)} %get-tuple-element.33), channel_id=1, source_target_pairs={{0,2},{1,3},{2,0},{3,1},{4,6},{5,7},{6,4},{7,5},{8,10},{9,11},{10,... | collective-permute-start | bytes 393224 | tf_op jit(solution)/shard_map/ppermute | solution.py:294
  14.1 0.0 copy-done
  14.1 0.5 %shard_map.39 = (bf16[256,256]{1,0:T(8,128)(2,1)S(1)}, bf16[256,256]{1,0:T(8,128)(2,1)S(1)}, bf16[256,256]{1,0:T(8,128)(2,1)S(1)}, bf16[256,256]{1,0:T(8,128)(2,1)S(1)}) custom-call(f32[4,2,128,128]{3,2,1,0:T(8,128)S(1)} %copy-done, f32[512,128]{1,0:T(8,128)S(1)} %get-tuple-element.27.refs_1_.refs_0_), custom_call_target="tpu_custom_call" | custom-call | flops 1000000000 | tf_op jit(solution)/shard_map/pallas_call | solution.py:267
  14.6 2.5 %collective-permute-done.2.refs_4_ = f32[256,128]{1,0:T(8,128)S(1)} collective-permute-done((f32[256,128]{1,0:T(8,128)S(1)}, f32[256,128]{1,0:T(8,128)S(1)}, u32[]{:S(2)}, u32[]{:S(2)}) %collective-permute-start.2) | collective-permute-done | bytes 131104 | tf_op jit(solution)/shard_map/ppermute | solution.py:294
  17.1 2.7 %collective-permute-done.3.refs_5_ = f32[256,128]{1,0:T(8,128)S(1)} collective-permute-done((f32[256,128]{1,0:T(8,128)S(1)}, f32[256,128]{1,0:T(8,128)S(1)}, u32[]{:S(2)}, u32[]{:S(2)}) %collective-permute-start.3) | collective-permute-done | bytes 131104 | tf_op jit(solution)/shard_map/ppermute | solution.py:294
  19.8 0.4 shard_map.40
  20.2 2.5 %collective-permute-start.6 = (f32[512,128]{1,0:T(8,128)S(1)}, f32[512,128]{1,0:T(8,128)S(1)}, u32[]{:S(2)}, u32[]{:S(2)}) collective-permute-start(f32[512,128]{1,0:T(8,128)S(1)} %get-tuple-element.35), channel_id=1, source_target_pairs={{0,17},{1,16},{2,19},{3,18},{4,21},{5,20},{6,23},{7,22},{8,25},{9,... | collective-permute-start | bytes 786440 | tf_op jit(solution)/shard_map/ppermute | solution.py:294
  22.7 0.5 %collective-permute-start.5 = (f32[512,128]{1,0:T(8,128)S(1)}, f32[512,128]{1,0:T(8,128)S(1)}, u32[]{:S(2)}, u32[]{:S(2)}) collective-permute-start(f32[512,128]{1,0:T(8,128)S(1)} %get-tuple-element.35), channel_id=1, source_target_pairs={{0,1},{1,0},{2,3},{3,2},{4,5},{5,4},{6,7},{7,6},{8,9},{9,8},{10,11... | collective-permute-start | bytes 786440 | tf_op jit(solution)/shard_map/ppermute | solution.py:294
  23.2 0.0 collective-permute-done.8.refs_1_
  23.2 0.5 %collective-permute-start.4 = (f32[512,128]{1,0:T(8,128)S(1)}, f32[512,128]{1,0:T(8,128)S(1)}, u32[]{:S(2)}, u32[]{:S(2)}) collective-permute-start(f32[512,128]{1,0:T(8,128)S(1)} %get-tuple-element.34.refs_1_.refs_2_), channel_id=1, source_target_pairs={{0,16},{1,17},{2,18},{3,19},{4,20},{5,21},{6,22},{7,23},{8,24},{9,... | collective-permute-start | bytes 786440 | tf_op jit(solution)/shard_map/ppermute | solution.py:294
  23.7 0.0 collective-permute-done.9.refs_2_
  23.7 0.0 collective-permute-done.10.refs_3_
  23.7 0.4 shard_map.42
  24.1 2.0 %collective-permute-start.11 = (f32[256,128]{1,0:T(8,128)S(1)}, f32[256,128]{1,0:T(8,128)S(1)}, u32[]{:S(2)}, u32[]{:S(2)}) collective-permute-start(f32[256,128]{1,0:T(8,128)S(1)} %get-tuple-element.42), channel_id=1, source_target_pairs={{0,4},{1,5},{2,6},{3,7},{4,0},{5,1},{6,2},{7,3},{8,12},{9,13},{10,... | collective-permute-start | bytes 393224 | tf_op jit(solution)/shard_map/ppermute | solution.py:294
  26.2 1.5 %collective-permute-start.12 = (f32[256,128]{1,0:T(8,128)S(1)}, f32[256,128]{1,0:T(8,128)S(1)}, u32[]{:S(2)}, u32[]{:S(2)}) collective-permute-start(f32[256,128]{1,0:T(8,128)S(1)} %get-tuple-element.43), channel_id=1, source_target_pairs={{0,6},{1,7},{2,4},{3,5},{4,2},{5,3},{6,0},{7,1},{8,14},{9,15},{10,... | collective-permute-start | bytes 393224 | tf_op jit(solution)/shard_map/ppermute | solution.py:294
  27.7 2.6 %collective-permute-done.6.refs_4_.refs_5_ = f32[512,128]{1,0:T(8,128)S(1)} collective-permute-done((f32[512,128]{1,0:T(8,128)S(1)}, f32[512,128]{1,0:T(8,128)S(1)}, u32[]{:S(2)}, u32[]{:S(2)}) %collective-permute-start.6) | collective-permute-done | bytes 262176 | tf_op jit(solution)/shard_map/ppermute | solution.py:294
  30.4 1.1 %collective-permute-start.13 = (f32[256,128]{1,0:T(8,128)S(1)}, f32[256,128]{1,0:T(8,128)S(1)}, u32[]{:S(2)}, u32[]{:S(2)}) collective-permute-start(f32[256,128]{1,0:T(8,128)S(1)} %get-tuple-element.44), channel_id=1, source_target_pairs={{0,2},{1,3},{2,0},{3,1},{4,6},{5,7},{6,4},{7,5},{8,10},{9,11},{10,... | collective-permute-start | bytes 393224 | tf_op jit(solution)/shard_map/ppermute | solution.py:294
  31.4 3.6 %collective-permute-done.5.refs_3_.refs_4_ = f32[512,128]{1,0:T(8,128)S(1)} collective-permute-done((f32[512,128]{1,0:T(8,128)S(1)}, f32[512,128]{1,0:T(8,128)S(1)}, u32[]{:S(2)}, u32[]{:S(2)}) %collective-permute-start.5) | collective-permute-done | bytes 262176 | tf_op jit(solution)/shard_map/ppermute | solution.py:294
  35.0 0.1 collective-permute-done.4.refs_2_.refs_3_
  35.1 0.1 shard_map.41
  35.2 0.1 collective-permute-start.7
  35.3 0.5 %collective-permute-done.11.refs_3_ = f32[256,128]{1,0:T(8,128)S(1)} collective-permute-done((f32[256,128]{1,0:T(8,128)S(1)}, f32[256,128]{1,0:T(8,128)S(1)}, u32[]{:S(2)}, u32[]{:S(2)}) %collective-permute-start.11) | collective-permute-done | bytes 131104 | tf_op jit(solution)/shard_map/ppermute | solution.py:294
  35.8 0.0 collective-permute-done.12.refs_4_
  35.8 1.3 %collective-permute-done.13.refs_5_ = f32[256,128]{1,0:T(8,128)S(1)} collective-permute-done((f32[256,128]{1,0:T(8,128)S(1)}, f32[256,128]{1,0:T(8,128)S(1)}, u32[]{:S(2)}, u32[]{:S(2)}) %collective-permute-start.13) | collective-permute-done | bytes 131104 | tf_op jit(solution)/shard_map/ppermute | solution.py:294
  37.1 0.4 %shard_map.43.refs_8_ = f32[128,8,128]{2,1,0:T(8,128)S(1)} custom-call(bf16[256,256]{1,0:T(8,128)(2,1)S(1)} %get-tuple-element.36.refs_0_.refs_6_, bf16[256,256]{1,0:T(8,128)(2,1)S(1)} %get-tuple-element.37.refs_1_.refs_7_, f32[256,128]{1,0:T(8,128)S(1)} %get-tuple-element.41.refs_2_, f32[256,128]{1,0:T(8,128)S(1)} %collective-permute-done.11.refs_3_, ...), custom_call_target="tpu_custom_call" | custom-call | flops 5000000000 | tf_op jit(solution)/shard_map/pallas_call | solution.py:267
  37.5 0.0 collective-permute-done.7.refs_1_
  37.5 1.3 %shard_map.44 = f32[128,16,128]{2,1,0:T(8,128)} custom-call(f32[16,128]{1,0:T(8,128)S(1)} %get-tuple-element.25.refs_2_.refs_0_, f32[1024,128]{1,0:T(8,128)S(1)} %collective-permute-done.7.refs_1_, f32[512,128]{1,0:T(8,128)S(1)} %get-tuple-element.34.refs_1_.refs_2_, f32[512,128]{1,0:T(8,128)S(1)} %collective-permute-done.4.refs_2_.refs_3_, ...), custom_call_target="tpu_custom_call" | custom-call | flops 2000000000 | tf_op jit(solution)/shard_map/pallas_call | solution.py:267
Async XLA Ops:
  2.2 4.2 %collective-permute-start = (f32[1024,128]{1,0:T(8,128)S(1)}, f32[1024,128]{1,0:T(8,128)S(1)}, u32[]{:S(2)}, u32[]{:S(2)}) collective-permute-start(f32[1024,128]{1,0:T(8,128)S(1)} %get-tuple-element.26.refs_0_), channel_id=1, source_target_pairs={{0,8},{1,9},{2,10},{3,11},{4,12},{5,13},{6,14},{7,15},{8,0},{9,1},... | collective-permute-start | bytes 1572872 | tf_op jit(solution)/shard_map/ppermute | solution.py:294
  2.7 10.6 %collective-permute-start.1 = (f32[256,128]{1,0:T(8,128)S(1)}, f32[256,128]{1,0:T(8,128)S(1)}, u32[]{:S(2)}, u32[]{:S(2)}) collective-permute-start(f32[256,128]{1,0:T(8,128)S(1)} %get-tuple-element.31), channel_id=1, source_target_pairs={{0,4},{1,5},{2,6},{3,7},{4,0},{5,1},{6,2},{7,3},{8,12},{9,13},{10,... | collective-permute-start | bytes 393224 | tf_op jit(solution)/shard_map/ppermute | solution.py:294
  6.4 7.8 %copy-start = (f32[4,2,128,128]{3,2,1,0:T(8,128)S(1)}, f32[4,2,128,128]{3,2,1,0:T(8,128)}, u32[]{:S(2)}) copy-start(f32[4,2,128,128]{3,2,1,0:T(8,128)} %refs_0_.1) | copy-start | bytes 1572868
  6.7 16.5 %collective-permute-start.8 = (f32[512,128]{1,0:T(8,128)S(1)}, f32[512,128]{1,0:T(8,128)S(1)}, u32[]{:S(2)}, u32[]{:S(2)}) collective-permute-start(f32[512,128]{1,0:T(8,128)S(1)} %get-tuple-element.38), channel_id=1, source_target_pairs={{0,16},{1,17},{2,18},{3,19},{4,20},{5,21},{6,22},{7,23},{8,24},{9,... | collective-permute-start | bytes 786440 | tf_op jit(solution)/shard_map/ppermute | solution.py:294
  8.2 15.5 %collective-permute-start.9 = (f32[512,128]{1,0:T(8,128)S(1)}, f32[512,128]{1,0:T(8,128)S(1)}, u32[]{:S(2)}, u32[]{:S(2)}) collective-permute-start(f32[512,128]{1,0:T(8,128)S(1)} %get-tuple-element.39), channel_id=1, source_target_pairs={{0,1},{1,0},{2,3},{3,2},{4,5},{5,4},{6,7},{7,6},{8,9},{9,8},{10,11... | collective-permute-start | bytes 786440 | tf_op jit(solution)/shard_map/ppermute | solution.py:294
  9.8 14.0 %collective-permute-start.10 = (f32[512,128]{1,0:T(8,128)S(1)}, f32[512,128]{1,0:T(8,128)S(1)}, u32[]{:S(2)}, u32[]{:S(2)}) collective-permute-start(f32[512,128]{1,0:T(8,128)S(1)} %get-tuple-element.40), channel_id=1, source_target_pairs={{0,17},{1,16},{2,19},{3,18},{4,21},{5,20},{6,23},{7,22},{8,25},{9,... | collective-permute-start | bytes 786440 | tf_op jit(solution)/shard_map/ppermute | solution.py:294
  10.2 6.9 %collective-permute-start.2 = (f32[256,128]{1,0:T(8,128)S(1)}, f32[256,128]{1,0:T(8,128)S(1)}, u32[]{:S(2)}, u32[]{:S(2)}) collective-permute-start(f32[256,128]{1,0:T(8,128)S(1)} %get-tuple-element.32), channel_id=1, source_target_pairs={{0,6},{1,7},{2,4},{3,5},{4,2},{5,3},{6,0},{7,1},{8,14},{9,15},{10,... | collective-permute-start | bytes 393224 | tf_op jit(solution)/shard_map/ppermute | solution.py:294
  13.3 6.5 %collective-permute-start.3 = (f32[256,128]{1,0:T(8,128)S(1)}, f32[256,128]{1,0:T(8,128)S(1)}, u32[]{:S(2)}, u32[]{:S(2)}) collective-permute-start(f32[256,128]{1,0:T(8,128)S(1)} %get-tuple-element.33), channel_id=1, source_target_pairs={{0,2},{1,3},{2,0},{3,1},{4,6},{5,7},{6,4},{7,5},{8,10},{9,11},{10,... | collective-permute-start | bytes 393224 | tf_op jit(solution)/shard_map/ppermute | solution.py:294
  20.2 10.2 %collective-permute-start.6 = (f32[512,128]{1,0:T(8,128)S(1)}, f32[512,128]{1,0:T(8,128)S(1)}, u32[]{:S(2)}, u32[]{:S(2)}) collective-permute-start(f32[512,128]{1,0:T(8,128)S(1)} %get-tuple-element.35), channel_id=1, source_target_pairs={{0,17},{1,16},{2,19},{3,18},{4,21},{5,20},{6,23},{7,22},{8,25},{9,... | collective-permute-start | bytes 786440 | tf_op jit(solution)/shard_map/ppermute | solution.py:294
  22.7 12.3 %collective-permute-start.5 = (f32[512,128]{1,0:T(8,128)S(1)}, f32[512,128]{1,0:T(8,128)S(1)}, u32[]{:S(2)}, u32[]{:S(2)}) collective-permute-start(f32[512,128]{1,0:T(8,128)S(1)} %get-tuple-element.35), channel_id=1, source_target_pairs={{0,1},{1,0},{2,3},{3,2},{4,5},{5,4},{6,7},{7,6},{8,9},{9,8},{10,11... | collective-permute-start | bytes 786440 | tf_op jit(solution)/shard_map/ppermute | solution.py:294
  23.2 11.9 %collective-permute-start.4 = (f32[512,128]{1,0:T(8,128)S(1)}, f32[512,128]{1,0:T(8,128)S(1)}, u32[]{:S(2)}, u32[]{:S(2)}) collective-permute-start(f32[512,128]{1,0:T(8,128)S(1)} %get-tuple-element.34.refs_1_.refs_2_), channel_id=1, source_target_pairs={{0,16},{1,17},{2,18},{3,19},{4,20},{5,21},{6,22},{7,23},{8,24},{9,... | collective-permute-start | bytes 786440 | tf_op jit(solution)/shard_map/ppermute | solution.py:294
  24.1 11.6 %collective-permute-start.11 = (f32[256,128]{1,0:T(8,128)S(1)}, f32[256,128]{1,0:T(8,128)S(1)}, u32[]{:S(2)}, u32[]{:S(2)}) collective-permute-start(f32[256,128]{1,0:T(8,128)S(1)} %get-tuple-element.42), channel_id=1, source_target_pairs={{0,4},{1,5},{2,6},{3,7},{4,0},{5,1},{6,2},{7,3},{8,12},{9,13},{10,... | collective-permute-start | bytes 393224 | tf_op jit(solution)/shard_map/ppermute | solution.py:294
  26.2 9.6 %collective-permute-start.12 = (f32[256,128]{1,0:T(8,128)S(1)}, f32[256,128]{1,0:T(8,128)S(1)}, u32[]{:S(2)}, u32[]{:S(2)}) collective-permute-start(f32[256,128]{1,0:T(8,128)S(1)} %get-tuple-element.43), channel_id=1, source_target_pairs={{0,6},{1,7},{2,4},{3,5},{4,2},{5,3},{6,0},{7,1},{8,14},{9,15},{10,... | collective-permute-start | bytes 393224 | tf_op jit(solution)/shard_map/ppermute | solution.py:294
  30.4 6.7 %collective-permute-start.13 = (f32[256,128]{1,0:T(8,128)S(1)}, f32[256,128]{1,0:T(8,128)S(1)}, u32[]{:S(2)}, u32[]{:S(2)}) collective-permute-start(f32[256,128]{1,0:T(8,128)S(1)} %get-tuple-element.44), channel_id=1, source_target_pairs={{0,2},{1,3},{2,0},{3,1},{4,6},{5,7},{6,4},{7,5},{8,10},{9,11},{10,... | collective-permute-start | bytes 393224 | tf_op jit(solution)/shard_map/ppermute | solution.py:294
  35.2 2.3 %collective-permute-start.7 = (f32[1024,128]{1,0:T(8,128)S(1)}, f32[1024,128]{1,0:T(8,128)S(1)}, u32[]{:S(2)}, u32[]{:S(2)}) collective-permute-start(f32[1024,128]{1,0:T(8,128)S(1)} %shard_map.41), channel_id=1, source_target_pairs={{0,8},{1,9},{2,10},{3,11},{4,12},{5,13},{6,14},{7,15},{8,0},{9,1},... | collective-permute-start | bytes 1572872 | tf_op jit(solution)/shard_map/ppermute | solution.py:294

commit v5 on v4

--- a/solution.py
+++ b/solution.py
@@ -37,6 +37,10 @@
     own, *rest = pieces
     by %= max(len(rest), 1)
     return [own, *rest[by:], *rest[:by]]
+
+
+def backwards(pieces):
+    return [pieces[0], *pieces[:0:-1]]
 
 
 def select(width, block, by_rows):
@@ -209,7 +213,7 @@
 
 def between(s, lane_high, lane_low, *refs):
     *pieces, near, far = refs
-    pieces = turned(pieces, -1)
+    pieces = backwards(pieces)
     half, width = 2 * s.cell, s.width
     wide = rows([columns([p[pl.ds(0, half), :], p[pl.ds(half, half), :]]) for p in pieces])
     wide = dot_split(split(wide), (lane_high[...], lane_low[...]))
@@ -348,7 +352,7 @@
     sums_a = cross_first(own_a, a)
     *lane, third_high, third_low = call(bind(prepare, width, a.block), [table] * 4, layer_gates, after=sums_a[:1])
     third = third_high, third_low
-    near_b, far_b = call(bind(between, b), [pair(b)] * 2, *lane, *turned(pieces_b))
+    near_b, far_b = call(bind(between, b), [pair(b)] * 2, *lane, *backwards(pieces_b))
     pieces_a = call(bind(after_mix, a), piece(a), *sums_a, *lane)
     pieces_a = swap_upper(pieces_a)
     sums_b = cross(near_b, far_b, b)

time: 39.1 us -> 38.1 us (0.974)
  waiting for transfers between devices: 13.5 us -> 12.9 us
  starting transfers between devices: 19.7 us -> 19.3 us
    ppermute x14, waiting for transfers between devices: 13.5 us -> 12.9 us  [send(): return lax.ppermute(value, ('grp', 'qb'), perm)]
  transfers between devices with their start and end apart: 14 -> 14, of which waited for: 8 -> 7; matrix products, arithmetic and copies ran while one was open for 0% -> 0% of each run, Pallas kernels for 5% -> 6%
where the time goes in v5:
time: 38.1 us; the launch traced here: 37.9 us
  starting transfers between devices  19.3 us (51%)
  waiting for transfers between devices  12.9 us (34%)
  Pallas kernels  5.64 us (15%)
    ppermute x14, starting transfers between devices, send(): return lax.ppermute(value, ('grp', 'qb'), perm)  19.3 us
    ppermute x14, waiting for transfers between devices, send(): return lax.ppermute(value, ('grp', 'qb'), perm)  12.9 us
    pallas_call x8, Pallas kernels, call(): pl.pallas_call(kernel, out_shape=outs, in_specs=specs + [pl.BlockSpec(mem...  5.64 us
  transfers between devices with their start and end apart: 14, of which 7 were waited for; matrix products, arithmetic and copies ran while one was open for 0% of the time, Pallas kernels for 6%

profile of v5, /device:TPU:0, one launch (start us, length us, event | category | flops | bytes accessed | tf_op | source)
XLA Modules:
  0.0 37.9 jit_solution(12169610780764920877)
XLA Ops:
  0.0 2.2 %shard_map.37 = (f32[16,128]{1,0:T(8,128)S(1)}, f32[1024,128]{1,0:T(8,128)S(1)}, f32[256,128]{1,0:T(8,128)S(1)}, f32[256,128]{1,0:T(8,128)S(1)}, f32[256,128]{1,0:T(8,128)S(1)}, /*index=5*/f32[256,128]{1,0:T(8,128)S(1)}) custom-call(f32[2048,128]{1,0:T(8,128)} %bitcast.10, f32[4,2,128,128]{3,2,1,0:T(8,128)} %refs_0_.1, f32[2,2,4,4]{3,2,1,0:T(4,128)} %refs_2_.1), custom_call_target="tpu_custom_call" | custom-call | flops 2000000000 | tf_op jit(solution)/shard_map/pallas_call | solution.py:271
  2.2 0.5 %collective-permute-start = (f32[1024,128]{1,0:T(8,128)S(1)}, f32[1024,128]{1,0:T(8,128)S(1)}, u32[]{:S(2)}, u32[]{:S(2)}) collective-permute-start(f32[1024,128]{1,0:T(8,128)S(1)} %get-tuple-element.26.refs_0_), channel_id=1, source_target_pairs={{0,8},{1,9},{2,10},{3,11},{4,12},{5,13},{6,14},{7,15},{8,0},{9,1},... | collective-permute-start | bytes 1572872 | tf_op jit(solution)/shard_map/ppermute | solution.py:298
  2.7 4.7 %collective-permute-start.1 = (f32[256,128]{1,0:T(8,128)S(1)}, f32[256,128]{1,0:T(8,128)S(1)}, u32[]{:S(2)}, u32[]{:S(2)}) collective-permute-start(f32[256,128]{1,0:T(8,128)S(1)} %get-tuple-element.31), channel_id=1, source_target_pairs={{0,6},{1,7},{2,4},{3,5},{4,2},{5,3},{6,0},{7,1},{8,14},{9,15},{10,... | collective-permute-start | bytes 393224 | tf_op jit(solution)/shard_map/ppermute | solution.py:298
  7.4 0.0 collective-permute-done.refs_1_
  7.4 0.0 copy-start
  7.4 0.3 shard_map.38
  7.7 1.5 %collective-permute-start.8 = (f32[512,128]{1,0:T(8,128)S(1)}, f32[512,128]{1,0:T(8,128)S(1)}, u32[]{:S(2)}, u32[]{:S(2)}) collective-permute-start(f32[512,128]{1,0:T(8,128)S(1)} %get-tuple-element.38), channel_id=1, source_target_pairs={{0,16},{1,17},{2,18},{3,19},{4,20},{5,21},{6,22},{7,23},{8,24},{9,... | collective-permute-start | bytes 786440 | tf_op jit(solution)/shard_map/ppermute | solution.py:298
  9.2 1.5 %collective-permute-start.9 = (f32[512,128]{1,0:T(8,128)S(1)}, f32[512,128]{1,0:T(8,128)S(1)}, u32[]{:S(2)}, u32[]{:S(2)}) collective-permute-start(f32[512,128]{1,0:T(8,128)S(1)} %get-tuple-element.39), channel_id=1, source_target_pairs={{0,1},{1,0},{2,3},{3,2},{4,5},{5,4},{6,7},{7,6},{8,9},{9,8},{10,11... | collective-permute-start | bytes 786440 | tf_op jit(solution)/shard_map/ppermute | solution.py:298
  10.8 0.5 %collective-permute-start.10 = (f32[512,128]{1,0:T(8,128)S(1)}, f32[512,128]{1,0:T(8,128)S(1)}, u32[]{:S(2)}, u32[]{:S(2)}) collective-permute-start(f32[512,128]{1,0:T(8,128)S(1)} %get-tuple-element.40), channel_id=1, source_target_pairs={{0,17},{1,16},{2,19},{3,18},{4,21},{5,20},{6,23},{7,22},{8,25},{9,... | collective-permute-start | bytes 786440 | tf_op jit(solution)/shard_map/ppermute | solution.py:298
  11.2 0.8 %collective-permute-start.2 = (f32[256,128]{1,0:T(8,128)S(1)}, f32[256,128]{1,0:T(8,128)S(1)}, u32[]{:S(2)}, u32[]{:S(2)}) collective-permute-start(f32[256,128]{1,0:T(8,128)S(1)} %get-tuple-element.32), channel_id=1, source_target_pairs={{0,4},{1,5},{2,6},{3,7},{4,0},{5,1},{6,2},{7,3},{8,12},{9,13},{10,... | collective-permute-start | bytes 393224 | tf_op jit(solution)/shard_map/ppermute | solution.py:298
  12.0 0.0 collective-permute-done.1.refs_3_
  12.0 3.4 %collective-permute-start.3 = (f32[256,128]{1,0:T(8,128)S(1)}, f32[256,128]{1,0:T(8,128)S(1)}, u32[]{:S(2)}, u32[]{:S(2)}) collective-permute-start(f32[256,128]{1,0:T(8,128)S(1)} %get-tuple-element.33), channel_id=1, source_target_pairs={{0,2},{1,3},{2,0},{3,1},{4,6},{5,7},{6,4},{7,5},{8,10},{9,11},{10,... | collective-permute-start | bytes 393224 | tf_op jit(solution)/shard_map/ppermute | solution.py:298
  15.5 0.0 copy-done
  15.5 0.5 %shard_map.39 = (bf16[256,256]{1,0:T(8,128)(2,1)S(1)}, bf16[256,256]{1,0:T(8,128)(2,1)S(1)}, bf16[256,256]{1,0:T(8,128)(2,1)S(1)}, bf16[256,256]{1,0:T(8,128)(2,1)S(1)}) custom-call(f32[4,2,128,128]{3,2,1,0:T(8,128)S(1)} %copy-done, f32[512,128]{1,0:T(8,128)S(1)} %get-tuple-element.27.refs_1_.refs_0_), custom_call_target="tpu_custom_call" | custom-call | flops 1000000000 | tf_op jit(solution)/shard_map/pallas_call | solution.py:271
  15.9 3.2 %collective-permute-done.2.refs_4_ = f32[256,128]{1,0:T(8,128)S(1)} collective-permute-done((f32[256,128]{1,0:T(8,128)S(1)}, f32[256,128]{1,0:T(8,128)S(1)}, u32[]{:S(2)}, u32[]{:S(2)}) %collective-permute-start.2) | collective-permute-done | bytes 131104 | tf_op jit(solution)/shard_map/ppermute | solution.py:298
  19.2 1.3 %collective-permute-done.3.refs_5_ = f32[256,128]{1,0:T(8,128)S(1)} collective-permute-done((f32[256,128]{1,0:T(8,128)S(1)}, f32[256,128]{1,0:T(8,128)S(1)}, u32[]{:S(2)}, u32[]{:S(2)}) %collective-permute-start.3) | collective-permute-done | bytes 131104 | tf_op jit(solution)/shard_map/ppermute | solution.py:298
  20.5 0.4 shard_map.40
  20.9 2.5 %collective-permute-start.6 = (f32[512,128]{1,0:T(8,128)S(1)}, f32[512,128]{1,0:T(8,128)S(1)}, u32[]{:S(2)}, u32[]{:S(2)}) collective-permute-start(f32[512,128]{1,0:T(8,128)S(1)} %get-tuple-element.35), channel_id=1, source_target_pairs={{0,17},{1,16},{2,19},{3,18},{4,21},{5,20},{6,23},{7,22},{8,25},{9,... | collective-permute-start | bytes 786440 | tf_op jit(solution)/shard_map/ppermute | solution.py:298
  23.4 0.5 %collective-permute-start.5 = (f32[512,128]{1,0:T(8,128)S(1)}, f32[512,128]{1,0:T(8,128)S(1)}, u32[]{:S(2)}, u32[]{:S(2)}) collective-permute-start(f32[512,128]{1,0:T(8,128)S(1)} %get-tuple-element.35), channel_id=1, source_target_pairs={{0,1},{1,0},{2,3},{3,2},{4,5},{5,4},{6,7},{7,6},{8,9},{9,8},{10,11... | collective-permute-start | bytes 786440 | tf_op jit(solution)/shard_map/ppermute | solution.py:298
  23.9 0.0 collective-permute-done.8.refs_1_
  23.9 0.5 %collective-permute-start.4 = (f32[512,128]{1,0:T(8,128)S(1)}, f32[512,128]{1,0:T(8,128)S(1)}, u32[]{:S(2)}, u32[]{:S(2)}) collective-permute-start(f32[512,128]{1,0:T(8,128)S(1)} %get-tuple-element.34.refs_1_.refs_2_), channel_id=1, source_target_pairs={{0,16},{1,17},{2,18},{3,19},{4,20},{5,21},{6,22},{7,23},{8,24},{9,... | collective-permute-start | bytes 786440 | tf_op jit(solution)/shard_map/ppermute | solution.py:298
  24.4 0.0 collective-permute-done.9.refs_2_
  24.4 0.0 collective-permute-done.10.refs_3_
  24.4 0.4 %shard_map.42 = (f32[256,128]{1,0:T(8,128)S(1)}, f32[256,128]{1,0:T(8,128)S(1)}, f32[256,128]{1,0:T(8,128)S(1)}, f32[256,128]{1,0:T(8,128)S(1)}) custom-call(f32[512,128]{1,0:T(8,128)S(1)} %get-tuple-element.27.refs_1_.refs_0_, f32[512,128]{1,0:T(8,128)S(1)} %collective-permute-done.8.refs_1_, f32[512,128]{1,0:T(8,128)S(1)} %collective-permute-done.9.refs_2_, ...), custom_call_target="tpu_custom_call" | custom-call | flops 10000000000 | tf_op jit(solution)/shard_map/pallas_call | solution.py:271
  24.8 2.7 %collective-permute-start.11 = (f32[256,128]{1,0:T(8,128)S(1)}, f32[256,128]{1,0:T(8,128)S(1)}, u32[]{:S(2)}, u32[]{:S(2)}) collective-permute-start(f32[256,128]{1,0:T(8,128)S(1)} %get-tuple-element.42), channel_id=1, source_target_pairs={{0,4},{1,5},{2,6},{3,7},{4,0},{5,1},{6,2},{7,3},{8,12},{9,13},{10,... | collective-permute-start | bytes 393224 | tf_op jit(solution)/shard_map/ppermute | solution.py:298
  27.5 0.0 collective-permute-start.12
  27.6 3.5 %collective-permute-done.6.refs_4_.refs_5_ = f32[512,128]{1,0:T(8,128)S(1)} collective-permute-done((f32[512,128]{1,0:T(8,128)S(1)}, f32[512,128]{1,0:T(8,128)S(1)}, u32[]{:S(2)}, u32[]{:S(2)}) %collective-permute-start.6) | collective-permute-done | bytes 262176 | tf_op jit(solution)/shard_map/ppermute | solution.py:298
  31.1 0.0 collective-permute-start.13
  31.1 3.3 %collective-permute-done.5.refs_3_.refs_4_ = f32[512,128]{1,0:T(8,128)S(1)} collective-permute-done((f32[512,128]{1,0:T(8,128)S(1)}, f32[512,128]{1,0:T(8,128)S(1)}, u32[]{:S(2)}, u32[]{:S(2)}) %collective-permute-start.5) | collective-permute-done | bytes 262176 | tf_op jit(solution)/shard_map/ppermute | solution.py:298
  34.3 0.1 collective-permute-done.4.refs_2_.refs_3_
  34.4 0.1 shard_map.41
  34.6 0.1 collective-permute-start.7
  34.7 0.0 collective-permute-done.11.refs_3_
  34.7 0.0 collective-permute-done.12.refs_4_
  34.7 1.3 %collective-permute-done.13.refs_5_ = f32[256,128]{1,0:T(8,128)S(1)} collective-permute-done((f32[256,128]{1,0:T(8,128)S(1)}, f32[256,128]{1,0:T(8,128)S(1)}, u32[]{:S(2)}, u32[]{:S(2)}) %collective-permute-start.13) | collective-permute-done | bytes 131104 | tf_op jit(solution)/shard_map/ppermute | solution.py:298
  36.0 0.4 %shard_map.43.refs_8_ = f32[128,8,128]{2,1,0:T(8,128)S(1)} custom-call(bf16[256,256]{1,0:T(8,128)(2,1)S(1)} %get-tuple-element.36.refs_0_.refs_6_, bf16[256,256]{1,0:T(8,128)(2,1)S(1)} %get-tuple-element.37.refs_1_.refs_7_, f32[256,128]{1,0:T(8,128)S(1)} %get-tuple-element.41.refs_2_, f32[256,128]{1,0:T(8,128)S(1)} %collective-permute-done.11.refs_3_, ...), custom_call_target="tpu_custom_call" | custom-call | flops 5000000000 | tf_op jit(solution)/shard_map/pallas_call | solution.py:271
  36.5 0.1 collective-permute-done.7.refs_1_
  36.6 1.3 %shard_map.44 = f32[128,16,128]{2,1,0:T(8,128)} custom-call(f32[16,128]{1,0:T(8,128)S(1)} %get-tuple-element.25.refs_2_.refs_0_, f32[1024,128]{1,0:T(8,128)S(1)} %collective-permute-done.7.refs_1_, f32[512,128]{1,0:T(8,128)S(1)} %get-tuple-element.34.refs_1_.refs_2_, f32[512,128]{1,0:T(8,128)S(1)} %collective-permute-done.4.refs_2_.refs_3_, ...), custom_call_target="tpu_custom_call" | custom-call | flops 2000000000 | tf_op jit(solution)/shard_map/pallas_call | solution.py:271
Async XLA Ops:
  2.2 5.2 %collective-permute-start = (f32[1024,128]{1,0:T(8,128)S(1)}, f32[1024,128]{1,0:T(8,128)S(1)}, u32[]{:S(2)}, u32[]{:S(2)}) collective-permute-start(f32[1024,128]{1,0:T(8,128)S(1)} %get-tuple-element.26.refs_0_), channel_id=1, source_target_pairs={{0,8},{1,9},{2,10},{3,11},{4,12},{5,13},{6,14},{7,15},{8,0},{9,1},... | collective-permute-start | bytes 1572872 | tf_op jit(solution)/shard_map/ppermute | solution.py:298
  2.7 9.3 %collective-permute-start.1 = (f32[256,128]{1,0:T(8,128)S(1)}, f32[256,128]{1,0:T(8,128)S(1)}, u32[]{:S(2)}, u32[]{:S(2)}) collective-permute-start(f32[256,128]{1,0:T(8,128)S(1)} %get-tuple-element.31), channel_id=1, source_target_pairs={{0,6},{1,7},{2,4},{3,5},{4,2},{5,3},{6,0},{7,1},{8,14},{9,15},{10,... | collective-permute-start | bytes 393224 | tf_op jit(solution)/shard_map/ppermute | solution.py:298
  7.4 8.1 %copy-start = (f32[4,2,128,128]{3,2,1,0:T(8,128)S(1)}, f32[4,2,128,128]{3,2,1,0:T(8,128)}, u32[]{:S(2)}) copy-start(f32[4,2,128,128]{3,2,1,0:T(8,128)} %refs_0_.1) | copy-start | bytes 1572868
  7.7 16.2 %collective-permute-start.8 = (f32[512,128]{1,0:T(8,128)S(1)}, f32[512,128]{1,0:T(8,128)S(1)}, u32[]{:S(2)}, u32[]{:S(2)}) collective-permute-start(f32[512,128]{1,0:T(8,128)S(1)} %get-tuple-element.38), channel_id=1, source_target_pairs={{0,16},{1,17},{2,18},{3,19},{4,20},{5,21},{6,22},{7,23},{8,24},{9,... | collective-permute-start | bytes 786440 | tf_op jit(solution)/shard_map/ppermute | solution.py:298
  9.2 15.2 %collective-permute-start.9 = (f32[512,128]{1,0:T(8,128)S(1)}, f32[512,128]{1,0:T(8,128)S(1)}, u32[]{:S(2)}, u32[]{:S(2)}) collective-permute-start(f32[512,128]{1,0:T(8,128)S(1)} %get-tuple-element.39), channel_id=1, source_target_pairs={{0,1},{1,0},{2,3},{3,2},{4,5},{5,4},{6,7},{7,6},{8,9},{9,8},{10,11... | collective-permute-start | bytes 786440 | tf_op jit(solution)/shard_map/ppermute | solution.py:298
  10.8 13.7 %collective-permute-start.10 = (f32[512,128]{1,0:T(8,128)S(1)}, f32[512,128]{1,0:T(8,128)S(1)}, u32[]{:S(2)}, u32[]{:S(2)}) collective-permute-start(f32[512,128]{1,0:T(8,128)S(1)} %get-tuple-element.40), channel_id=1, source_target_pairs={{0,17},{1,16},{2,19},{3,18},{4,21},{5,20},{6,23},{7,22},{8,25},{9,... | collective-permute-start | bytes 786440 | tf_op jit(solution)/shard_map/ppermute | solution.py:298
  11.2 7.9 %collective-permute-start.2 = (f32[256,128]{1,0:T(8,128)S(1)}, f32[256,128]{1,0:T(8,128)S(1)}, u32[]{:S(2)}, u32[]{:S(2)}) collective-permute-start(f32[256,128]{1,0:T(8,128)S(1)} %get-tuple-element.32), channel_id=1, source_target_pairs={{0,4},{1,5},{2,6},{3,7},{4,0},{5,1},{6,2},{7,3},{8,12},{9,13},{10,... | collective-permute-start | bytes 393224 | tf_op jit(solution)/shard_map/ppermute | solution.py:298
  12.0 8.4 %collective-permute-start.3 = (f32[256,128]{1,0:T(8,128)S(1)}, f32[256,128]{1,0:T(8,128)S(1)}, u32[]{:S(2)}, u32[]{:S(2)}) collective-permute-start(f32[256,128]{1,0:T(8,128)S(1)} %get-tuple-element.33), channel_id=1, source_target_pairs={{0,2},{1,3},{2,0},{3,1},{4,6},{5,7},{6,4},{7,5},{8,10},{9,11},{10,... | collective-permute-start | bytes 393224 | tf_op jit(solution)/shard_map/ppermute | solution.py:298
  20.9 10.2 %collective-permute-start.6 = (f32[512,128]{1,0:T(8,128)S(1)}, f32[512,128]{1,0:T(8,128)S(1)}, u32[]{:S(2)}, u32[]{:S(2)}) collective-permute-start(f32[512,128]{1,0:T(8,128)S(1)} %get-tuple-element.35), channel_id=1, source_target_pairs={{0,17},{1,16},{2,19},{3,18},{4,21},{5,20},{6,23},{7,22},{8,25},{9,... | collective-permute-start | bytes 786440 | tf_op jit(solution)/shard_map/ppermute | solution.py:298
  23.4 11.0 %collective-permute-start.5 = (f32[512,128]{1,0:T(8,128)S(1)}, f32[512,128]{1,0:T(8,128)S(1)}, u32[]{:S(2)}, u32[]{:S(2)}) collective-permute-start(f32[512,128]{1,0:T(8,128)S(1)} %get-tuple-element.35), channel_id=1, source_target_pairs={{0,1},{1,0},{2,3},{3,2},{4,5},{5,4},{6,7},{7,6},{8,9},{9,8},{10,11... | collective-permute-start | bytes 786440 | tf_op jit(solution)/shard_map/ppermute | solution.py:298
  23.9 10.5 %collective-permute-start.4 = (f32[512,128]{1,0:T(8,128)S(1)}, f32[512,128]{1,0:T(8,128)S(1)}, u32[]{:S(2)}, u32[]{:S(2)}) collective-permute-start(f32[512,128]{1,0:T(8,128)S(1)} %get-tuple-element.34.refs_1_.refs_2_), channel_id=1, source_target_pairs={{0,16},{1,17},{2,18},{3,19},{4,20},{5,21},{6,22},{7,23},{8,24},{9,... | collective-permute-start | bytes 786440 | tf_op jit(solution)/shard_map/ppermute | solution.py:298
  24.8 9.8 %collective-permute-start.11 = (f32[256,128]{1,0:T(8,128)S(1)}, f32[256,128]{1,0:T(8,128)S(1)}, u32[]{:S(2)}, u32[]{:S(2)}) collective-permute-start(f32[256,128]{1,0:T(8,128)S(1)} %get-tuple-element.42), channel_id=1, source_target_pairs={{0,4},{1,5},{2,6},{3,7},{4,0},{5,1},{6,2},{7,3},{8,12},{9,13},{10,... | collective-permute-start | bytes 393224 | tf_op jit(solution)/shard_map/ppermute | solution.py:298
  27.5 7.1 %collective-permute-start.12 = (f32[256,128]{1,0:T(8,128)S(1)}, f32[256,128]{1,0:T(8,128)S(1)}, u32[]{:S(2)}, u32[]{:S(2)}) collective-permute-start(f32[256,128]{1,0:T(8,128)S(1)} %get-tuple-element.43), channel_id=1, source_target_pairs={{0,6},{1,7},{2,4},{3,5},{4,2},{5,3},{6,0},{7,1},{8,14},{9,15},{10,... | collective-permute-start | bytes 393224 | tf_op jit(solution)/shard_map/ppermute | solution.py:298
  31.1 5.0 %collective-permute-start.13 = (f32[256,128]{1,0:T(8,128)S(1)}, f32[256,128]{1,0:T(8,128)S(1)}, u32[]{:S(2)}, u32[]{:S(2)}) collective-permute-start(f32[256,128]{1,0:T(8,128)S(1)} %get-tuple-element.44), channel_id=1, source_target_pairs={{0,2},{1,3},{2,0},{3,1},{4,6},{5,7},{6,4},{7,5},{8,10},{9,11},{10,... | collective-permute-start | bytes 393224 | tf_op jit(solution)/shard_map/ppermute | solution.py:298
  34.6 2.0 %collective-permute-start.7 = (f32[1024,128]{1,0:T(8,128)S(1)}, f32[1024,128]{1,0:T(8,128)S(1)}, u32[]{:S(2)}, u32[]{:S(2)}) collective-permute-start(f32[1024,128]{1,0:T(8,128)S(1)} %shard_map.41), channel_id=1, source_target_pairs={{0,8},{1,9},{2,10},{3,11},{4,12},{5,13},{6,14},{7,15},{8,0},{9,1},... | collective-permute-start | bytes 1572872 | tf_op jit(solution)/shard_map/ppermute | solution.py:298

commit v6 on v5

--- a/solution.py
+++ b/solution.py
@@ -8,7 +8,7 @@
 from jax.sharding import PartitionSpec as P
 
 F32, BF16 = jnp.float32, jnp.bfloat16
-COST = dict(enter=2, mix_cores=1, prepare=1, mix=1, after_mix=10, between=1, finish=5, last=2)
+COST = dict(enter=2, mix_cores=1, prepare=1, mix=1, after_mix=30, between=1, finish=10, last=2)
 
 
 def split(value):
@@ -89,40 +89,49 @@
 
 
 def enter(a, b, which, stride, x, gates, cross, mixing, own, *refs):
-    *pieces, held, table, elements, sems = refs
-    width, mid = a.width, a.mid
+    *pieces, held_a, held_b, table, elements, sems = refs
+    width, first = a.width, 2 * a.count
     copies = [
         pltpu.make_async_copy(gates.at[0], table, sems.at[0]),
-        pltpu.make_async_copy(x, held, sems.at[1]),
-        pltpu.make_async_copy(cross, elements, sems.at[2]),
+        pltpu.make_async_copy(x.at[:, pl.ds(first, 2 * b.count), :], held_b, sems.at[1]),
+        pltpu.make_async_copy(x.at[:, pl.ds(0, first), :], held_a, sems.at[2]),
+        pltpu.make_async_copy(cross, elements, sems.at[3]),
     ]
     for copy in copies:
         copy.start()
-    chosen = select(width, a.block, True)
     me = (lax.axis_index("grp") // stride) % 4
-    copies[2].wait()
+    copies[3].wait()
     at = 0
     for target, source in [(0, 0), (0, 2), (1, 0), (1, 2), (0, 0), (0, 1), (2, 0), (2, 1)]:
         for number in entry(elements, which, me ^ target, me ^ source):
             mixing[pl.ds(at, 1), :] = jnp.full((1, width), number, F32)
             at += 1
     copies[0].wait()
-    gate = split(joined(table[0], table[1]))
-    gate = pick(chosen, gate[0]), pick(chosen, gate[1])
+    if a.block % 8:
+        gate = split(joined(table[0], table[1]))
+        chosen = select(width, a.block, True)
+        gate = pick(chosen, gate[0]), pick(chosen, gate[1])
+    else:
+        blocks = []
+        for slot in range(a.inner):
+            at = pl.ds(pl.multiple_of((slot ^ lax.axis_index("qb")) * a.block, a.block), a.block)
+            blocks.append(joined(table[0, at, :], table[1, at, :]))
+        gate = split(rows(blocks))
+
+    def apply(s, held):
+        step = 2 * s.count
+        flat = held.reshape(width * step, width)
+        state = columns([rows([flat[pl.ds(2 * i + part, width, step), :] for part in range(2)]) for i in range(s.count)])
+        return dot_split(gate, split(state))
+
     copies[1].wait()
-
-    def apply(first, s):
-        state = columns(
-            [rows([held[pl.ds(2 * m + part, width, 2 * mid), :] for part in range(2)]) for m in range(first, first + s.count)]
-        )
-        return dot_split(gate, split(state))
-
-    state = apply(a.count, b)
+    state = apply(b, held_b)
     for slot in range(b.inner):
         for part in range(2):
             for i in range(b.count):
                 pieces[slot // 2][b.in_piece(part, slot, i), :] = b.cut(state, slot, part, i)
-    state = apply(0, a)
+    copies[2].wait()
+    state = apply(a, held_a)
     for slot in range(a.inner):
         for part in range(2):
             for i in range(a.count):
@@ -226,14 +235,15 @@
                 ]
 
 
-def third_gate(s, gate, state, out):
-    step = 2 * s.count
+def third_gate(s, gate, state, out, first=0, count=None):
+    step, count = 2 * s.count, count or s.width
     flat = out.reshape(s.width * step, s.width)
-    state = dot_split(gate, split(state))
+    gate = [rows([part[t : t + count] for t in (first, s.width + first)]) for part in gate]
+    state = dot_split(gate, state)
     for i in range(s.count):
         for part in range(2):
-            flat[pl.ds(2 * i + part, s.width, step), :] = state[
-                part * s.width : (part + 1) * s.width, i * s.width : (i + 1) * s.width
+            flat[pl.ds(first * step + 2 * i + part, count, step), :] = state[
+                part * count : (part + 1) * count, i * s.width : (i + 1) * s.width
             ]
 
 
@@ -241,10 +251,11 @@
     *pieces, out = refs
     pieces = turned(pieces, -1)
     state = s.collect(lambda part, slot, i: pieces[slot // 2][s.in_piece(part, slot, i), :])
-    third_gate(s, (high[...], low[...]), state, out)
+    third_gate(s, (high[...], low[...]), split(state), out)
 
 
 def last(a, b, mixing, got, near, near_got, far, far_got, high, low, done, out, held, sems):
+    width = a.width
     first = pltpu.make_async_copy(done, out.at[:, pl.ds(0, 2 * a.count), :], sems.at[0])
     first.start()
     pairs = sums(mixing, got, (near, near_got, far, far_got))
@@ -253,11 +264,18 @@
         at = slot // 2 * b.cell + i * b.block
         return pairs[slot % 2][part][at : at + b.block]
 
-    third_gate(b, (high[...], low[...]), b.collect(read), held)
-    second = pltpu.make_async_copy(held, out.at[:, pl.ds(2 * a.count, 2 * b.count), :], sems.at[1])
-    second.start()
-    first.wait()
-    second.wait()
+    copies, state, half = [first], split(b.collect(read)), width // 2
+    for part in range(2):
+        third_gate(b, (high[...], low[...]), state, held, part * half, half)
+        at = pl.ds(part * half, half)
+        copies.append(
+            pltpu.make_async_copy(
+                held.at[at], out.at[at, pl.ds(2 * a.count, 2 * b.count), :], sems.at[1 + part]
+            )
+        )
+        copies[-1].start()
+    for copy in copies:
+        copy.wait()
 
 
 def call(body, outs, *args, places={}, scratch=(), after=(), out_place=pltpu.VMEM):
@@ -321,17 +339,18 @@
     def lines(value):
         return value.reshape(2, local // width, width).transpose(1, 0, 2).reshape(2 * local // width, width)
 
-    x = lines(amplitudes)
+    x = lines(amplitudes).reshape(width, 2 * mid, width)
     mixing, own_a, *pieces_b = call(
         bind(enter, a, b, which, stride),
         [array(16), whole(a)] + piece(b),
         *(pltpu.with_memory_space_constraint(ref, pltpu.HBM) for ref in (x, layer_gates, cross_gates)),
         places={i: pltpu.HBM for i in range(3)},
         scratch=[
-            pltpu.VMEM(x.shape, F32),
+            pltpu.VMEM((width, 2 * a.count, width), F32),
+            pltpu.VMEM((width, 2 * b.count, width), F32),
             pltpu.VMEM(layer_gates.shape[1:], F32),
             pltpu.SMEM(cross_gates.shape, F32),
-            pltpu.SemaphoreType.DMA((3,)),
+            pltpu.SemaphoreType.DMA((4,)),
         ],
     )
 
@@ -364,7 +383,7 @@
         *sums_b,
         *third,
         done,
-        scratch=[pltpu.VMEM(tiles(b).shape, F32), pltpu.SemaphoreType.DMA((2,))],
+        scratch=[pltpu.VMEM(tiles(b).shape, F32), pltpu.SemaphoreType.DMA((3,))],
         out_place=pltpu.HBM,
     )
     return out.reshape(local // width, 2, width).transpose(1, 0, 2).reshape(2, local)

time: 38.1 us -> 37.9 us (level)
  no operation moved by 1% of the time
where the time goes in v6:
time: 37.9 us; the launch traced here: 37.7 us
  starting transfers between devices  19.2 us (51%)
  waiting for transfers between devices  13 us (34%)
  Pallas kernels  5.4 us (14%)
    ppermute x14, starting transfers between devices, send(): return lax.ppermute(value, ('grp', 'qb'), perm)  19.2 us
    ppermute x14, waiting for transfers between devices, send(): return lax.ppermute(value, ('grp', 'qb'), perm)  13 us
    pallas_call x8, Pallas kernels, call(): pl.pallas_call(kernel, out_shape=outs, in_specs=specs + [pl.BlockSpec(mem...  5.4 us
  transfers between devices with their start and end apart: 14, of which 7 were waited for; matrix products, arithmetic and copies ran while one was open for 0% of the time, Pallas kernels for 6%

profile of v6, /device:TPU:0, one launch (start us, length us, event | category | flops | bytes accessed | tf_op | source)
XLA Modules:
  0.0 37.7 jit_solution(11664249202032776682)
XLA Ops:
  0.0 2.0 %shard_map.37 = (f32[16,128]{1,0:T(8,128)S(1)}, f32[1024,128]{1,0:T(8,128)S(1)}, f32[256,128]{1,0:T(8,128)S(1)}, f32[256,128]{1,0:T(8,128)S(1)}, f32[256,128]{1,0:T(8,128)S(1)}, /*index=5*/f32[256,128]{1,0:T(8,128)S(1)}) custom-call(f32[128,16,128]{2,1,0:T(8,128)} %bitcast.10, f32[4,2,128,128]{3,2,1,0:T(8,128)} %refs_0_.1, f32[2,2,4,4]{3,2,1,0:T(4,128)} %refs_2_.1), custom_call_target="tpu_custom_call" | custom-call | flops 2000000000 | tf_op jit(solution)/shard_map/pallas_call | solution.py:289
  2.0 0.5 %collective-permute-start = (f32[1024,128]{1,0:T(8,128)S(1)}, f32[1024,128]{1,0:T(8,128)S(1)}, u32[]{:S(2)}, u32[]{:S(2)}) collective-permute-start(f32[1024,128]{1,0:T(8,128)S(1)} %get-tuple-element.26.refs_0_), channel_id=1, source_target_pairs={{0,8},{1,9},{2,10},{3,11},{4,12},{5,13},{6,14},{7,15},{8,0},{9,1},... | collective-permute-start | bytes 1572872 | tf_op jit(solution)/shard_map/ppermute | solution.py:316
  2.6 4.7 %collective-permute-start.1 = (f32[256,128]{1,0:T(8,128)S(1)}, f32[256,128]{1,0:T(8,128)S(1)}, u32[]{:S(2)}, u32[]{:S(2)}) collective-permute-start(f32[256,128]{1,0:T(8,128)S(1)} %get-tuple-element.31), channel_id=1, source_target_pairs={{0,6},{1,7},{2,4},{3,5},{4,2},{5,3},{6,0},{7,1},{8,14},{9,15},{10,... | collective-permute-start | bytes 393224 | tf_op jit(solution)/shard_map/ppermute | solution.py:316
  7.2 0.0 collective-permute-done.refs_1_
  7.2 0.0 copy-start
  7.2 0.3 shard_map.38
  7.5 1.6 %collective-permute-start.8 = (f32[512,128]{1,0:T(8,128)S(1)}, f32[512,128]{1,0:T(8,128)S(1)}, u32[]{:S(2)}, u32[]{:S(2)}) collective-permute-start(f32[512,128]{1,0:T(8,128)S(1)} %get-tuple-element.38), channel_id=1, source_target_pairs={{0,16},{1,17},{2,18},{3,19},{4,20},{5,21},{6,22},{7,23},{8,24},{9,... | collective-permute-start | bytes 786440 | tf_op jit(solution)/shard_map/ppermute | solution.py:316
  9.1 1.5 %collective-permute-start.9 = (f32[512,128]{1,0:T(8,128)S(1)}, f32[512,128]{1,0:T(8,128)S(1)}, u32[]{:S(2)}, u32[]{:S(2)}) collective-permute-start(f32[512,128]{1,0:T(8,128)S(1)} %get-tuple-element.39), channel_id=1, source_target_pairs={{0,1},{1,0},{2,3},{3,2},{4,5},{5,4},{6,7},{7,6},{8,9},{9,8},{10,11... | collective-permute-start | bytes 786440 | tf_op jit(solution)/shard_map/ppermute | solution.py:316
  10.6 0.5 %collective-permute-start.10 = (f32[512,128]{1,0:T(8,128)S(1)}, f32[512,128]{1,0:T(8,128)S(1)}, u32[]{:S(2)}, u32[]{:S(2)}) collective-permute-start(f32[512,128]{1,0:T(8,128)S(1)} %get-tuple-element.40), channel_id=1, source_target_pairs={{0,17},{1,16},{2,19},{3,18},{4,21},{5,20},{6,23},{7,22},{8,25},{9,... | collective-permute-start | bytes 786440 | tf_op jit(solution)/shard_map/ppermute | solution.py:316
  11.1 0.8 %collective-permute-start.2 = (f32[256,128]{1,0:T(8,128)S(1)}, f32[256,128]{1,0:T(8,128)S(1)}, u32[]{:S(2)}, u32[]{:S(2)}) collective-permute-start(f32[256,128]{1,0:T(8,128)S(1)} %get-tuple-element.32), channel_id=1, source_target_pairs={{0,4},{1,5},{2,6},{3,7},{4,0},{5,1},{6,2},{7,3},{8,12},{9,13},{10,... | collective-permute-start | bytes 393224 | tf_op jit(solution)/shard_map/ppermute | solution.py:316
  11.9 0.0 collective-permute-done.1.refs_3_
  11.9 3.4 %collective-permute-start.3 = (f32[256,128]{1,0:T(8,128)S(1)}, f32[256,128]{1,0:T(8,128)S(1)}, u32[]{:S(2)}, u32[]{:S(2)}) collective-permute-start(f32[256,128]{1,0:T(8,128)S(1)} %get-tuple-element.33), channel_id=1, source_target_pairs={{0,2},{1,3},{2,0},{3,1},{4,6},{5,7},{6,4},{7,5},{8,10},{9,11},{10,... | collective-permute-start | bytes 393224 | tf_op jit(solution)/shard_map/ppermute | solution.py:316
  15.3 0.0 copy-done
  15.3 0.5 %shard_map.39 = (bf16[256,256]{1,0:T(8,128)(2,1)S(1)}, bf16[256,256]{1,0:T(8,128)(2,1)S(1)}, bf16[256,256]{1,0:T(8,128)(2,1)S(1)}, bf16[256,256]{1,0:T(8,128)(2,1)S(1)}) custom-call(f32[4,2,128,128]{3,2,1,0:T(8,128)S(1)} %copy-done, f32[512,128]{1,0:T(8,128)S(1)} %get-tuple-element.27.refs_1_.refs_0_), custom_call_target="tpu_custom_call" | custom-call | flops 1000000000 | tf_op jit(solution)/shard_map/pallas_call | solution.py:289
  15.8 3.2 %collective-permute-done.2.refs_4_ = f32[256,128]{1,0:T(8,128)S(1)} collective-permute-done((f32[256,128]{1,0:T(8,128)S(1)}, f32[256,128]{1,0:T(8,128)S(1)}, u32[]{:S(2)}, u32[]{:S(2)}) %collective-permute-start.2) | collective-permute-done | bytes 131104 | tf_op jit(solution)/shard_map/ppermute | solution.py:316
  19.0 1.3 %collective-permute-done.3.refs_5_ = f32[256,128]{1,0:T(8,128)S(1)} collective-permute-done((f32[256,128]{1,0:T(8,128)S(1)}, f32[256,128]{1,0:T(8,128)S(1)}, u32[]{:S(2)}, u32[]{:S(2)}) %collective-permute-start.3) | collective-permute-done | bytes 131104 | tf_op jit(solution)/shard_map/ppermute | solution.py:316
  20.3 0.4 shard_map.40
  20.7 2.5 %collective-permute-start.6 = (f32[512,128]{1,0:T(8,128)S(1)}, f32[512,128]{1,0:T(8,128)S(1)}, u32[]{:S(2)}, u32[]{:S(2)}) collective-permute-start(f32[512,128]{1,0:T(8,128)S(1)} %get-tuple-element.35), channel_id=1, source_target_pairs={{0,17},{1,16},{2,19},{3,18},{4,21},{5,20},{6,23},{7,22},{8,25},{9,... | collective-permute-start | bytes 786440 | tf_op jit(solution)/shard_map/ppermute | solution.py:316
  23.2 0.5 %collective-permute-start.5 = (f32[512,128]{1,0:T(8,128)S(1)}, f32[512,128]{1,0:T(8,128)S(1)}, u32[]{:S(2)}, u32[]{:S(2)}) collective-permute-start(f32[512,128]{1,0:T(8,128)S(1)} %get-tuple-element.35), channel_id=1, source_target_pairs={{0,1},{1,0},{2,3},{3,2},{4,5},{5,4},{6,7},{7,6},{8,9},{9,8},{10,11... | collective-permute-start | bytes 786440 | tf_op jit(solution)/shard_map/ppermute | solution.py:316
  23.7 0.0 collective-permute-done.8.refs_1_
  23.7 0.5 %collective-permute-start.4 = (f32[512,128]{1,0:T(8,128)S(1)}, f32[512,128]{1,0:T(8,128)S(1)}, u32[]{:S(2)}, u32[]{:S(2)}) collective-permute-start(f32[512,128]{1,0:T(8,128)S(1)} %get-tuple-element.34.refs_1_.refs_2_), channel_id=1, source_target_pairs={{0,16},{1,17},{2,18},{3,19},{4,20},{5,21},{6,22},{7,23},{8,24},{9,... | collective-permute-start | bytes 786440 | tf_op jit(solution)/shard_map/ppermute | solution.py:316
  24.3 0.0 collective-permute-done.9.refs_2_
  24.3 0.0 collective-permute-done.10.refs_3_
  24.3 0.4 %shard_map.42 = (f32[256,128]{1,0:T(8,128)S(1)}, f32[256,128]{1,0:T(8,128)S(1)}, f32[256,128]{1,0:T(8,128)S(1)}, f32[256,128]{1,0:T(8,128)S(1)}) custom-call(f32[512,128]{1,0:T(8,128)S(1)} %get-tuple-element.27.refs_1_.refs_0_, f32[512,128]{1,0:T(8,128)S(1)} %collective-permute-done.8.refs_1_, f32[512,128]{1,0:T(8,128)S(1)} %collective-permute-done.9.refs_2_, ...), custom_call_target="tpu_custom_call" | custom-call | flops 30000001024 | tf_op jit(solution)/shard_map/pallas_call | solution.py:289
  24.7 2.6 %collective-permute-start.11 = (f32[256,128]{1,0:T(8,128)S(1)}, f32[256,128]{1,0:T(8,128)S(1)}, u32[]{:S(2)}, u32[]{:S(2)}) collective-permute-start(f32[256,128]{1,0:T(8,128)S(1)} %get-tuple-element.42), channel_id=1, source_target_pairs={{0,4},{1,5},{2,6},{3,7},{4,0},{5,1},{6,2},{7,3},{8,12},{9,13},{10,... | collective-permute-start | bytes 393224 | tf_op jit(solution)/shard_map/ppermute | solution.py:316
  27.3 0.0 collective-permute-start.12
  27.3 3.6 %collective-permute-done.6.refs_4_.refs_5_ = f32[512,128]{1,0:T(8,128)S(1)} collective-permute-done((f32[512,128]{1,0:T(8,128)S(1)}, f32[512,128]{1,0:T(8,128)S(1)}, u32[]{:S(2)}, u32[]{:S(2)}) %collective-permute-start.6) | collective-permute-done | bytes 262176 | tf_op jit(solution)/shard_map/ppermute | solution.py:316
  30.9 0.0 collective-permute-start.13
  30.9 3.3 %collective-permute-done.5.refs_3_.refs_4_ = f32[512,128]{1,0:T(8,128)S(1)} collective-permute-done((f32[512,128]{1,0:T(8,128)S(1)}, f32[512,128]{1,0:T(8,128)S(1)}, u32[]{:S(2)}, u32[]{:S(2)}) %collective-permute-start.5) | collective-permute-done | bytes 262176 | tf_op jit(solution)/shard_map/ppermute | solution.py:316
  34.2 0.1 collective-permute-done.4.refs_2_.refs_3_
  34.3 0.1 shard_map.41
  34.4 0.1 collective-permute-start.7
  34.5 0.0 collective-permute-done.11.refs_3_
  34.5 0.0 collective-permute-done.12.refs_4_
  34.5 1.4 %collective-permute-done.13.refs_5_ = f32[256,128]{1,0:T(8,128)S(1)} collective-permute-done((f32[256,128]{1,0:T(8,128)S(1)}, f32[256,128]{1,0:T(8,128)S(1)}, u32[]{:S(2)}, u32[]{:S(2)}) %collective-permute-start.13) | collective-permute-done | bytes 131104 | tf_op jit(solution)/shard_map/ppermute | solution.py:316
  35.9 0.4 %shard_map.43.refs_8_ = f32[128,8,128]{2,1,0:T(8,128)S(1)} custom-call(bf16[256,256]{1,0:T(8,128)(2,1)S(1)} %get-tuple-element.36.refs_0_.refs_6_, bf16[256,256]{1,0:T(8,128)(2,1)S(1)} %get-tuple-element.37.refs_1_.refs_7_, f32[256,128]{1,0:T(8,128)S(1)} %get-tuple-element.41.refs_2_, f32[256,128]{1,0:T(8,128)S(1)} %collective-permute-done.11.refs_3_, ...), custom_call_target="tpu_custom_call" | custom-call | flops 10000000000 | tf_op jit(solution)/shard_map/pallas_call | solution.py:289
  36.3 0.1 collective-permute-done.7.refs_1_
  36.4 1.3 %shard_map.44 = f32[128,16,128]{2,1,0:T(8,128)} custom-call(f32[16,128]{1,0:T(8,128)S(1)} %get-tuple-element.25.refs_2_.refs_0_, f32[1024,128]{1,0:T(8,128)S(1)} %collective-permute-done.7.refs_1_, f32[512,128]{1,0:T(8,128)S(1)} %get-tuple-element.34.refs_1_.refs_2_, f32[512,128]{1,0:T(8,128)S(1)} %collective-permute-done.4.refs_2_.refs_3_, ...), custom_call_target="tpu_custom_call" | custom-call | flops 2000000000 | tf_op jit(solution)/shard_map/pallas_call | solution.py:289
Async XLA Ops:
  2.0 5.2 %collective-permute-start = (f32[1024,128]{1,0:T(8,128)S(1)}, f32[1024,128]{1,0:T(8,128)S(1)}, u32[]{:S(2)}, u32[]{:S(2)}) collective-permute-start(f32[1024,128]{1,0:T(8,128)S(1)} %get-tuple-element.26.refs_0_), channel_id=1, source_target_pairs={{0,8},{1,9},{2,10},{3,11},{4,12},{5,13},{6,14},{7,15},{8,0},{9,1},... | collective-permute-start | bytes 1572872 | tf_op jit(solution)/shard_map/ppermute | solution.py:316
  2.6 9.3 %collective-permute-start.1 = (f32[256,128]{1,0:T(8,128)S(1)}, f32[256,128]{1,0:T(8,128)S(1)}, u32[]{:S(2)}, u32[]{:S(2)}) collective-permute-start(f32[256,128]{1,0:T(8,128)S(1)} %get-tuple-element.31), channel_id=1, source_target_pairs={{0,6},{1,7},{2,4},{3,5},{4,2},{5,3},{6,0},{7,1},{8,14},{9,15},{10,... | collective-permute-start | bytes 393224 | tf_op jit(solution)/shard_map/ppermute | solution.py:316
  7.2 8.1 %copy-start = (f32[4,2,128,128]{3,2,1,0:T(8,128)S(1)}, f32[4,2,128,128]{3,2,1,0:T(8,128)}, u32[]{:S(2)}) copy-start(f32[4,2,128,128]{3,2,1,0:T(8,128)} %refs_0_.1) | copy-start | bytes 1572868
  7.5 16.2 %collective-permute-start.8 = (f32[512,128]{1,0:T(8,128)S(1)}, f32[512,128]{1,0:T(8,128)S(1)}, u32[]{:S(2)}, u32[]{:S(2)}) collective-permute-start(f32[512,128]{1,0:T(8,128)S(1)} %get-tuple-element.38), channel_id=1, source_target_pairs={{0,16},{1,17},{2,18},{3,19},{4,20},{5,21},{6,22},{7,23},{8,24},{9,... | collective-permute-start | bytes 786440 | tf_op jit(solution)/shard_map/ppermute | solution.py:316
  9.1 15.2 %collective-permute-start.9 = (f32[512,128]{1,0:T(8,128)S(1)}, f32[512,128]{1,0:T(8,128)S(1)}, u32[]{:S(2)}, u32[]{:S(2)}) collective-permute-start(f32[512,128]{1,0:T(8,128)S(1)} %get-tuple-element.39), channel_id=1, source_target_pairs={{0,1},{1,0},{2,3},{3,2},{4,5},{5,4},{6,7},{7,6},{8,9},{9,8},{10,11... | collective-permute-start | bytes 786440 | tf_op jit(solution)/shard_map/ppermute | solution.py:316
  10.6 13.7 %collective-permute-start.10 = (f32[512,128]{1,0:T(8,128)S(1)}, f32[512,128]{1,0:T(8,128)S(1)}, u32[]{:S(2)}, u32[]{:S(2)}) collective-permute-start(f32[512,128]{1,0:T(8,128)S(1)} %get-tuple-element.40), channel_id=1, source_target_pairs={{0,17},{1,16},{2,19},{3,18},{4,21},{5,20},{6,23},{7,22},{8,25},{9,... | collective-permute-start | bytes 786440 | tf_op jit(solution)/shard_map/ppermute | solution.py:316
  11.1 8.0 %collective-permute-start.2 = (f32[256,128]{1,0:T(8,128)S(1)}, f32[256,128]{1,0:T(8,128)S(1)}, u32[]{:S(2)}, u32[]{:S(2)}) collective-permute-start(f32[256,128]{1,0:T(8,128)S(1)} %get-tuple-element.32), channel_id=1, source_target_pairs={{0,4},{1,5},{2,6},{3,7},{4,0},{5,1},{6,2},{7,3},{8,12},{9,13},{10,... | collective-permute-start | bytes 393224 | tf_op jit(solution)/shard_map/ppermute | solution.py:316
  11.9 8.4 %collective-permute-start.3 = (f32[256,128]{1,0:T(8,128)S(1)}, f32[256,128]{1,0:T(8,128)S(1)}, u32[]{:S(2)}, u32[]{:S(2)}) collective-permute-start(f32[256,128]{1,0:T(8,128)S(1)} %get-tuple-element.33), channel_id=1, source_target_pairs={{0,2},{1,3},{2,0},{3,1},{4,6},{5,7},{6,4},{7,5},{8,10},{9,11},{10,... | collective-permute-start | bytes 393224 | tf_op jit(solution)/shard_map/ppermute | solution.py:316
  20.7 10.2 %collective-permute-start.6 = (f32[512,128]{1,0:T(8,128)S(1)}, f32[512,128]{1,0:T(8,128)S(1)}, u32[]{:S(2)}, u32[]{:S(2)}) collective-permute-start(f32[512,128]{1,0:T(8,128)S(1)} %get-tuple-element.35), channel_id=1, source_target_pairs={{0,17},{1,16},{2,19},{3,18},{4,21},{5,20},{6,23},{7,22},{8,25},{9,... | collective-permute-start | bytes 786440 | tf_op jit(solution)/shard_map/ppermute | solution.py:316
  23.2 11.0 %collective-permute-start.5 = (f32[512,128]{1,0:T(8,128)S(1)}, f32[512,128]{1,0:T(8,128)S(1)}, u32[]{:S(2)}, u32[]{:S(2)}) collective-permute-start(f32[512,128]{1,0:T(8,128)S(1)} %get-tuple-element.35), channel_id=1, source_target_pairs={{0,1},{1,0},{2,3},{3,2},{4,5},{5,4},{6,7},{7,6},{8,9},{9,8},{10,11... | collective-permute-start | bytes 786440 | tf_op jit(solution)/shard_map/ppermute | solution.py:316
  23.7 10.6 %collective-permute-start.4 = (f32[512,128]{1,0:T(8,128)S(1)}, f32[512,128]{1,0:T(8,128)S(1)}, u32[]{:S(2)}, u32[]{:S(2)}) collective-permute-start(f32[512,128]{1,0:T(8,128)S(1)} %get-tuple-element.34.refs_1_.refs_2_), channel_id=1, source_target_pairs={{0,16},{1,17},{2,18},{3,19},{4,20},{5,21},{6,22},{7,23},{8,24},{9,... | collective-permute-start | bytes 786440 | tf_op jit(solution)/shard_map/ppermute | solution.py:316
  24.7 9.8 %collective-permute-start.11 = (f32[256,128]{1,0:T(8,128)S(1)}, f32[256,128]{1,0:T(8,128)S(1)}, u32[]{:S(2)}, u32[]{:S(2)}) collective-permute-start(f32[256,128]{1,0:T(8,128)S(1)} %get-tuple-element.42), channel_id=1, source_target_pairs={{0,4},{1,5},{2,6},{3,7},{4,0},{5,1},{6,2},{7,3},{8,12},{9,13},{10,... | collective-permute-start | bytes 393224 | tf_op jit(solution)/shard_map/ppermute | solution.py:316
  27.3 7.2 %collective-permute-start.12 = (f32[256,128]{1,0:T(8,128)S(1)}, f32[256,128]{1,0:T(8,128)S(1)}, u32[]{:S(2)}, u32[]{:S(2)}) collective-permute-start(f32[256,128]{1,0:T(8,128)S(1)} %get-tuple-element.43), channel_id=1, source_target_pairs={{0,6},{1,7},{2,4},{3,5},{4,2},{5,3},{6,0},{7,1},{8,14},{9,15},{10,... | collective-permute-start | bytes 393224 | tf_op jit(solution)/shard_map/ppermute | solution.py:316
  30.9 5.0 %collective-permute-start.13 = (f32[256,128]{1,0:T(8,128)S(1)}, f32[256,128]{1,0:T(8,128)S(1)}, u32[]{:S(2)}, u32[]{:S(2)}) collective-permute-start(f32[256,128]{1,0:T(8,128)S(1)} %get-tuple-element.44), channel_id=1, source_target_pairs={{0,2},{1,3},{2,0},{3,1},{4,6},{5,7},{6,4},{7,5},{8,10},{9,11},{10,... | collective-permute-start | bytes 393224 | tf_op jit(solution)/shard_map/ppermute | solution.py:316
  34.4 2.0 %collective-permute-start.7 = (f32[1024,128]{1,0:T(8,128)S(1)}, f32[1024,128]{1,0:T(8,128)S(1)}, u32[]{:S(2)}, u32[]{:S(2)}) collective-permute-start(f32[1024,128]{1,0:T(8,128)S(1)} %shard_map.41), channel_id=1, source_target_pairs={{0,8},{1,9},{2,10},{3,11},{4,12},{5,13},{6,14},{7,15},{8,0},{9,1},... | collective-permute-start | bytes 1572872 | tf_op jit(solution)/shard_map/ppermute | solution.py:316

commit v7 on v6

--- a/solution.py
+++ b/solution.py
@@ -371,7 +371,7 @@
     sums_a = cross_first(own_a, a)
     *lane, third_high, third_low = call(bind(prepare, width, a.block), [table] * 4, layer_gates, after=sums_a[:1])
     third = third_high, third_low
-    near_b, far_b = call(bind(between, b), [pair(b)] * 2, *lane, *backwards(pieces_b))
+    near_b, far_b = call(bind(between, b), [pair(b)] * 2, *lane, *backwards(pieces_b), after=sums_a[1:2])
     pieces_a = call(bind(after_mix, a), piece(a), *sums_a, *lane)
     pieces_a = swap_upper(pieces_a)
     sums_b = cross(near_b, far_b, b)

time: 37.9 us -> 37.9 us (level)
  no operation moved by 1% of the time
where the time goes in v7:
time: 37.9 us; the launch traced here: 37.7 us
  starting transfers between devices  19.2 us (51%)
  waiting for transfers between devices  13 us (34%)
  Pallas kernels  5.4 us (14%)
    ppermute x14, starting transfers between devices, send(): return lax.ppermute(value, ('grp', 'qb'), perm)  19.2 us
    ppermute x14, waiting for transfers between devices, send(): return lax.ppermute(value, ('grp', 'qb'), perm)  13 us
    pallas_call x8, Pallas kernels, call(): pl.pallas_call(kernel, out_shape=outs, in_specs=specs + [pl.BlockSpec(mem...  5.4 us
  transfers between devices with their start and end apart: 14, of which 7 were waited for; matrix products, arithmetic and copies ran while one was open for 0% of the time, Pallas kernels for 6%

profile of v7, /device:TPU:0, one launch (start us, length us, event | category | flops | bytes accessed | tf_op | source)
XLA Modules:
  0.0 37.7 jit_solution(14137545773730540062)
XLA Ops:
  0.0 2.0 %shard_map.37 = (f32[16,128]{1,0:T(8,128)S(1)}, f32[1024,128]{1,0:T(8,128)S(1)}, f32[256,128]{1,0:T(8,128)S(1)}, f32[256,128]{1,0:T(8,128)S(1)}, f32[256,128]{1,0:T(8,128)S(1)}, /*index=5*/f32[256,128]{1,0:T(8,128)S(1)}) custom-call(f32[128,16,128]{2,1,0:T(8,128)} %bitcast.10, f32[4,2,128,128]{3,2,1,0:T(8,128)} %refs_0_.1, f32[2,2,4,4]{3,2,1,0:T(4,128)} %refs_2_.1), custom_call_target="tpu_custom_call" | custom-call | flops 2000000000 | tf_op jit(solution)/shard_map/pallas_call | solution.py:289
  2.0 0.5 %collective-permute-start = (f32[1024,128]{1,0:T(8,128)S(1)}, f32[1024,128]{1,0:T(8,128)S(1)}, u32[]{:S(2)}, u32[]{:S(2)}) collective-permute-start(f32[1024,128]{1,0:T(8,128)S(1)} %get-tuple-element.26.refs_0_), channel_id=1, source_target_pairs={{0,8},{1,9},{2,10},{3,11},{4,12},{5,13},{6,14},{7,15},{8,0},{9,1},... | collective-permute-start | bytes 1572872 | tf_op jit(solution)/shard_map/ppermute | solution.py:316
  2.6 4.7 %collective-permute-start.1 = (f32[256,128]{1,0:T(8,128)S(1)}, f32[256,128]{1,0:T(8,128)S(1)}, u32[]{:S(2)}, u32[]{:S(2)}) collective-permute-start(f32[256,128]{1,0:T(8,128)S(1)} %get-tuple-element.31), channel_id=1, source_target_pairs={{0,6},{1,7},{2,4},{3,5},{4,2},{5,3},{6,0},{7,1},{8,14},{9,15},{10,... | collective-permute-start | bytes 393224 | tf_op jit(solution)/shard_map/ppermute | solution.py:316
  7.2 0.0 collective-permute-done.refs_1_
  7.2 0.0 copy-start
  7.2 0.3 shard_map.38
  7.5 1.6 %collective-permute-start.4 = (f32[512,128]{1,0:T(8,128)S(1)}, f32[512,128]{1,0:T(8,128)S(1)}, u32[]{:S(2)}, u32[]{:S(2)}) collective-permute-start(f32[512,128]{1,0:T(8,128)S(1)} %get-tuple-element.34), channel_id=1, source_target_pairs={{0,16},{1,17},{2,18},{3,19},{4,20},{5,21},{6,22},{7,23},{8,24},{9,... | collective-permute-start | bytes 786440 | tf_op jit(solution)/shard_map/ppermute | solution.py:316
  9.1 1.5 %collective-permute-start.9 = (f32[512,128]{1,0:T(8,128)S(1)}, f32[512,128]{1,0:T(8,128)S(1)}, u32[]{:S(2)}, u32[]{:S(2)}) collective-permute-start(f32[512,128]{1,0:T(8,128)S(1)} %get-tuple-element.39), channel_id=1, source_target_pairs={{0,1},{1,0},{2,3},{3,2},{4,5},{5,4},{6,7},{7,6},{8,9},{9,8},{10,11... | collective-permute-start | bytes 786440 | tf_op jit(solution)/shard_map/ppermute | solution.py:316
  10.6 0.5 %collective-permute-start.10 = (f32[512,128]{1,0:T(8,128)S(1)}, f32[512,128]{1,0:T(8,128)S(1)}, u32[]{:S(2)}, u32[]{:S(2)}) collective-permute-start(f32[512,128]{1,0:T(8,128)S(1)} %get-tuple-element.40), channel_id=1, source_target_pairs={{0,17},{1,16},{2,19},{3,18},{4,21},{5,20},{6,23},{7,22},{8,25},{9,... | collective-permute-start | bytes 786440 | tf_op jit(solution)/shard_map/ppermute | solution.py:316
  11.1 0.8 %collective-permute-start.2 = (f32[256,128]{1,0:T(8,128)S(1)}, f32[256,128]{1,0:T(8,128)S(1)}, u32[]{:S(2)}, u32[]{:S(2)}) collective-permute-start(f32[256,128]{1,0:T(8,128)S(1)} %get-tuple-element.32), channel_id=1, source_target_pairs={{0,4},{1,5},{2,6},{3,7},{4,0},{5,1},{6,2},{7,3},{8,12},{9,13},{10,... | collective-permute-start | bytes 393224 | tf_op jit(solution)/shard_map/ppermute | solution.py:316
  11.9 0.0 collective-permute-done.1.refs_3_
  11.9 3.4 %collective-permute-start.3 = (f32[256,128]{1,0:T(8,128)S(1)}, f32[256,128]{1,0:T(8,128)S(1)}, u32[]{:S(2)}, u32[]{:S(2)}) collective-permute-start(f32[256,128]{1,0:T(8,128)S(1)} %get-tuple-element.33), channel_id=1, source_target_pairs={{0,2},{1,3},{2,0},{3,1},{4,6},{5,7},{6,4},{7,5},{8,10},{9,11},{10,... | collective-permute-start | bytes 393224 | tf_op jit(solution)/shard_map/ppermute | solution.py:316
  15.3 0.0 copy-done
  15.3 0.5 %shard_map.39 = (bf16[256,256]{1,0:T(8,128)(2,1)S(1)}, bf16[256,256]{1,0:T(8,128)(2,1)S(1)}, bf16[256,256]{1,0:T(8,128)(2,1)S(1)}, bf16[256,256]{1,0:T(8,128)(2,1)S(1)}) custom-call(f32[4,2,128,128]{3,2,1,0:T(8,128)S(1)} %copy-done, f32[512,128]{1,0:T(8,128)S(1)} %get-tuple-element.27.refs_1_.refs_0_), custom_call_target="tpu_custom_call" | custom-call | flops 1000000000 | tf_op jit(solution)/shard_map/pallas_call | solution.py:289
  15.8 3.2 %collective-permute-done.2.refs_4_ = f32[256,128]{1,0:T(8,128)S(1)} collective-permute-done((f32[256,128]{1,0:T(8,128)S(1)}, f32[256,128]{1,0:T(8,128)S(1)}, u32[]{:S(2)}, u32[]{:S(2)}) %collective-permute-start.2) | collective-permute-done | bytes 131104 | tf_op jit(solution)/shard_map/ppermute | solution.py:316
  19.0 1.3 %collective-permute-done.3.refs_5_ = f32[256,128]{1,0:T(8,128)S(1)} collective-permute-done((f32[256,128]{1,0:T(8,128)S(1)}, f32[256,128]{1,0:T(8,128)S(1)}, u32[]{:S(2)}, u32[]{:S(2)}) %collective-permute-start.3) | collective-permute-done | bytes 131104 | tf_op jit(solution)/shard_map/ppermute | solution.py:316
  20.3 0.0 collective-permute-done.4.refs_6_.refs_1_
  20.3 0.4 %shard_map.40 = (f32[512,128]{1,0:T(8,128)S(1)}, f32[512,128]{1,0:T(8,128)S(1)}) custom-call(bf16[256,256]{1,0:T(8,128)(2,1)S(1)} %get-tuple-element.28.refs_0_.refs_4_, bf16[256,256]{1,0:T(8,128)(2,1)S(1)} %get-tuple-element.29.refs_1_.refs_5_, f32[256,128]{1,0:T(8,128)S(1)} %get-tuple-element.30.refs_2_, f32[256,128]{1,0:T(8,128)S(1)} %collective-permute-done.1.refs_3_, ...), custom_call_target="tpu_custom_call" | custom-call | flops 1000000000 | tf_op jit(solution)/shard_map/pallas_call | solution.py:289
  20.7 2.5 %collective-permute-start.7 = (f32[512,128]{1,0:T(8,128)S(1)}, f32[512,128]{1,0:T(8,128)S(1)}, u32[]{:S(2)}, u32[]{:S(2)}) collective-permute-start(f32[512,128]{1,0:T(8,128)S(1)} %get-tuple-element.36), channel_id=1, source_target_pairs={{0,17},{1,16},{2,19},{3,18},{4,21},{5,20},{6,23},{7,22},{8,25},{9,... | collective-permute-start | bytes 786440 | tf_op jit(solution)/shard_map/ppermute | solution.py:316
  23.2 0.5 %collective-permute-start.6 = (f32[512,128]{1,0:T(8,128)S(1)}, f32[512,128]{1,0:T(8,128)S(1)}, u32[]{:S(2)}, u32[]{:S(2)}) collective-permute-start(f32[512,128]{1,0:T(8,128)S(1)} %get-tuple-element.36), channel_id=1, source_target_pairs={{0,1},{1,0},{2,3},{3,2},{4,5},{5,4},{6,7},{7,6},{8,9},{9,8},{10,11... | collective-permute-start | bytes 786440 | tf_op jit(solution)/shard_map/ppermute | solution.py:316
  23.7 0.5 %collective-permute-start.5 = (f32[512,128]{1,0:T(8,128)S(1)}, f32[512,128]{1,0:T(8,128)S(1)}, u32[]{:S(2)}, u32[]{:S(2)}) collective-permute-start(f32[512,128]{1,0:T(8,128)S(1)} %get-tuple-element.35.refs_1_.refs_2_), channel_id=1, source_target_pairs={{0,16},{1,17},{2,18},{3,19},{4,20},{5,21},{6,22},{7,23},{8,24},{9,... | collective-permute-start | bytes 786440 | tf_op jit(solution)/shard_map/ppermute | solution.py:316
  24.3 0.0 collective-permute-done.9.refs_2_
  24.3 0.0 collective-permute-done.10.refs_3_
  24.3 0.4 %shard_map.42 = (f32[256,128]{1,0:T(8,128)S(1)}, f32[256,128]{1,0:T(8,128)S(1)}, f32[256,128]{1,0:T(8,128)S(1)}, f32[256,128]{1,0:T(8,128)S(1)}) custom-call(f32[512,128]{1,0:T(8,128)S(1)} %get-tuple-element.27.refs_1_.refs_0_, f32[512,128]{1,0:T(8,128)S(1)} %collective-permute-done.4.refs_6_.refs_1_, f32[512,128]{1,0:T(8,128)S(1)} %collective-permute-done.9.refs_2_, ...), custom_call_target="tpu_custom_call" | custom-call | flops 30000001024 | tf_op jit(solution)/shard_map/pallas_call | solution.py:289
  24.7 2.6 %collective-permute-start.11 = (f32[256,128]{1,0:T(8,128)S(1)}, f32[256,128]{1,0:T(8,128)S(1)}, u32[]{:S(2)}, u32[]{:S(2)}) collective-permute-start(f32[256,128]{1,0:T(8,128)S(1)} %get-tuple-element.42), channel_id=1, source_target_pairs={{0,4},{1,5},{2,6},{3,7},{4,0},{5,1},{6,2},{7,3},{8,12},{9,13},{10,... | collective-permute-start | bytes 393224 | tf_op jit(solution)/shard_map/ppermute | solution.py:316
  27.3 0.0 collective-permute-start.12
  27.3 3.6 %collective-permute-done.7.refs_4_.refs_5_ = f32[512,128]{1,0:T(8,128)S(1)} collective-permute-done((f32[512,128]{1,0:T(8,128)S(1)}, f32[512,128]{1,0:T(8,128)S(1)}, u32[]{:S(2)}, u32[]{:S(2)}) %collective-permute-start.7) | collective-permute-done | bytes 262176 | tf_op jit(solution)/shard_map/ppermute | solution.py:316
  30.9 0.0 collective-permute-start.13
  30.9 3.3 %collective-permute-done.6.refs_3_.refs_4_ = f32[512,128]{1,0:T(8,128)S(1)} collective-permute-done((f32[512,128]{1,0:T(8,128)S(1)}, f32[512,128]{1,0:T(8,128)S(1)}, u32[]{:S(2)}, u32[]{:S(2)}) %collective-permute-start.6) | collective-permute-done | bytes 262176 | tf_op jit(solution)/shard_map/ppermute | solution.py:316
  34.2 0.1 collective-permute-done.5.refs_2_.refs_3_
  34.3 0.1 shard_map.41
  34.4 0.1 collective-permute-start.8
  34.5 0.0 collective-permute-done.11.refs_3_
  34.5 0.0 collective-permute-done.12.refs_4_
  34.5 1.4 %collective-permute-done.13.refs_5_ = f32[256,128]{1,0:T(8,128)S(1)} collective-permute-done((f32[256,128]{1,0:T(8,128)S(1)}, f32[256,128]{1,0:T(8,128)S(1)}, u32[]{:S(2)}, u32[]{:S(2)}) %collective-permute-start.13) | collective-permute-done | bytes 131104 | tf_op jit(solution)/shard_map/ppermute | solution.py:316
  35.9 0.4 %shard_map.43.refs_8_ = f32[128,8,128]{2,1,0:T(8,128)S(1)} custom-call(bf16[256,256]{1,0:T(8,128)(2,1)S(1)} %get-tuple-element.37.refs_0_.refs_6_, bf16[256,256]{1,0:T(8,128)(2,1)S(1)} %get-tuple-element.38.refs_1_.refs_7_, f32[256,128]{1,0:T(8,128)S(1)} %get-tuple-element.41.refs_2_, f32[256,128]{1,0:T(8,128)S(1)} %collective-permute-done.11.refs_3_, ...), custom_call_target="tpu_custom_call" | custom-call | flops 10000000000 | tf_op jit(solution)/shard_map/pallas_call | solution.py:289
  36.3 0.1 collective-permute-done.8.refs_1_
  36.4 1.3 %shard_map.44 = f32[128,16,128]{2,1,0:T(8,128)} custom-call(f32[16,128]{1,0:T(8,128)S(1)} %get-tuple-element.25.refs_2_.refs_0_, f32[1024,128]{1,0:T(8,128)S(1)} %collective-permute-done.8.refs_1_, f32[512,128]{1,0:T(8,128)S(1)} %get-tuple-element.35.refs_1_.refs_2_, f32[512,128]{1,0:T(8,128)S(1)} %collective-permute-done.5.refs_2_.refs_3_, ...), custom_call_target="tpu_custom_call" | custom-call | flops 2000000000 | tf_op jit(solution)/shard_map/pallas_call | solution.py:289
Async XLA Ops:
  2.0 5.2 %collective-permute-start = (f32[1024,128]{1,0:T(8,128)S(1)}, f32[1024,128]{1,0:T(8,128)S(1)}, u32[]{:S(2)}, u32[]{:S(2)}) collective-permute-start(f32[1024,128]{1,0:T(8,128)S(1)} %get-tuple-element.26.refs_0_), channel_id=1, source_target_pairs={{0,8},{1,9},{2,10},{3,11},{4,12},{5,13},{6,14},{7,15},{8,0},{9,1},... | collective-permute-start | bytes 1572872 | tf_op jit(solution)/shard_map/ppermute | solution.py:316
  2.6 9.3 %collective-permute-start.1 = (f32[256,128]{1,0:T(8,128)S(1)}, f32[256,128]{1,0:T(8,128)S(1)}, u32[]{:S(2)}, u32[]{:S(2)}) collective-permute-start(f32[256,128]{1,0:T(8,128)S(1)} %get-tuple-element.31), channel_id=1, source_target_pairs={{0,6},{1,7},{2,4},{3,5},{4,2},{5,3},{6,0},{7,1},{8,14},{9,15},{10,... | collective-permute-start | bytes 393224 | tf_op jit(solution)/shard_map/ppermute | solution.py:316
  7.2 8.1 %copy-start = (f32[4,2,128,128]{3,2,1,0:T(8,128)S(1)}, f32[4,2,128,128]{3,2,1,0:T(8,128)}, u32[]{:S(2)}) copy-start(f32[4,2,128,128]{3,2,1,0:T(8,128)} %refs_0_.1) | copy-start | bytes 1572868
  7.5 12.8 %collective-permute-start.4 = (f32[512,128]{1,0:T(8,128)S(1)}, f32[512,128]{1,0:T(8,128)S(1)}, u32[]{:S(2)}, u32[]{:S(2)}) collective-permute-start(f32[512,128]{1,0:T(8,128)S(1)} %get-tuple-element.34), channel_id=1, source_target_pairs={{0,16},{1,17},{2,18},{3,19},{4,20},{5,21},{6,22},{7,23},{8,24},{9,... | collective-permute-start | bytes 786440 | tf_op jit(solution)/shard_map/ppermute | solution.py:316
  9.1 15.2 %collective-permute-start.9 = (f32[512,128]{1,0:T(8,128)S(1)}, f32[512,128]{1,0:T(8,128)S(1)}, u32[]{:S(2)}, u32[]{:S(2)}) collective-permute-start(f32[512,128]{1,0:T(8,128)S(1)} %get-tuple-element.39), channel_id=1, source_target_pairs={{0,1},{1,0},{2,3},{3,2},{4,5},{5,4},{6,7},{7,6},{8,9},{9,8},{10,11... | collective-permute-start | bytes 786440 | tf_op jit(solution)/shard_map/ppermute | solution.py:316
  10.6 13.7 %collective-permute-start.10 = (f32[512,128]{1,0:T(8,128)S(1)}, f32[512,128]{1,0:T(8,128)S(1)}, u32[]{:S(2)}, u32[]{:S(2)}) collective-permute-start(f32[512,128]{1,0:T(8,128)S(1)} %get-tuple-element.40), channel_id=1, source_target_pairs={{0,17},{1,16},{2,19},{3,18},{4,21},{5,20},{6,23},{7,22},{8,25},{9,... | collective-permute-start | bytes 786440 | tf_op jit(solution)/shard_map/ppermute | solution.py:316
  11.1 8.0 %collective-permute-start.2 = (f32[256,128]{1,0:T(8,128)S(1)}, f32[256,128]{1,0:T(8,128)S(1)}, u32[]{:S(2)}, u32[]{:S(2)}) collective-permute-start(f32[256,128]{1,0:T(8,128)S(1)} %get-tuple-element.32), channel_id=1, source_target_pairs={{0,4},{1,5},{2,6},{3,7},{4,0},{5,1},{6,2},{7,3},{8,12},{9,13},{10,... | collective-permute-start | bytes 393224 | tf_op jit(solution)/shard_map/ppermute | solution.py:316
  11.9 8.4 %collective-permute-start.3 = (f32[256,128]{1,0:T(8,128)S(1)}, f32[256,128]{1,0:T(8,128)S(1)}, u32[]{:S(2)}, u32[]{:S(2)}) collective-permute-start(f32[256,128]{1,0:T(8,128)S(1)} %get-tuple-element.33), channel_id=1, source_target_pairs={{0,2},{1,3},{2,0},{3,1},{4,6},{5,7},{6,4},{7,5},{8,10},{9,11},{10,... | collective-permute-start | bytes 393224 | tf_op jit(solution)/shard_map/ppermute | solution.py:316
  20.7 10.2 %collective-permute-start.7 = (f32[512,128]{1,0:T(8,128)S(1)}, f32[512,128]{1,0:T(8,128)S(1)}, u32[]{:S(2)}, u32[]{:S(2)}) collective-permute-start(f32[512,128]{1,0:T(8,128)S(1)} %get-tuple-element.36), channel_id=1, source_target_pairs={{0,17},{1,16},{2,19},{3,18},{4,21},{5,20},{6,23},{7,22},{8,25},{9,... | collective-permute-start | bytes 786440 | tf_op jit(solution)/shard_map/ppermute | solution.py:316
  23.2 11.0 %collective-permute-start.6 = (f32[512,128]{1,0:T(8,128)S(1)}, f32[512,128]{1,0:T(8,128)S(1)}, u32[]{:S(2)}, u32[]{:S(2)}) collective-permute-start(f32[512,128]{1,0:T(8,128)S(1)} %get-tuple-element.36), channel_id=1, source_target_pairs={{0,1},{1,0},{2,3},{3,2},{4,5},{5,4},{6,7},{7,6},{8,9},{9,8},{10,11... | collective-permute-start | bytes 786440 | tf_op jit(solution)/shard_map/ppermute | solution.py:316
  23.7 10.6 %collective-permute-start.5 = (f32[512,128]{1,0:T(8,128)S(1)}, f32[512,128]{1,0:T(8,128)S(1)}, u32[]{:S(2)}, u32[]{:S(2)}) collective-permute-start(f32[512,128]{1,0:T(8,128)S(1)} %get-tuple-element.35.refs_1_.refs_2_), channel_id=1, source_target_pairs={{0,16},{1,17},{2,18},{3,19},{4,20},{5,21},{6,22},{7,23},{8,24},{9,... | collective-permute-start | bytes 786440 | tf_op jit(solution)/shard_map/ppermute | solution.py:316
  24.7 9.9 %collective-permute-start.11 = (f32[256,128]{1,0:T(8,128)S(1)}, f32[256,128]{1,0:T(8,128)S(1)}, u32[]{:S(2)}, u32[]{:S(2)}) collective-permute-start(f32[256,128]{1,0:T(8,128)S(1)} %get-tuple-element.42), channel_id=1, source_target_pairs={{0,4},{1,5},{2,6},{3,7},{4,0},{5,1},{6,2},{7,3},{8,12},{9,13},{10,... | collective-permute-start | bytes 393224 | tf_op jit(solution)/shard_map/ppermute | solution.py:316
  27.3 7.3 %collective-permute-start.12 = (f32[256,128]{1,0:T(8,128)S(1)}, f32[256,128]{1,0:T(8,128)S(1)}, u32[]{:S(2)}, u32[]{:S(2)}) collective-permute-start(f32[256,128]{1,0:T(8,128)S(1)} %get-tuple-element.43), channel_id=1, source_target_pairs={{0,6},{1,7},{2,4},{3,5},{4,2},{5,3},{6,0},{7,1},{8,14},{9,15},{10,... | collective-permute-start | bytes 393224 | tf_op jit(solution)/shard_map/ppermute | solution.py:316
  30.9 5.0 %collective-permute-start.13 = (f32[256,128]{1,0:T(8,128)S(1)}, f32[256,128]{1,0:T(8,128)S(1)}, u32[]{:S(2)}, u32[]{:S(2)}) collective-permute-start(f32[256,128]{1,0:T(8,128)S(1)} %get-tuple-element.44), channel_id=1, source_target_pairs={{0,2},{1,3},{2,0},{3,1},{4,6},{5,7},{6,4},{7,5},{8,10},{9,11},{10,... | collective-permute-start | bytes 393224 | tf_op jit(solution)/shard_map/ppermute | solution.py:316
  34.4 2.0 %collective-permute-start.8 = (f32[1024,128]{1,0:T(8,128)S(1)}, f32[1024,128]{1,0:T(8,128)S(1)}, u32[]{:S(2)}, u32[]{:S(2)}) collective-permute-start(f32[1024,128]{1,0:T(8,128)S(1)} %shard_map.41), channel_id=1, source_target_pairs={{0,8},{1,9},{2,10},{3,11},{4,12},{5,13},{6,14},{7,15},{8,0},{9,1},... | collective-permute-start | bytes 1572872 | tf_op jit(solution)/shard_map/ppermute | solution.py:316
